TPU v7x, 32 devices: a whole 2x2x4 slice. The times are simulated.
32 devices in a mesh: var: 4 (over x, core), tm: 8 (over z, y).
Axes of the slice: x: 2, y: 2, z: 4, core: 2. Of those that a mesh axis runs over, the one named last changes fastest.
Arguments:
- latent: bfloat16 [4, 2048, 1536], P('var', 'tm')
- fresh_noise: bfloat16 [4, 2048, 1536], P('var', 'tm'), may hold values from -6 to 6
- timestep: int32 [1], replicated, may hold values from 400 to 800
- prompt_ids: int32 [4, 64], P('var'), may hold values from 0 to 16383
- block_table: int32 [3, 3], replicated, may hold values from 0 to 1, as said below
- prompt_table: bfloat16 [16384, 1536], P(None, 'tm'), may hold values from -12 to 12
- w_query: bfloat16 [1536, 768], P('var')
- w_keyval: bfloat16 [1536, 1536], P('var')
- w_out: bfloat16 [768, 1536], P('var'), may hold values from -0.4375 to 0.4375
Outputs:
- stepped: bfloat16 [4, 2048, 1536], P('var', 'tm')
Inputs may be any that keep to these rules, and one draw needn't show every extreme that they name: `block_table`: the diagonal and the first column of the table are always 1.
All inputs are finite; a program needn't handle non-finite values.
Results may differ from a plain program's by a relative error of at most 0.0048.
Values may be sent and summed in bfloat16 or wider, within the bound.
No kernel may reach another device: no remote copies, remote signals or barrier semaphores. Data moves between devices by JAX's collectives and lax.ppermute only.
A program may use at most 64 MiB of HBM per device.

v0:
```python
import math

import jax
import jax.numpy as jnp
from jax import lax
from jax.sharding import PartitionSpec as P

HEADS = 12
HS = 64
SEAM = 128
BLK = 128
TSTEPS = 1000
STRIDE = 200


epsilon = 1e-06


def shifted(block, axis, distance):
    devices = range(lax.axis_size(axis))
    route = [(i - distance, i) for i in devices if i - distance in devices]
    return lax.ppermute(block, axis, route)


def broadcast(value, axis, source):
    kept = jnp.where(lax.axis_index(axis) == source, value, 0).astype(value.dtype)
    return lax.psum(kept, axis)


def plan(moment):
    return jnp.cos((moment / TSTEPS + 0.008) / 1.008 * (math.pi / 2.0)) ** 2


def coefficients(timestep):
    current = timestep[0].astype(jnp.float32)
    abar_now = plan(current)
    abar_prev = plan(current - STRIDE)
    spread = jnp.sqrt((1.0 - abar_prev) / (1.0 - abar_now) * (1.0 - abar_now / abar_prev))
    carried = jnp.sqrt((1.0 - abar_prev) * (abar_now / abar_prev - abar_now) / (1.0 - abar_now))
    coef_pred = carried - jnp.sqrt(abar_prev) * jnp.sqrt(1.0 - abar_now) / jnp.sqrt(abar_now)
    coef_latent = jnp.sqrt(abar_prev / abar_now)
    return (current, coef_latent, coef_pred, spread)


def time_embedding(current, model_width):
    half_width = model_width // 2
    frequency = jnp.exp(-math.log(10000.0) * jnp.arange(half_width, dtype=jnp.float32) / half_width)
    angles = current * frequency
    return jnp.concatenate([jnp.cos(angles), jnp.sin(angles)])


def attend(queries, keys, values, both_masks):
    window_rows = queries.shape[0]
    key_rows = keys.shape[0]
    query_heads = queries.reshape(window_rows, HEADS, HS).transpose(1, 0, 2)
    key_heads = keys.reshape(key_rows, HEADS, HS).transpose(1, 0, 2)
    value_heads = values.reshape(key_rows, HEADS, HS).transpose(1, 0, 2)

    def one_head(operands):
        head_query, head_key, head_value = operands
        scores = jnp.einsum(
            "qd,kd->qk", head_query, head_key, preferred_element_type=jnp.float32
        ) * (1.0 / math.sqrt(HS))
        scores = jnp.where(both_masks, scores, -1e30)
        row_max = jnp.max(scores, axis=-1, keepdims=True)
        weights = jnp.exp(scores - row_max)
        row_sum = jnp.sum(weights, axis=-1, keepdims=True)
        probs = (weights / row_sum).astype(jnp.bfloat16)
        return jnp.dot(probs, head_value, preferred_element_type=jnp.float32)

    attended = lax.map(one_head, (query_heads, key_heads, value_heads))
    return attended.transpose(1, 0, 2).reshape(window_rows, HEADS * HS)


def local(
    latent, fresh_noise, timestep, prompt_ids, block_table, prompt_table, w_query, w_keyval, w_out
):
    own_rows = latent.shape[1]
    model_width = latent.shape[2]
    head_width = w_query.shape[1]
    tm_count = lax.axis_size("tm")
    tm_place = lax.axis_index("tm")
    current, coef_latent, coef_pred, spread = coefficients(timestep)
    embedded = time_embedding(current, model_width)
    local_pooled = jnp.mean(prompt_table[prompt_ids[0]].astype(jnp.float32), axis=0)
    pooled = lax.all_gather(local_pooled, "tm", axis=0, tiled=True)
    condition = embedded + pooled
    values = latent[0].astype(jnp.float32)
    inv_norm = lax.rsqrt(jnp.mean(values * values, axis=-1, keepdims=True) + epsilon)
    normed = (values * inv_norm * (1.0 + condition[None, :])).astype(jnp.bfloat16)
    window_rows = own_rows + SEAM
    allowed = jnp.repeat(jnp.repeat(block_table, BLK, axis=0), BLK, axis=1) > 0
    key_valid = (jnp.arange(window_rows) < own_rows) | (tm_place != tm_count - 1)
    key_mask = allowed & key_valid[None, :]
    both_masks = jnp.concatenate([key_mask, key_mask], axis=1)
    arrived = shifted(normed[:SEAM], "tm", -1)
    window_inputs = jnp.concatenate([normed, arrived], axis=0)
    columns = window_inputs
    query_sum = jnp.dot(
        columns,
        lax.all_gather(w_query, "var", axis=0, tiled=True),
        preferred_element_type=jnp.float32,
    )
    keyval_sum = jnp.dot(
        columns,
        lax.all_gather(w_keyval, "var", axis=0, tiled=True),
        preferred_element_type=jnp.float32,
    )
    window_query = query_sum.astype(jnp.bfloat16)
    window_keyval = keyval_sum.astype(jnp.bfloat16)
    source_window = broadcast(window_keyval, "var", 0)
    all_keys = jnp.concatenate(
        [window_keyval[:, :head_width], source_window[:, :head_width]], axis=0
    )
    all_values = jnp.concatenate(
        [window_keyval[:, head_width:], source_window[:, head_width:]], axis=0
    )
    attended = attend(window_query, all_keys, all_values, both_masks)
    ramp_up = (jnp.arange(SEAM, dtype=jnp.float32) + 0.5) / SEAM
    tail_part = attended[own_rows:] * (1.0 - ramp_up)[:, None]
    received = shifted(tail_part.astype(jnp.bfloat16), "tm", 1).astype(tail_part.dtype)
    lead_weight = jnp.where(tm_place == 0, 1.0, ramp_up)
    lead_part = attended[:SEAM] * lead_weight[:, None] + received
    blended = jnp.concatenate([lead_part, attended[SEAM:own_rows]], axis=0).astype(jnp.bfloat16)
    columns = blended
    prediction = jnp.dot(
        columns,
        lax.all_gather(w_out, "var", axis=0, tiled=True),
        preferred_element_type=jnp.float32,
    )
    result = (
        coef_latent * values + coef_pred * prediction + spread * fresh_noise[0].astype(jnp.float32)
    )
    return result.astype(jnp.bfloat16)[None]


def solution(mesh):
    placed = (
        P("var", "tm", None),
        P("var", "tm", None),
        P(),
        P("var", None),
        P(),
        P(None, "tm"),
        P("var", None),
        P("var", None),
        P("var", None),
    )
    return jax.shard_map(
        local, mesh=mesh, in_specs=placed, out_specs=P("var", "tm", None), check_vma=False
    )
```

profile of v0, /device:TPU:10, one launch (start us, length us, event | category | flops | bytes accessed | tf_op | source)
XLA Modules:
  0.0 180.9 jit_solution(16629851288748817635)
XLA Ops:
  8.7 10.2 %copy.14 = bf16[16384,192]{1,0:T(8,128)(2,1)} copy(bf16[16384,192]{0,1:T(8,128)(2,1)} %param.16) | data formatting | bytes 12582912 | tf_op args[5]
  20.2 5.2 %gather_fusion = bf16[64,192]{1,0:T(8,128)(2,1)S(1)} fusion(bf16[16384,192]{1,0:T(8,128)(2,1)} %copy.14, s32[1024]{0:T(1024)S(1)} %pad_clamp_fusion), kind=kCustom, calls=%fused_computation | custom fusion | bytes 49408 | tf_op jit(solution)/shard_map/gather | solution.py:85
  25.5 19.1 %all-reduce = f32[1536]{0:T(1024)S(1)} all-reduce(f32[1536]{0:T(1024)S(1)} %multiply_dynamic-update-slice_fusion), channel_id=1, replica_groups=mesh['var'=4,'tm'=8] {'tm'}, use_global_device_ids=true, to_apply=%add | all-reduce | flops 1536 | bytes 12288
  45.2 2.4 %collective-permute-start = (bf16[128,1536]{1,0:T(8,128)(2,1)S(1)}, bf16[128,1536]{1,0:T(8,128)(2,1)S(1)}, u32[]{:S(2)}, u32[]{:S(2)}) collective-permute-start(bf16[128,1536]{1,0:T(8,128)(2,1)S(1)} %slice.47), channel_id=1, source_target_pairs={{1,0},{2,1},{3,2},{4,3},{5,4},{6,5},{7,6},{9,8},{10,9},{11,10},{12... | collective-permute-start | bytes 1179656 | tf_op jit(solution)/shard_map/ppermute | solution.py:22
  47.6 7.2 %collective-permute-done = bf16[128,1536]{1,0:T(8,128)(2,1)S(1)} collective-permute-done((bf16[128,1536]{1,0:T(8,128)(2,1)S(1)}, bf16[128,1536]{1,0:T(8,128)(2,1)S(1)}, u32[]{:S(2)}, u32[]{:S(2)}) %collective-permute-start) | collective-permute-done | bytes 393248 | tf_op jit(solution)/shard_map/ppermute | solution.py:22
  54.9 6.1 %broadcast_select_fusion = (bf16[384,1536]{1,0:T(8,128)(2,1)}, bf16[384,1536]{1,0:T(8,128)(2,1)}) fusion(pred[]{:T(512)S(6)} %eq.6, bf16[1536,1536]{1,0:T(8,128)(2,1)} %all-gather.6.cloned.1.call-done, bf16[128,1536]{1,0:T(8,128)(2,1)S(1)} %collective-permute-done, bf16[256,1536]{1,0:T(8,128)(2,1)S(1)} %fusion.19), kind=kOutput, calls=%fused_computation.35 | convolution fusion | flops 1815478272 | bytes 8257537 | tf_op jit(solution)/shard_map/dot_general | solution.py:104
  62.5 9.8 %all-gather.4.cloned.1.call-done = bf16[1536,768]{1,0:T(8,128)(2,1)} async-done(((bf16[384,768]{1,0:T(8,128)(2,1)}), bf16[1536,768]{1,0:T(8,128)(2,1)}) %all-gather.4.cloned.1.call-update) | async-done | bytes 2359312 | tf_op jit(solution)/shard_map/all_gather | solution.py:101
  72.3 2.7 %convolution_convert_fusion.1 = bf16[384,768]{1,0:T(8,128)(2,1)S(1)} fusion(bf16[1536,768]{1,0:T(8,128)(2,1)} %all-gather.4.cloned.1.call-done, bf16[128,1536]{1,0:T(8,128)(2,1)S(1)} %collective-permute-done, bf16[256,1536]{1,0:T(8,128)(2,1)S(1)} %fusion.19), kind=kOutput, calls=%fused_computation.30 | convolution fusion | flops 908623872 | bytes 4128768 | tf_op jit(solution)/shard_map/dot_general | solution.py:99
  76.6 35.5 %all-reduce.3.cloned.1.call-done = bf16[384,1536]{1,0:T(8,128)(2,1)} async-done(((bf16[384,1536]{1,0:T(8,128)(2,1)}), bf16[384,1536]{1,0:T(8,128)(2,1)}) %all-reduce.3.cloned.1.call-update) | async-done | bytes 1179664 | tf_op jit(solution)/shard_map/psum | solution.py:27
  112.1 2.1 %fusion.38 = (bf16[384,768]{1,0:T(8,128)(2,1)S(1)}, bf16[384,768]{1,0:T(8,128)(2,1)}) fusion(bf16[384,1536]{1,0:T(8,128)(2,1)} %all-reduce.3.cloned.1.call-done), kind=kLoop, calls=%fused_computation.71 | loop fusion | bytes 2359296 | tf_op jit(solution)/shard_map/slice | solution.py:116
  114.4 1.4 copy.18
  116.6 43.4 %while.10 = (s32[]{:T(128)}, f32[12,384,64]{1,2,0:T(8,128)}, bf16[12,384,64]{1,2,0:T(8,128)(2,1)}, bf16[12,768,64]{1,2,0:T(8,128)(2,1)S(1)}, pred[384,768]{1,0:T...) while((s32[]{:T(128)}, f32[12,384,64]{1,2,0:T(8,128)}, bf16[12,384,64]{1,2,0:T(8,128)(2,1)}, ...), condition=%wide.region_6.7_spmd, body=%wide.region_3.6_spmd.sunk | while | flops 77856000 | bytes 4187725 | solution.py:71
  116.6 1.3 fusion.47
  118.2 2.0 %fusion.49 = f32[12,384,64]{1,2,0:T(8,128)} fusion(f32[12,384,64]{1,2,0:T(8,128)} %get-tuple-element.117, s32[]{:T(128)} %get-tuple-element.116, f32[384,768]{1,0:T(8,128)S(1)} %get-tuple-element.107, f32[384]{0:T(512)S(1)} %fusion.48, f32[384]{0:T(512)S(1)} %get-tuple-element.108, bf16[12,768,64]{1,2,0:T(8,128)(2,1)} %get-tuple-element.128), kind=kOutput, calls=%fused_computation.6.clone.1 | convolution fusion | flops 38633472 | bytes 1380352 | tf_op jit(solution)/shard_map/while/body/eval_jaxpr/dot_general | solution.py:69
  121.8 2.0 %fusion.49 = f32[12,384,64]{1,2,0:T(8,128)} fusion(f32[12,384,64]{1,2,0:T(8,128)} %get-tuple-element.117, s32[]{:T(128)} %get-tuple-element.116, f32[384,768]{1,0:T(8,128)S(1)} %get-tuple-element.107, f32[384]{0:T(512)S(1)} %fusion.48, f32[384]{0:T(512)S(1)} %get-tuple-element.108, bf16[12,768,64]{1,2,0:T(8,128)(2,1)} %get-tuple-element.128), kind=kOutput, calls=%fused_computation.6.clone.1 | convolution fusion | flops 38633472 | bytes 1380352 | tf_op jit(solution)/shard_map/while/body/eval_jaxpr/dot_general | solution.py:69
  125.4 2.0 %fusion.49 = f32[12,384,64]{1,2,0:T(8,128)} fusion(f32[12,384,64]{1,2,0:T(8,128)} %get-tuple-element.117, s32[]{:T(128)} %get-tuple-element.116, f32[384,768]{1,0:T(8,128)S(1)} %get-tuple-element.107, f32[384]{0:T(512)S(1)} %fusion.48, f32[384]{0:T(512)S(1)} %get-tuple-element.108, bf16[12,768,64]{1,2,0:T(8,128)(2,1)} %get-tuple-element.128), kind=kOutput, calls=%fused_computation.6.clone.1 | convolution fusion | flops 38633472 | bytes 1380352 | tf_op jit(solution)/shard_map/while/body/eval_jaxpr/dot_general | solution.py:69
  127.4 1.3 fusion.47
  129.0 2.0 %fusion.49 = f32[12,384,64]{1,2,0:T(8,128)} fusion(f32[12,384,64]{1,2,0:T(8,128)} %get-tuple-element.117, s32[]{:T(128)} %get-tuple-element.116, f32[384,768]{1,0:T(8,128)S(1)} %get-tuple-element.107, f32[384]{0:T(512)S(1)} %fusion.48, f32[384]{0:T(512)S(1)} %get-tuple-element.108, bf16[12,768,64]{1,2,0:T(8,128)(2,1)} %get-tuple-element.128), kind=kOutput, calls=%fused_computation.6.clone.1 | convolution fusion | flops 38633472 | bytes 1380352 | tf_op jit(solution)/shard_map/while/body/eval_jaxpr/dot_general | solution.py:69
  131.0 1.3 fusion.47
  132.7 2.0 %fusion.49 = f32[12,384,64]{1,2,0:T(8,128)} fusion(f32[12,384,64]{1,2,0:T(8,128)} %get-tuple-element.117, s32[]{:T(128)} %get-tuple-element.116, f32[384,768]{1,0:T(8,128)S(1)} %get-tuple-element.107, f32[384]{0:T(512)S(1)} %fusion.48, f32[384]{0:T(512)S(1)} %get-tuple-element.108, bf16[12,768,64]{1,2,0:T(8,128)(2,1)} %get-tuple-element.128), kind=kOutput, calls=%fused_computation.6.clone.1 | convolution fusion | flops 38633472 | bytes 1380352 | tf_op jit(solution)/shard_map/while/body/eval_jaxpr/dot_general | solution.py:69
  136.3 2.0 %fusion.49 = f32[12,384,64]{1,2,0:T(8,128)} fusion(f32[12,384,64]{1,2,0:T(8,128)} %get-tuple-element.117, s32[]{:T(128)} %get-tuple-element.116, f32[384,768]{1,0:T(8,128)S(1)} %get-tuple-element.107, f32[384]{0:T(512)S(1)} %fusion.48, f32[384]{0:T(512)S(1)} %get-tuple-element.108, bf16[12,768,64]{1,2,0:T(8,128)(2,1)} %get-tuple-element.128), kind=kOutput, calls=%fused_computation.6.clone.1 | convolution fusion | flops 38633472 | bytes 1380352 | tf_op jit(solution)/shard_map/while/body/eval_jaxpr/dot_general | solution.py:69
  139.9 2.0 %fusion.49 = f32[12,384,64]{1,2,0:T(8,128)} fusion(f32[12,384,64]{1,2,0:T(8,128)} %get-tuple-element.117, s32[]{:T(128)} %get-tuple-element.116, f32[384,768]{1,0:T(8,128)S(1)} %get-tuple-element.107, f32[384]{0:T(512)S(1)} %fusion.48, f32[384]{0:T(512)S(1)} %get-tuple-element.108, bf16[12,768,64]{1,2,0:T(8,128)(2,1)} %get-tuple-element.128), kind=kOutput, calls=%fused_computation.6.clone.1 | convolution fusion | flops 38633472 | bytes 1380352 | tf_op jit(solution)/shard_map/while/body/eval_jaxpr/dot_general | solution.py:69
  143.5 2.0 %fusion.49 = f32[12,384,64]{1,2,0:T(8,128)} fusion(f32[12,384,64]{1,2,0:T(8,128)} %get-tuple-element.117, s32[]{:T(128)} %get-tuple-element.116, f32[384,768]{1,0:T(8,128)S(1)} %get-tuple-element.107, f32[384]{0:T(512)S(1)} %fusion.48, f32[384]{0:T(512)S(1)} %get-tuple-element.108, bf16[12,768,64]{1,2,0:T(8,128)(2,1)} %get-tuple-element.128), kind=kOutput, calls=%fused_computation.6.clone.1 | convolution fusion | flops 38633472 | bytes 1380352 | tf_op jit(solution)/shard_map/while/body/eval_jaxpr/dot_general | solution.py:69
  147.1 2.0 %fusion.49 = f32[12,384,64]{1,2,0:T(8,128)} fusion(f32[12,384,64]{1,2,0:T(8,128)} %get-tuple-element.117, s32[]{:T(128)} %get-tuple-element.116, f32[384,768]{1,0:T(8,128)S(1)} %get-tuple-element.107, f32[384]{0:T(512)S(1)} %fusion.48, f32[384]{0:T(512)S(1)} %get-tuple-element.108, bf16[12,768,64]{1,2,0:T(8,128)(2,1)} %get-tuple-element.128), kind=kOutput, calls=%fused_computation.6.clone.1 | convolution fusion | flops 38633472 | bytes 1380352 | tf_op jit(solution)/shard_map/while/body/eval_jaxpr/dot_general | solution.py:69
  149.1 1.3 fusion.47
  150.7 2.0 %fusion.49 = f32[12,384,64]{1,2,0:T(8,128)} fusion(f32[12,384,64]{1,2,0:T(8,128)} %get-tuple-element.117, s32[]{:T(128)} %get-tuple-element.116, f32[384,768]{1,0:T(8,128)S(1)} %get-tuple-element.107, f32[384]{0:T(512)S(1)} %fusion.48, f32[384]{0:T(512)S(1)} %get-tuple-element.108, bf16[12,768,64]{1,2,0:T(8,128)(2,1)} %get-tuple-element.128), kind=kOutput, calls=%fused_computation.6.clone.1 | convolution fusion | flops 38633472 | bytes 1380352 | tf_op jit(solution)/shard_map/while/body/eval_jaxpr/dot_general | solution.py:69
  152.7 1.3 fusion.47
  154.3 2.0 %fusion.49 = f32[12,384,64]{1,2,0:T(8,128)} fusion(f32[12,384,64]{1,2,0:T(8,128)} %get-tuple-element.117, s32[]{:T(128)} %get-tuple-element.116, f32[384,768]{1,0:T(8,128)S(1)} %get-tuple-element.107, f32[384]{0:T(512)S(1)} %fusion.48, f32[384]{0:T(512)S(1)} %get-tuple-element.108, bf16[12,768,64]{1,2,0:T(8,128)(2,1)} %get-tuple-element.128), kind=kOutput, calls=%fused_computation.6.clone.1 | convolution fusion | flops 38633472 | bytes 1380352 | tf_op jit(solution)/shard_map/while/body/eval_jaxpr/dot_general | solution.py:69
  157.9 2.0 %fusion.49 = f32[12,384,64]{1,2,0:T(8,128)} fusion(f32[12,384,64]{1,2,0:T(8,128)} %get-tuple-element.117, s32[]{:T(128)} %get-tuple-element.116, f32[384,768]{1,0:T(8,128)S(1)} %get-tuple-element.107, f32[384]{0:T(512)S(1)} %fusion.48, f32[384]{0:T(512)S(1)} %get-tuple-element.108, bf16[12,768,64]{1,2,0:T(8,128)(2,1)} %get-tuple-element.128), kind=kOutput, calls=%fused_computation.6.clone.1 | convolution fusion | flops 38633472 | bytes 1380352 | tf_op jit(solution)/shard_map/while/body/eval_jaxpr/dot_general | solution.py:69
  161.1 3.5 %collective-permute-start.1 = (bf16[128,768]{0,1:T(8,128)(2,1)S(1)}, bf16[128,768]{0,1:T(8,128)(2,1)S(1)}, u32[]{:S(2)}, u32[]{:S(2)}) collective-permute-start(bf16[128,768]{0,1:T(8,128)(2,1)S(1)} %fusion.23), channel_id=1, source_target_pairs={{0,1},{1,2},{2,3},{3,4},{4,5},{5,6},{6,7},{8,9},{9,10},{10,11},{11... | collective-permute-start | bytes 589832 | tf_op jit(solution)/shard_map/ppermute | solution.py:22
  166.3 4.5 %collective-permute-done.1 = bf16[128,768]{0,1:T(8,128)(2,1)S(1)} collective-permute-done((bf16[128,768]{0,1:T(8,128)(2,1)S(1)}, bf16[128,768]{0,1:T(8,128)(2,1)S(1)}, u32[]{:S(2)}, u32[]{:S(2)}) %collective-permute-start.1) | collective-permute-done | bytes 196640 | tf_op jit(solution)/shard_map/ppermute | solution.py:22
  170.9 3.5 %fusion.16 = bf16[1,256,1536]{2,1,0:T(8,128)(2,1)} fusion(bf16[768,1536]{1,0:T(8,128)(2,1)} %all-gather.8.cloned.1.call-done, bf16[1,256,1536]{2,1,0:T(8,128)(2,1)S(1)} %copy-done.4, bf16[1,256,1536]{2,1,0:T(8,128)(2,1)S(1)} %copy-done, f32[]{:T(128)S(6)} %sqrt.23, f32[]{:T(128)S(6)} %sub.41, f32[]{:T(128)S(6)} %sqrt.18, bf16[128,768]{0,1:T(8,128)(2,1)S(1)} %bitcast.81, ...), kind=kOutput, calls=%fused_computation.23 | convolution fusion | flops 607911936 | bytes 5111820 | tf_op jit(solution)/shard_map/dot_general | solution.py:126
  (75 shorter events, 21.9 us)
Async XLA Ops:
  6.5 48.3 %all-gather.6.cloned.1.call-start = ((), (), s32[]{:S(2)}) async-start(), calls=%async_computation.1 | async-start | bytes 5898240 | tf_op jit(solution)/shard_map/all_gather | solution.py:106
  7.3 65.0 %all-gather.4.cloned.1.call-start = ((), (), s32[]{:S(2)}) async-start(), calls=%async_computation | async-start | bytes 2949120 | tf_op jit(solution)/shard_map/all_gather | solution.py:101
  8.0 104.1 %all-reduce.3.cloned.1.call-start = ((), (), s32[]{:S(2)}) async-start(), calls=%async_computation.2 | async-start | bytes 2359296 | tf_op jit(solution)/shard_map/psum | solution.py:27
  8.7 10.2 %copy-start.6 = (u32[32]{0:T(128)S(1)}, u32[32]{0:T(128)}, u32[]{:S(2)}) copy-start(u32[32]{0:T(128)} %constant.86) | copy-start | bytes 388
  8.7 11.5 %copy-start.5 = (s32[1,64]{1,0:T(1,128)S(1)}, s32[1,64]{1,0:T(1,128)}, u32[]{:S(2)}) copy-start(s32[1,64]{1,0:T(1,128)} %param.14) | copy-start | bytes 772
  8.7 35.9 %copy-start = (bf16[1,256,1536]{2,1,0:T(8,128)(2,1)S(1)}, bf16[1,256,1536]{2,1,0:T(8,128)(2,1)}, u32[]{:S(2)}) copy-start(bf16[1,256,1536]{2,1,0:T(8,128)(2,1)} %param.11) | copy-start | bytes 2359300
  45.2 9.7 %collective-permute-start = (bf16[128,1536]{1,0:T(8,128)(2,1)S(1)}, bf16[128,1536]{1,0:T(8,128)(2,1)S(1)}, u32[]{:S(2)}, u32[]{:S(2)}) collective-permute-start(bf16[128,1536]{1,0:T(8,128)(2,1)S(1)} %slice.47), channel_id=1, source_target_pairs={{1,0},{2,1},{3,2},{4,3},{5,4},{6,5},{7,6},{9,8},{10,9},{11,10},{12... | collective-permute-start | bytes 1179656 | tf_op jit(solution)/shard_map/ppermute | solution.py:22
  60.9 0.7 copy-start.3
  61.0 109.9 %all-gather.8.cloned.1.call-start = ((), (), s32[]{:S(2)}) async-start(), calls=%async_computation.3 | async-start | bytes 2949120 | tf_op jit(solution)/shard_map/all_gather | solution.py:128
  75.0 1.5 copy-start.2
  114.4 1.5 copy-start.1
  161.1 9.8 %copy-start.4 = (bf16[1,256,1536]{2,1,0:T(8,128)(2,1)S(1)}, bf16[1,256,1536]{2,1,0:T(8,128)(2,1)}, u32[]{:S(2)}) copy-start(bf16[1,256,1536]{2,1,0:T(8,128)(2,1)} %param.12) | copy-start | bytes 2359300
  161.1 9.7 %collective-permute-start.1 = (bf16[128,768]{0,1:T(8,128)(2,1)S(1)}, bf16[128,768]{0,1:T(8,128)(2,1)S(1)}, u32[]{:S(2)}, u32[]{:S(2)}) collective-permute-start(bf16[128,768]{0,1:T(8,128)(2,1)S(1)} %fusion.23), channel_id=1, source_target_pairs={{0,1},{1,2},{2,3},{3,4},{4,5},{5,6},{6,7},{8,9},{9,10},{10,11},{11... | collective-permute-start | bytes 589832 | tf_op jit(solution)/shard_map/ppermute | solution.py:22
Sparse Core Ops, SparseCore 0:
  8.9 37.6 all-gather.5
  48.2 24.0 all-gather.3
  74.7 37.3 all-reduce.2
  113.5 24.0 all-gather.7
where the time goes:
time: 183 us; the launch traced here: 181 us
  waiting for transfers between devices  59.1 us (32%)
  matrix products  51.4 us (28%)
  local copies, waits for them, and re-layouts  24.6 us (13%)
  blocking collectives  19.1 us (10%)
  between operations  15.3 us (8%)
  starting transfers between devices  6.05 us (3%)
  other arithmetic  5.4 us (3%)
    psum x1, waiting for transfers between devices, broadcast(): return lax.psum(kept, axis)  35.5 us
    dot_general x12, matrix products, one_head(): return jnp.dot(probs, head_value, preferred_element_type=jnp.float32)  24.1 us
    unnamed x1, blocking collectives  19.1 us
    dot_general x12, matrix products, one_head(): jnp.einsum('qd,kd->qk', head_query, head_key, preferred_element_type=jnp....  15.1 us
    ppermute x2, waiting for transfers between devices, shifted(): return lax.ppermute(block, axis, route)  11.8 us
    unnamed x19, local copies, waits for them, and re-layouts  11.3 us
    all_gather x1, waiting for transfers between devices, local(): lax.all_gather(w_query, 'var', axis=0, tiled=True)  9.85 us
    dot_general x1, matrix products, local(): jnp.dot(columns, lax.all_gather(w_keyval, 'var', axis=0, tiled=True), pre...  6.06 us
  transfers between devices with their start and end apart: 6, of which 4 were waited for; matrix products, arithmetic and copies ran while one was open for 43% of the time, Pallas kernels for 0%

commit v1 on v0

v1 whole, which is shorter than its diff:
```python
import functools
import math

import jax
import jax.numpy as jnp
from jax import lax
from jax.experimental import pallas as pl
from jax.experimental.pallas import tpu as pltpu
from jax.sharding import PartitionSpec as P

HEADS = 12
HS = 64
SEAM = 128
BLK = 128
TSTEPS = 1000
STRIDE = 200
LANES = 128

epsilon = 1e-06
MASKED = -1e30
VMEM_LIMIT = 56 * 1024 * 1024

BF16 = jnp.bfloat16
F32 = jnp.float32


def plan(moment):
    return jnp.cos((moment / TSTEPS + 0.008) / 1.008 * (math.pi / 2.0)) ** 2


def coefficients(timestep):
    current = timestep[0].astype(jnp.float32)
    abar_now = plan(current)
    abar_prev = plan(current - STRIDE)
    spread = jnp.sqrt((1.0 - abar_prev) / (1.0 - abar_now) * (1.0 - abar_now / abar_prev))
    carried = jnp.sqrt((1.0 - abar_prev) * (abar_now / abar_prev - abar_now) / (1.0 - abar_now))
    coef_pred = carried - jnp.sqrt(abar_prev) * jnp.sqrt(1.0 - abar_now) / jnp.sqrt(abar_now)
    coef_latent = jnp.sqrt(abar_prev / abar_now)
    return (current, coef_latent, coef_pred, spread)


def time_embedding(current, model_width):
    half_width = model_width // 2
    frequency = jnp.exp(-math.log(10000.0) * jnp.arange(half_width, dtype=jnp.float32) / half_width)
    angles = current * frequency
    return jnp.concatenate([jnp.cos(angles), jnp.sin(angles)])


def swapped(block, axis, bit):
    route = [(i, i ^ bit) for i in range(lax.axis_size(axis))]
    return lax.ppermute(block, axis, route)


def shifted(block, axis, distance):
    devices = range(lax.axis_size(axis))
    route = [(i - distance, i) for i in devices if i - distance in devices]
    return lax.ppermute(block, axis, route)


def vmem():
    return pl.BlockSpec(memory_space=pltpu.VMEM)


def smem():
    return pl.BlockSpec(memory_space=pltpu.SMEM)


def anywhere():
    return pl.BlockSpec(memory_space=pl.ANY)


def params():
    return pltpu.CompilerParams(vmem_limit_bytes=VMEM_LIMIT)


def pool_kernel(count, ids_ref, table_ref, out_ref, blocks, sems):
    def copy(j):
        start = pl.multiple_of((ids_ref[0, j] >> 7) * LANES, LANES)
        return pltpu.make_async_copy(
            table_ref.at[:, pl.ds(start, LANES)], blocks.at[j], sems.at[j]
        )

    for j in range(count):
        copy(j).start()
    lane = lax.broadcasted_iota(jnp.int32, (1, LANES), 1)
    total = jnp.zeros(blocks.shape[1:], F32)
    for j in range(count):
        copy(j).wait()
        total += jnp.where(lane == (ids_ref[0, j] & (LANES - 1)), blocks[j].astype(F32), 0.0)
    ones = jnp.full((8, LANES), 1.0 / count, F32)
    out_ref[...] = lax.dot_general(
        ones,
        total,
        (((1,), (1,)), ((), ())),
        precision=lax.Precision.HIGHEST,
        preferred_element_type=F32,
    )


def pool(prompt_ids, table_columns):
    count = prompt_ids.shape[1]
    width = table_columns.shape[0]
    pooled = pl.pallas_call(
        functools.partial(pool_kernel, count),
        out_shape=jax.ShapeDtypeStruct((8, width), F32),
        in_specs=[smem(), anywhere()],
        out_specs=vmem(),
        scratch_shapes=[
            pltpu.VMEM((count, width, LANES), BF16),
            pltpu.SemaphoreType.DMA((count,)),
        ],
        compiler_params=params(),
        name="pool_prompt",
    )(prompt_ids, table_columns)
    return pooled[:1]


def gather_pooled(pooled):
    place = lax.axis_index("tm")
    bit = 1
    while bit < lax.axis_size("tm"):
        other = swapped(pooled, "tm", bit)
        upper = (place & bit) != 0
        pooled = jnp.concatenate(
            [jnp.where(upper, other, pooled), jnp.where(upper, pooled, other)], axis=0
        )
        bit *= 2
    return pooled.reshape(1, -1)


def gather_rows(weights):
    var_count = lax.axis_size("var")
    tm_count = lax.axis_size("tm")
    rows = weights[0].shape[0]
    quarter = rows // 4
    joined = lambda parts: parts[0] if len(parts) == 1 else jnp.concatenate(parts, axis=1)
    if var_count != 4 or tm_count % 4 or quarter % 16:
        return [(joined([lax.all_gather(w, "var", axis=0, tiled=True) for w in weights]), 0)]
    var_place = lax.axis_index("var")
    corner = lax.axis_index("tm") & 3

    def cut(which):
        return joined(
            [lax.dynamic_slice_in_dim(w, which * quarter, quarter, 0) for w in weights]
        )

    own = joined(weights)
    partner = swapped(own, "var", 1)
    first = swapped(cut(corner), "var", 2)
    fourth = swapped(cut(corner ^ 3), "var", 2)
    second = swapped(first, "tm", 1)
    third = swapped(first, "tm", 2)
    pieces = [(own, var_place * rows), (partner, (var_place ^ 1) * rows)]
    for k, piece in enumerate((first, second, third, fourth)):
        offset = (corner ^ k) * quarter
        pieces.append((piece, (var_place ^ 2) * rows + offset))
        pieces.append((swapped(piece, "var", 1), (var_place ^ 3) * rows + offset))
    return pieces


def project_kernel(
    n_pieces, column_from, places_ref, latent_ref, halo_ref, scale_ref, *refs
):
    pieces, (out_ref, weights, normed, sems) = refs[:n_pieces], refs[n_pieces:]
    copies = []
    for k, piece in enumerate(pieces):
        rows = piece.shape[0]
        start = pl.multiple_of(places_ref[k], 16)
        copies.append(
            pltpu.make_async_copy(
                piece.at[:, column_from:], weights.at[pl.ds(start, rows), :], sems.at[k]
            )
        )
    for copy in copies:
        copy.start()
    own_rows = latent_ref.shape[0]
    width = latent_ref.shape[1]
    scale = 1.0 + scale_ref[...]
    for begin, ref in ((0, latent_ref), (own_rows, halo_ref)):
        for row in range(0, ref.shape[0], 64):
            values = ref[row : row + 64, :].astype(F32)
            inv_norm = lax.rsqrt(jnp.sum(values * values, axis=-1, keepdims=True) / width + epsilon)
            normed[begin + row : begin + row + 64, :] = (values * inv_norm * scale).astype(BF16)
    for copy in copies:
        copy.wait()
    columns = out_ref.shape[1]
    step = 256

    def body(n, carry):
        at = pl.ds(pl.multiple_of(n * step, step), step)
        out_ref[:, at] = jnp.dot(
            normed[...], weights[:, at], preferred_element_type=F32
        ).astype(BF16)
        return carry

    lax.fori_loop(0, columns // step, body, 0)


def project(name, latent, halo, condition, pieces, column_from):
    rows = latent.shape[0] + halo.shape[0]
    width = latent.shape[1]
    columns = pieces[0][0].shape[1] - column_from
    places = jnp.stack([jnp.asarray(place, jnp.int32) for _, place in pieces])
    return pl.pallas_call(
        functools.partial(project_kernel, len(pieces), column_from),
        out_shape=jax.ShapeDtypeStruct((rows, columns), BF16),
        in_specs=[smem(), vmem(), vmem(), vmem()] + [anywhere()] * len(pieces),
        out_specs=vmem(),
        scratch_shapes=[
            pltpu.VMEM((width, columns), BF16),
            pltpu.VMEM((rows, width), BF16),
            pltpu.SemaphoreType.DMA((len(pieces),)),
        ],
        compiler_params=params(),
        cost_estimate=pl.CostEstimate(
            flops=2 * rows * width * columns, bytes_accessed=2 * width * columns, transcendentals=0
        ),
        name=name,
    )(places, latent, halo, condition, *[piece for piece, _ in pieces])


def attend_rows(query, own_ref, source_ref, bias, pair):
    head_width = own_ref.shape[1] // 2
    blocks = own_ref.shape[0] // BLK
    at = pl.ds(pair * LANES, LANES)
    value_at = pl.ds(head_width + pair * LANES, LANES)
    left = lax.broadcasted_iota(jnp.int32, (1, LANES), 1) < HS
    zero = jnp.zeros((), BF16)
    both = jnp.concatenate([jnp.where(left, query, zero), jnp.where(left, zero, query)], axis=0)
    score_parts = []
    for ref in (own_ref, source_ref):
        score_parts.append(
            lax.dot_general(
                both, ref[:, at], (((1,), (1,)), ((), ())), preferred_element_type=F32
            )
        )
    cut = lambda part, j: part[:, j * BLK : (j + 1) * BLK]
    peak = None
    for j in range(blocks):
        top = jnp.maximum(cut(score_parts[0], j), cut(score_parts[1], j))
        if j:
            top = top + bias[j]
        peak = top if peak is None else jnp.maximum(peak, top)
    peak = jnp.max(peak, axis=-1, keepdims=True)
    total = None
    ones = jnp.ones((own_ref.shape[0], LANES), BF16)
    for part, ref in zip(score_parts, (own_ref, source_ref)):
        weights = jnp.concatenate(
            [jnp.exp(cut(part, j) - (peak - bias[j])).astype(BF16) for j in range(blocks)], axis=1
        )
        values = jnp.concatenate([ref[:, value_at], ones], axis=1)
        term = jnp.dot(weights, values, preferred_element_type=F32)
        total = term if total is None else total + term
    mixed = total[:, :LANES] / total[:, LANES:]
    return jnp.where(left, mixed[:BLK], mixed[BLK:])


def tail_kernel(bias_ref, query_ref, own_ref, source_ref, out_ref):
    blocks = own_ref.shape[0] // BLK
    row = lax.broadcasted_iota(jnp.int32, (BLK, 1), 0).astype(F32)
    fade = 1.0 - (row + 0.5) / SEAM
    bias = [bias_ref[blocks - 1, j] for j in range(blocks)]
    for pair in range(HEADS // 2):
        at = pl.ds(pair * LANES, LANES)
        query = query_ref[(blocks - 1) * BLK :, at] * BF16(1.0 / math.sqrt(HS))
        out_ref[:, at] = (attend_rows(query, own_ref, source_ref, bias, pair) * fade).astype(BF16)


def main_kernel(bias_ref, query_ref, own_ref, source_ref, out_ref):
    blocks = own_ref.shape[0] // BLK
    for i in range(blocks - 1):
        bias = [bias_ref[i, j] for j in range(blocks)]
        for pair in range(HEADS // 2):
            at = pl.ds(pair * LANES, LANES)
            rows = pl.ds(i * BLK, BLK)
            query = query_ref[rows, at] * BF16(1.0 / math.sqrt(HS))
            out_ref[rows, at] = attend_rows(query, own_ref, source_ref, bias, pair)


def attend(name, kernel, rows, dtype, bias, query, own, source):
    width = own.shape[1] // 2
    return pl.pallas_call(
        kernel,
        out_shape=jax.ShapeDtypeStruct((rows, width), dtype),
        in_specs=[smem(), vmem(), vmem(), vmem()],
        out_specs=vmem(),
        compiler_params=params(),
        cost_estimate=pl.CostEstimate(
            flops=16 * rows * own.shape[0] * width, bytes_accessed=0, transcendentals=0
        ),
        name=name,
    )(bias, query, own, source)


def finish_kernel(
    n_pieces, places_ref, coef_ref, attended_ref, received_ref, latent_ref, noise_ref, *refs
):
    pieces, (out_ref, weights, sems) = refs[:n_pieces], refs[n_pieces:]
    copies = []
    for k, piece in enumerate(pieces):
        start = pl.multiple_of(places_ref[k], 16)
        copies.append(
            pltpu.make_async_copy(
                piece, weights.at[pl.ds(start, piece.shape[0]), :], sems.at[k]
            )
        )
    for copy in copies:
        copy.start()
    row = lax.broadcasted_iota(jnp.int32, (SEAM, 1), 0).astype(F32)
    ramp_up = jnp.where(coef_ref[3] > 0.5, 1.0, (row + 0.5) / SEAM)
    lead = attended_ref[:SEAM, :] * ramp_up + received_ref[...].astype(F32)
    blended = jnp.concatenate([lead, attended_ref[SEAM:, :]], axis=0).astype(BF16)
    for copy in copies:
        copy.wait()
    step = 256
    for begin in range(0, out_ref.shape[1], step):
        at = pl.ds(begin, step)
        prediction = jnp.dot(blended, weights[:, at], preferred_element_type=F32)
        result = (
            coef_ref[0] * latent_ref[:, at].astype(F32)
            + coef_ref[1] * prediction
            + coef_ref[2] * noise_ref[:, at].astype(F32)
        )
        out_ref[:, at] = result.astype(BF16)


def finish(coefs, attended, received, latent, noise, pieces):
    places = jnp.stack([jnp.asarray(place, jnp.int32) for _, place in pieces])
    return pl.pallas_call(
        functools.partial(finish_kernel, len(pieces)),
        out_shape=jax.ShapeDtypeStruct(latent.shape, BF16),
        in_specs=[smem(), smem()] + [vmem()] * 4 + [anywhere()] * len(pieces),
        out_specs=vmem(),
        scratch_shapes=[
            pltpu.VMEM((attended.shape[1], latent.shape[1]), BF16),
            pltpu.SemaphoreType.DMA((len(pieces),)),
        ],
        compiler_params=params(),
        name="blend_and_step",
    )(places, coefs, attended, received, latent, noise, *[piece for piece, _ in pieces])


def broadcast(value, axis):
    count = lax.axis_size(axis)
    place = lax.axis_index(axis)
    step = count // 2
    while step:
        route = [(i, i + step) for i in range(0, count, 2 * step)]
        arrived = lax.ppermute(value, axis, route)
        value = jnp.where((place & step) != 0, arrived, value)
        step //= 2
    return value


def local(
    latent, fresh_noise, timestep, prompt_ids, block_table, prompt_table, w_query, w_keyval, w_out
):
    latent = latent[0]
    own_rows, model_width = latent.shape
    head_width = w_query.shape[1]
    tm_count = lax.axis_size("tm")
    tm_place = lax.axis_index("tm")

    halo = shifted(latent[:SEAM], "tm", -1)
    pieces = gather_rows([w_query, w_keyval])
    pooled = gather_pooled(pool(prompt_ids, prompt_table.T))
    source_pooled = broadcast(pooled, "var")
    source_window = broadcast(jnp.concatenate([latent, halo], axis=0), "var")
    out_pieces = gather_rows([w_out])

    current, coef_latent, coef_pred, spread = coefficients(timestep)
    embedded = time_embedding(current, model_width)[None, :]
    first = (tm_place == 0).astype(F32)
    coefs = jnp.stack([coef_latent, coef_pred, spread, first])

    blocks = block_table.shape[0]
    present = (jnp.arange(blocks) < own_rows // BLK) | (tm_place != tm_count - 1)
    bias = jnp.where((block_table > 0) & present[None, :], 0.0, MASKED).astype(F32)

    window = project("project_own", latent, halo, embedded + pooled, pieces, 0)
    query, own = window[:, :head_width], window[:, head_width:]
    source = project(
        "project_source",
        source_window[:own_rows],
        source_window[own_rows:],
        embedded + source_pooled,
        pieces,
        head_width,
    )
    tail = attend("attend_tail", tail_kernel, SEAM, BF16, bias, query, own, source)
    received = shifted(tail, "tm", 1)
    attended = attend("attend_main", main_kernel, own_rows, F32, bias, query, own, source)
    return finish(coefs, attended, received, latent, fresh_noise[0], out_pieces)[None]


def solution(mesh):
    placed = (
        P("var", "tm", None),
        P("var", "tm", None),
        P(),
        P("var", None),
        P(),
        P(None, "tm"),
        P("var", None),
        P("var", None),
        P("var", None),
    )
    return jax.shard_map(
        local, mesh=mesh, in_specs=placed, out_specs=P("var", "tm", None), check_vma=False
    )
```

time: 183 us -> 118 us (0.64)
  the two profiles are of different devices: /device:TPU:10 before, /device:TPU:0 now
where the time goes in v1:
time: 118 us; the launch traced here: 117 us
  Pallas kernels  39.2 us (33%)
  starting transfers between devices  33.5 us (28%)
  waiting for transfers between devices  24.2 us (21%)
  local copies, waits for them, and re-layouts  12.8 us (11%)
  other arithmetic  5.9 us (5%)
  between operations  1.76 us (1%)
    ppermute x21, starting transfers between devices, swapped(): return lax.ppermute(block, axis, route)  18.9 us
    pallas_call x2, Pallas kernels, project(): pl.pallas_call(functools.partial(project_kernel, len(pieces), column_from...  17.4 us
    ppermute x21, waiting for transfers between devices, swapped(): return lax.ppermute(block, axis, route)  15.4 us
    pallas_call x2, Pallas kernels, attend(): pl.pallas_call(kernel, out_shape=jax.ShapeDtypeStruct((rows, width), dtyp...  12.6 us
    ppermute x4, starting transfers between devices, broadcast(): arrived = lax.ppermute(value, axis, route)  10 us
    ppermute x4, waiting for transfers between devices, broadcast(): arrived = lax.ppermute(value, axis, route)  8.78 us
    pallas_call x1, Pallas kernels, finish(): pl.pallas_call(functools.partial(finish_kernel, len(pieces)), out_shape=j...  5.07 us
    ppermute x2, starting transfers between devices, shifted(): return lax.ppermute(block, axis, route)  4.62 us
  transfers between devices with their start and end apart: 27, of which 6 were waited for; matrix products, arithmetic and copies ran while one was open for 15% of the time, Pallas kernels for 26%

profile of v1, /device:TPU:0, one launch (start us, length us, event | category | flops | bytes accessed | tf_op | source)
XLA Modules:
  0.0 117.4 jit_solution(2170814741547363555)
XLA Ops:
  0.0 4.2 %pool_prompt.1 = f32[8,192]{1,0:T(8,128)} custom-call(s32[1,64]{1,0:T(1,128)} %ids_ref.1, bf16[192,16384]{1,0:T(8,128)(2,1)} %bitcast.35), custom_call_target="tpu_custom_call" | custom-call | tf_op jit(solution)/shard_map/pool_prompt/pallas_call | solution.py:103
  5.0 3.0 %collective-permute-start.1 = (f32[1,192]{1,0:T(1,128)S(1)}, f32[1,192]{1,0:T(1,128)S(1)}, u32[]{:S(2)}, u32[]{:S(2)}) collective-permute-start(f32[1,192]{1,0:T(1,128)S(1)} %slice.28), channel_id=1, source_target_pairs={{0,1},{1,0},{2,3},{3,2},{4,5},{5,4},{6,7},{7,6},{8,9},{9,8},{10,11... | collective-permute-start | bytes 2312 | tf_op jit(solution)/shard_map/ppermute | solution.py:51
  8.0 0.8 pad_maximum_fusion.1
  8.8 1.5 %collective-permute-start.5 = (bf16[96,2304]{1,0:T(8,128)(2,1)}, bf16[96,2304]{1,0:T(8,128)(2,1)}, u32[]{:S(2)}, u32[]{:S(2)}) collective-permute-start(bf16[96,2304]{1,0:T(8,128)(2,1)} %pad_maximum_fusion.1), channel_id=1, source_target_pairs={{0,16},{8,24},{16,0},{24,8},{1,17},{9,25},{17,1},{25,9},{2,18},{10... | collective-permute-start | bytes 1327112 | tf_op jit(solution)/shard_map/ppermute | solution.py:51
  11.7 1.3 %collective-permute-start = (bf16[128,1536]{1,0:T(8,128)(2,1)}, bf16[128,1536]{1,0:T(8,128)(2,1)S(1)}, u32[]{:S(2)}, u32[]{:S(2)}) collective-permute-start(bf16[128,1536]{1,0:T(8,128)(2,1)} %slice_bitcast_fusion), channel_id=1, source_target_pairs={{1,0},{2,1},{3,2},{4,3},{5,4},{6,5},{7,6},{9,8},{10,9},{11,10},{12... | collective-permute-start | bytes 1179656 | tf_op jit(solution)/shard_map/ppermute | solution.py:57
  13.0 1.0 constant_dynamic-update-slice_fusion.1
  14.7 2.4 %collective-permute-start.2 = (f32[2,192]{1,0:T(2,128)S(1)}, f32[2,192]{1,0:T(2,128)S(1)}, u32[]{:S(2)}, u32[]{:S(2)}) collective-permute-start(f32[2,192]{1,0:T(2,128)S(1)} %pad_maximum_fusion.6), channel_id=1, source_target_pairs={{0,2},{1,3},{2,0},{3,1},{4,6},{5,7},{6,4},{7,5},{8,10},{9,11},{10,... | collective-permute-start | bytes 4616 | tf_op jit(solution)/shard_map/ppermute | solution.py:51
  17.1 1.2 %constant_dynamic-update-slice_fusion.refs_0_ = bf16[384,2304]{1,0:T(8,128)(2,1)} fusion(bf16[384,2304]{1,0:T(8,128)(2,1)} %constant_dynamic-update-slice_fusion.1, bf16[384,1536]{1,0:T(8,128)(2,1)S(1)} %copy-done.1), kind=kLoop, calls=%fused_computation.12 | loop fusion | bytes 2359296 | tf_op jit(solution)/shard_map/concatenate | solution.py:136
  18.3 5.6 %collective-permute-done.2 = f32[2,192]{1,0:T(2,128)S(1)} collective-permute-done((f32[2,192]{1,0:T(2,128)S(1)}, f32[2,192]{1,0:T(2,128)S(1)}, u32[]{:S(2)}, u32[]{:S(2)}) %collective-permute-start.2) | collective-permute-done | bytes 1568 | tf_op jit(solution)/shard_map/ppermute | solution.py:51
  24.0 4.6 %collective-permute-start.13 = (bf16[384,1536]{1,0:T(8,128)(2,1)S(1)}, bf16[384,1536]{1,0:T(8,128)(2,1)}, u32[]{:S(2)}, u32[]{:S(2)}) collective-permute-start(bf16[384,1536]{1,0:T(8,128)(2,1)S(1)} %pad_maximum_fusion), channel_id=1, source_target_pairs={{0,16},{1,17},{2,18},{3,19},{4,20},{5,21},{6,22},{7,23}} | collective-permute-start | bytes 3538952 | tf_op jit(solution)/shard_map/ppermute | solution.py:349
  28.5 2.6 %collective-permute-start.3 = (f32[4,192]{1,0:T(4,128)S(1)}, f32[4,192]{1,0:T(4,128)S(1)}, u32[]{:S(2)}, u32[]{:S(2)}) collective-permute-start(f32[4,192]{1,0:T(4,128)S(1)} %pad_maximum_fusion.5), channel_id=1, source_target_pairs={{0,4},{1,5},{2,6},{3,7},{4,0},{5,1},{6,2},{7,3},{8,12},{9,13},{10,... | collective-permute-start | bytes 9224 | tf_op jit(solution)/shard_map/ppermute | solution.py:51
  33.2 1.9 %collective-permute-start.15 = (f32[1,1536]{1,0:T(1,128)S(1)}, f32[1,1536]{1,0:T(1,128)}, u32[]{:S(2)}, u32[]{:S(2)}) collective-permute-start(f32[1,1536]{1,0:T(1,128)S(1)} %reshape.42), channel_id=1, source_target_pairs={{0,16},{1,17},{2,18},{3,19},{4,20},{5,21},{6,22},{7,23}} | collective-permute-start | bytes 18440 | tf_op jit(solution)/shard_map/ppermute | solution.py:349
  35.2 8.3 %collective-permute-done.15 = f32[1,1536]{1,0:T(1,128)} collective-permute-done((f32[1,1536]{1,0:T(1,128)S(1)}, f32[1,1536]{1,0:T(1,128)}, u32[]{:S(2)}, u32[]{:S(2)}) %collective-permute-start.15) | collective-permute-done | bytes 6176 | tf_op jit(solution)/shard_map/ppermute | solution.py:349
  43.4 2.6 %collective-permute-start.19 = (bf16[48,1536]{1,0:T(8,128)(2,1)S(1)}, bf16[48,1536]{1,0:T(8,128)(2,1)}, u32[]{:S(2)}, u32[]{:S(2)}) collective-permute-start(bf16[48,1536]{1,0:T(8,128)(2,1)S(1)} %get-tuple-element.8), channel_id=1, source_target_pairs={{0,16},{8,24},{16,0},{24,8},{1,17},{9,25},{17,1},{25,9},{2,18},{10... | collective-permute-start | bytes 442376 | tf_op jit(solution)/shard_map/ppermute | solution.py:51
  46.7 1.3 %collective-permute-start.16 = (f32[1,1536]{1,0:T(1,128)S(1)}, f32[1,1536]{1,0:T(1,128)S(1)}, u32[]{:S(2)}, u32[]{:S(2)}) collective-permute-start(f32[1,1536]{1,0:T(1,128)S(1)} %get-tuple-element.15), channel_id=1, source_target_pairs={{0,8},{16,24},{1,9},{17,25},{2,10},{18,26},{3,11},{19,27},{4,12},{... | collective-permute-start | bytes 18440 | tf_op jit(solution)/shard_map/ppermute | solution.py:349
  48.7 2.3 %collective-permute-start.14 = (bf16[384,1536]{1,0:T(8,128)(2,1)S(1)}, bf16[384,1536]{1,0:T(8,128)(2,1)S(1)}, u32[]{:S(2)}, u32[]{:S(2)}) collective-permute-start(bf16[384,1536]{1,0:T(8,128)(2,1)S(1)} %broadcast_select_fusion), channel_id=1, source_target_pairs={{0,8},{16,24},{1,9},{17,25},{2,10},{18,26},{3,11},{19,27},{4,12},{... | collective-permute-start | bytes 3538952 | tf_op jit(solution)/shard_map/ppermute | solution.py:349
  52.4 1.6 %collective-permute-start.9 = (bf16[96,2304]{1,0:T(8,128)(2,1)}, bf16[96,2304]{1,0:T(8,128)(2,1)S(1)}, u32[]{:S(2)}, u32[]{:S(2)}) collective-permute-start(bf16[96,2304]{1,0:T(8,128)(2,1)} %collective-permute-done.5.refs_2_), channel_id=1, source_target_pairs={{0,2},{1,3},{2,0},{3,1},{4,6},{5,7},{6,4},{7,5},{8,10},{9,11},{10,... | collective-permute-start | bytes 1327112 | tf_op jit(solution)/shard_map/ppermute | solution.py:51
  54.8 1.3 %and_select_fusion.bias_ref = f32[3,3]{1,0:T(4,128)} fusion(s32[3,3]{1,0:T(4,128)} %param.13, pred[3]{0:T(512)(128)(4,1)S(1)} %compare_or_fusion), kind=kLoop, calls=%fused_computation.25 | loop fusion | flops 27 | bytes 75 | tf_op jit(solution)/shard_map/jit(_where)/select_n | solution.py:378
  56.0 7.9 %collective-permute-done.9.refs_6_ = bf16[96,2304]{1,0:T(8,128)(2,1)S(1)} collective-permute-done((bf16[96,2304]{1,0:T(8,128)(2,1)}, bf16[96,2304]{1,0:T(8,128)(2,1)S(1)}, u32[]{:S(2)}, u32[]{:S(2)}) %collective-permute-start.9) | collective-permute-done | bytes 442400 | tf_op jit(solution)/shard_map/ppermute | solution.py:51
  64.0 1.3 %collective-permute-done.7.refs_4_ = bf16[96,2304]{1,0:T(8,128)(2,1)S(1)} collective-permute-done((bf16[96,2304]{1,0:T(8,128)(2,1)}, bf16[96,2304]{1,0:T(8,128)(2,1)S(1)}, u32[]{:S(2)}, u32[]{:S(2)}) %collective-permute-start.7) | collective-permute-done | bytes 442400 | tf_op jit(solution)/shard_map/ppermute | solution.py:51
  65.8 1.3 %fusion.scale_ref = f32[1,1536]{1,0:T(1,128)} fusion(f32[1,1536]{1,0:T(1,128)S(1)} %collective-permute-done.16, f32[1,1536]{1,0:T(1,128)} %copy-done.13, pred[]{:T(512)S(6)} %ne.24, f32[1536]{0:T(1024)S(1)} %pad_maximum_fusion.4), kind=kLoop, calls=%fused_computation.10 | loop fusion | flops 3072 | bytes 24577 | tf_op jit(solution)/shard_map/add | solution.py:386
  68.7 0.8 collective-permute-start.23
  69.5 9.8 %project_own.1 = bf16[384,2304]{1,0:T(8,128)(2,1)} custom-call(s32[10]{0:T(128)} %stack.122.places_ref, bf16[256,1536]{1,0:T(8,128)(2,1)} %bitcast.31, bf16[128,1536]{1,0:T(8,128)(2,1)} %copy-done.2, f32[1,1536]{1,0:T(1,128)} %get-tuple-element.16.scale_ref, bf16[384,2304]{1,0:T(8,128)(2,1)} %constant_dynamic-update-slice_fusion.refs_0_, ...), custom_call_target="tpu_custom_call" | custom-call | flops 2717908992 | bytes 7077888 | tf_op jit(solution)/shard_map/project_own/pallas_call | solution.py:204
  79.3 2.4 %slice.30.own_ref = bf16[384,1536]{1,0:T(8,128)(2,1)} slice(bf16[384,2304]{1,0:T(8,128)(2,1)} %project_own.1), slice={[0:384], [768:2304]} | slice | bytes 2359296 | tf_op jit(solution)/shard_map/slice | solution.py:381
  81.7 1.9 %slice.29.query_ref = bf16[384,768]{1,0:T(8,128)(2,1)} slice(bf16[384,2304]{1,0:T(8,128)(2,1)} %project_own.1), slice={[0:384], [0:768]} | slice | bytes 1179648 | tf_op jit(solution)/shard_map/slice | solution.py:381
  84.8 0.9 slice.31.latent_ref
  85.8 0.8 slice.32.halo_ref
  86.5 7.6 %project_source.1.source_ref = bf16[384,1536]{1,0:T(8,128)(2,1)} custom-call(s32[10]{0:T(128)} %stack.122.places_ref, bf16[256,1536]{1,0:T(8,128)(2,1)} %slice.31.latent_ref, bf16[128,1536]{1,0:T(8,128)(2,1)} %slice.32.halo_ref, f32[1,1536]{1,0:T(1,128)} %fusion.scale_ref, bf16[384,2304]{1,0:T(8,128)(2,1)} %constant_dynamic-update-slice_fusion.refs_0_, ...), custom_call_target="tpu_custom_call" | custom-call | flops 1811939328 | bytes 4718592 | tf_op jit(solution)/shard_map/project_source/pallas_call | solution.py:204
  94.1 5.0 %attend_tail.1 = bf16[128,768]{1,0:T(8,128)(2,1)} custom-call(f32[3,3]{1,0:T(4,128)} %and_select_fusion.bias_ref, bf16[384,768]{1,0:T(8,128)(2,1)} %slice.29.query_ref, bf16[384,1536]{1,0:T(8,128)(2,1)} %slice.30.own_ref, bf16[384,1536]{1,0:T(8,128)(2,1)} %project_source.1.source_ref), custom_call_target="tpu_custom_call" | custom-call | flops 603979776 | tf_op jit(solution)/shard_map/attend_tail/pallas_call | solution.py:282
  99.1 3.3 %collective-permute-start.17 = (bf16[128,768]{1,0:T(8,128)(2,1)}, bf16[128,768]{1,0:T(8,128)(2,1)S(1)}, u32[]{:S(2)}, u32[]{:S(2)}) collective-permute-start(bf16[128,768]{1,0:T(8,128)(2,1)} %attend_tail.1), channel_id=1, source_target_pairs={{0,1},{1,2},{2,3},{3,4},{4,5},{5,6},{6,7},{8,9},{9,10},{10,11},{11... | collective-permute-start | bytes 589832 | tf_op jit(solution)/shard_map/ppermute | solution.py:57
  103.7 7.6 %attend_main.1.attended_ref = f32[256,768]{1,0:T(8,128)} custom-call(f32[3,3]{1,0:T(4,128)} %and_select_fusion.bias_ref, bf16[384,768]{1,0:T(8,128)(2,1)} %slice.29.query_ref, bf16[384,1536]{1,0:T(8,128)(2,1)} %slice.30.own_ref, bf16[384,1536]{1,0:T(8,128)(2,1)} %project_source.1.source_ref), custom_call_target="tpu_custom_call" | custom-call | flops 1207959552 | tf_op jit(solution)/shard_map/attend_main/pallas_call | solution.py:282
  112.2 5.1 %blend_and_step.1 = bf16[256,1536]{1,0:T(8,128)(2,1)} custom-call(s32[10]{0:T(128)} %stack.105.places_ref, f32[4]{0:T(128)} %pad_maximum_fusion.7.coef_ref, f32[256,768]{1,0:T(8,128)} %attend_main.1.attended_ref, bf16[128,768]{1,0:T(8,128)(2,1)} %copy-done.12, bf16[256,1536]{1,0:T(8,128)(2,1)} %bitcast.32, bf16[256,1536]{1,0:T(8,128)(2,1)} %bitcast.36, ...), custom_call_target="tpu_custom_call" | custom-call | tf_op jit(solution)/shard_map/blend_and_step/pallas_call | solution.py:329
  (90 shorter events, 12.7 us)
Async XLA Ops:
  0.0 7.9 %copy-start.1 = (bf16[384,1536]{1,0:T(8,128)(2,1)S(1)}, bf16[384,1536]{1,0:T(8,128)(2,1)}, u32[]{:S(2)}) copy-start(bf16[384,1536]{1,0:T(8,128)(2,1)} %param.16) | copy-start | bytes 3538948
  5.0 9.0 %collective-permute-start.1 = (f32[1,192]{1,0:T(1,128)S(1)}, f32[1,192]{1,0:T(1,128)S(1)}, u32[]{:S(2)}, u32[]{:S(2)}) collective-permute-start(f32[1,192]{1,0:T(1,128)S(1)} %slice.28), channel_id=1, source_target_pairs={{0,1},{1,0},{2,3},{3,2},{4,5},{5,4},{6,7},{7,6},{8,9},{9,8},{10,11... | collective-permute-start | bytes 2312 | tf_op jit(solution)/shard_map/ppermute | solution.py:51
  8.8 43.5 %collective-permute-start.5 = (bf16[96,2304]{1,0:T(8,128)(2,1)}, bf16[96,2304]{1,0:T(8,128)(2,1)}, u32[]{:S(2)}, u32[]{:S(2)}) collective-permute-start(bf16[96,2304]{1,0:T(8,128)(2,1)} %pad_maximum_fusion.1), channel_id=1, source_target_pairs={{0,16},{8,24},{16,0},{24,8},{1,17},{9,25},{17,1},{25,9},{2,18},{10... | collective-permute-start | bytes 1327112 | tf_op jit(solution)/shard_map/ppermute | solution.py:51
  10.4 44.4 %collective-permute-start.11 = (bf16[96,2304]{1,0:T(8,128)(2,1)S(1)}, bf16[96,2304]{1,0:T(8,128)(2,1)}, u32[]{:S(2)}, u32[]{:S(2)}) collective-permute-start(bf16[96,2304]{1,0:T(8,128)(2,1)S(1)} %pad_maximum_fusion.2), channel_id=1, source_target_pairs={{0,16},{8,24},{16,0},{24,8},{1,17},{9,25},{17,1},{25,9},{2,18},{10... | collective-permute-start | bytes 1327112 | tf_op jit(solution)/shard_map/ppermute | solution.py:51
  11.7 12.1 %collective-permute-start = (bf16[128,1536]{1,0:T(8,128)(2,1)}, bf16[128,1536]{1,0:T(8,128)(2,1)S(1)}, u32[]{:S(2)}, u32[]{:S(2)}) collective-permute-start(bf16[128,1536]{1,0:T(8,128)(2,1)} %slice_bitcast_fusion), channel_id=1, source_target_pairs={{1,0},{2,1},{3,2},{4,3},{5,4},{6,5},{7,6},{9,8},{10,9},{11,10},{12... | collective-permute-start | bytes 1179656 | tf_op jit(solution)/shard_map/ppermute | solution.py:57
  14.7 9.1 %collective-permute-start.2 = (f32[2,192]{1,0:T(2,128)S(1)}, f32[2,192]{1,0:T(2,128)S(1)}, u32[]{:S(2)}, u32[]{:S(2)}) collective-permute-start(f32[2,192]{1,0:T(2,128)S(1)} %pad_maximum_fusion.6), channel_id=1, source_target_pairs={{0,2},{1,3},{2,0},{3,1},{4,6},{5,7},{6,4},{7,5},{8,10},{9,11},{10,... | collective-permute-start | bytes 4616 | tf_op jit(solution)/shard_map/ppermute | solution.py:51
  18.3 50.4 %collective-permute-start.4 = (bf16[384,2304]{1,0:T(8,128)(2,1)}, bf16[384,2304]{1,0:T(8,128)(2,1)}, u32[]{:S(2)}, u32[]{:S(2)}) collective-permute-start(bf16[384,2304]{1,0:T(8,128)(2,1)} %constant_dynamic-update-slice_fusion.refs_0_), channel_id=1, source_target_pairs={{0,8},{8,0},{16,24},{24,16},{1,9},{9,1},{17,25},{25,17},{2,10},{10... | collective-permute-start | bytes 5308424 | tf_op jit(solution)/shard_map/ppermute | solution.py:51
  23.9 24.1 %copy-start.2 = (bf16[128,1536]{1,0:T(8,128)(2,1)}, bf16[128,1536]{1,0:T(8,128)(2,1)S(1)}, u32[]{:S(2)}) copy-start(bf16[128,1536]{1,0:T(8,128)(2,1)S(1)} %collective-permute-done.halo_ref) | copy-start | bytes 1179652
  23.9 7.3 %copy-start.3 = (bf16[192,1536]{1,0:T(8,128)(2,1)S(1)}, bf16[192,1536]{1,0:T(8,128)(2,1)}, u32[]{:S(2)}) copy-start(bf16[192,1536]{1,0:T(8,128)(2,1)} %refs_0_.1) | copy-start | bytes 1769476
  24.0 22.7 %collective-permute-start.13 = (bf16[384,1536]{1,0:T(8,128)(2,1)S(1)}, bf16[384,1536]{1,0:T(8,128)(2,1)}, u32[]{:S(2)}, u32[]{:S(2)}) collective-permute-start(bf16[384,1536]{1,0:T(8,128)(2,1)S(1)} %pad_maximum_fusion), channel_id=1, source_target_pairs={{0,16},{1,17},{2,18},{3,19},{4,20},{5,21},{6,22},{7,23}} | collective-permute-start | bytes 3538952 | tf_op jit(solution)/shard_map/ppermute | solution.py:349
  28.5 4.6 %collective-permute-start.3 = (f32[4,192]{1,0:T(4,128)S(1)}, f32[4,192]{1,0:T(4,128)S(1)}, u32[]{:S(2)}, u32[]{:S(2)}) collective-permute-start(f32[4,192]{1,0:T(4,128)S(1)} %pad_maximum_fusion.5), channel_id=1, source_target_pairs={{0,4},{1,5},{2,6},{3,7},{4,0},{5,1},{6,2},{7,3},{8,12},{9,13},{10,... | collective-permute-start | bytes 9224 | tf_op jit(solution)/shard_map/ppermute | solution.py:51
  33.2 10.2 %collective-permute-start.15 = (f32[1,1536]{1,0:T(1,128)S(1)}, f32[1,1536]{1,0:T(1,128)}, u32[]{:S(2)}, u32[]{:S(2)}) collective-permute-start(f32[1,1536]{1,0:T(1,128)S(1)} %reshape.42), channel_id=1, source_target_pairs={{0,16},{1,17},{2,18},{3,19},{4,20},{5,21},{6,22},{7,23}} | collective-permute-start | bytes 18440 | tf_op jit(solution)/shard_map/ppermute | solution.py:349
  43.4 10.5 %collective-permute-start.19 = (bf16[48,1536]{1,0:T(8,128)(2,1)S(1)}, bf16[48,1536]{1,0:T(8,128)(2,1)}, u32[]{:S(2)}, u32[]{:S(2)}) collective-permute-start(bf16[48,1536]{1,0:T(8,128)(2,1)S(1)} %get-tuple-element.8), channel_id=1, source_target_pairs={{0,16},{8,24},{16,0},{24,8},{1,17},{9,25},{17,1},{25,9},{2,18},{10... | collective-permute-start | bytes 442376 | tf_op jit(solution)/shard_map/ppermute | solution.py:51
  46.7 2.1 %collective-permute-start.16 = (f32[1,1536]{1,0:T(1,128)S(1)}, f32[1,1536]{1,0:T(1,128)S(1)}, u32[]{:S(2)}, u32[]{:S(2)}) collective-permute-start(f32[1,1536]{1,0:T(1,128)S(1)} %get-tuple-element.15), channel_id=1, source_target_pairs={{0,8},{16,24},{1,9},{17,25},{2,10},{18,26},{3,11},{19,27},{4,12},{... | collective-permute-start | bytes 18440 | tf_op jit(solution)/shard_map/ppermute | solution.py:349
  48.7 35.5 %collective-permute-start.14 = (bf16[384,1536]{1,0:T(8,128)(2,1)S(1)}, bf16[384,1536]{1,0:T(8,128)(2,1)S(1)}, u32[]{:S(2)}, u32[]{:S(2)}) collective-permute-start(bf16[384,1536]{1,0:T(8,128)(2,1)S(1)} %broadcast_select_fusion), channel_id=1, source_target_pairs={{0,8},{16,24},{1,9},{17,25},{2,10},{18,26},{3,11},{19,27},{4,12},{... | collective-permute-start | bytes 3538952 | tf_op jit(solution)/shard_map/ppermute | solution.py:349
  52.4 11.6 %collective-permute-start.9 = (bf16[96,2304]{1,0:T(8,128)(2,1)}, bf16[96,2304]{1,0:T(8,128)(2,1)S(1)}, u32[]{:S(2)}, u32[]{:S(2)}) collective-permute-start(bf16[96,2304]{1,0:T(8,128)(2,1)} %collective-permute-done.5.refs_2_), channel_id=1, source_target_pairs={{0,2},{1,3},{2,0},{3,1},{4,6},{5,7},{6,4},{7,5},{8,10},{9,11},{10,... | collective-permute-start | bytes 1327112 | tf_op jit(solution)/shard_map/ppermute | solution.py:51
  54.0 11.3 %collective-permute-start.7 = (bf16[96,2304]{1,0:T(8,128)(2,1)}, bf16[96,2304]{1,0:T(8,128)(2,1)S(1)}, u32[]{:S(2)}, u32[]{:S(2)}) collective-permute-start(bf16[96,2304]{1,0:T(8,128)(2,1)} %collective-permute-done.5.refs_2_), channel_id=1, source_target_pairs={{0,1},{1,0},{2,3},{3,2},{4,5},{5,4},{6,7},{7,6},{8,9},{9,8},{10,11... | collective-permute-start | bytes 1327112 | tf_op jit(solution)/shard_map/ppermute | solution.py:51
  54.7 10.6 %collective-permute-start.6 = (bf16[96,2304]{1,0:T(8,128)(2,1)}, bf16[96,2304]{1,0:T(8,128)(2,1)S(1)}, u32[]{:S(2)}, u32[]{:S(2)}) collective-permute-start(bf16[96,2304]{1,0:T(8,128)(2,1)} %collective-permute-done.5.refs_2_), channel_id=1, source_target_pairs={{0,8},{8,0},{16,24},{24,16},{1,9},{9,1},{17,25},{25,17},{2,10},{10... | collective-permute-start | bytes 1327112 | tf_op jit(solution)/shard_map/ppermute | solution.py:51
  64.0 5.5 %copy-start.6 = (bf16[96,2304]{1,0:T(8,128)(2,1)}, bf16[96,2304]{1,0:T(8,128)(2,1)S(1)}, u32[]{:S(2)}) copy-start(bf16[96,2304]{1,0:T(8,128)(2,1)S(1)} %collective-permute-done.9.refs_6_) | copy-start | bytes 1327108
  64.0 3.1 %collective-permute-start.12 = (bf16[96,2304]{1,0:T(8,128)(2,1)}, bf16[96,2304]{1,0:T(8,128)(2,1)S(1)}, u32[]{:S(2)}, u32[]{:S(2)}) collective-permute-start(bf16[96,2304]{1,0:T(8,128)(2,1)} %collective-permute-done.11.refs_8_), channel_id=1, source_target_pairs={{0,8},{8,0},{16,24},{24,16},{1,9},{9,1},{17,25},{25,17},{2,10},{10... | collective-permute-start | bytes 1327112 | tf_op jit(solution)/shard_map/ppermute | solution.py:51
  65.3 4.2 %copy-start.7 = (bf16[96,2304]{1,0:T(8,128)(2,1)}, bf16[96,2304]{1,0:T(8,128)(2,1)S(1)}, u32[]{:S(2)}) copy-start(bf16[96,2304]{1,0:T(8,128)(2,1)S(1)} %collective-permute-done.7.refs_4_) | copy-start | bytes 1327108
  65.3 1.8 %collective-permute-start.10 = (bf16[96,2304]{1,0:T(8,128)(2,1)S(1)}, bf16[96,2304]{1,0:T(8,128)(2,1)S(1)}, u32[]{:S(2)}, u32[]{:S(2)}) collective-permute-start(bf16[96,2304]{1,0:T(8,128)(2,1)S(1)} %collective-permute-done.9.refs_6_), channel_id=1, source_target_pairs={{0,8},{8,0},{16,24},{24,16},{1,9},{9,1},{17,25},{25,17},{2,10},{10... | collective-permute-start | bytes 1327112 | tf_op jit(solution)/shard_map/ppermute | solution.py:51
  65.3 2.6 %collective-permute-start.8 = (bf16[96,2304]{1,0:T(8,128)(2,1)S(1)}, bf16[96,2304]{1,0:T(8,128)(2,1)S(1)}, u32[]{:S(2)}, u32[]{:S(2)}) collective-permute-start(bf16[96,2304]{1,0:T(8,128)(2,1)S(1)} %collective-permute-done.7.refs_4_), channel_id=1, source_target_pairs={{0,8},{8,0},{16,24},{24,16},{1,9},{9,1},{17,25},{25,17},{2,10},{10... | collective-permute-start | bytes 1327112 | tf_op jit(solution)/shard_map/ppermute | solution.py:51
  67.1 44.2 %collective-permute-start.18 = (bf16[192,1536]{1,0:T(8,128)(2,1)S(1)}, bf16[192,1536]{1,0:T(8,128)(2,1)S(1)}, u32[]{:S(2)}, u32[]{:S(2)}) collective-permute-start(bf16[192,1536]{1,0:T(8,128)(2,1)S(1)} %copy-done.3), channel_id=1, source_target_pairs={{0,8},{8,0},{16,24},{24,16},{1,9},{9,1},{17,25},{25,17},{2,10},{10... | collective-permute-start | bytes 1769480 | tf_op jit(solution)/shard_map/ppermute | solution.py:51
  67.1 16.5 %collective-permute-start.25 = (bf16[48,1536]{1,0:T(8,128)(2,1)}, bf16[48,1536]{1,0:T(8,128)(2,1)}, u32[]{:S(2)}, u32[]{:S(2)}) collective-permute-start(bf16[48,1536]{1,0:T(8,128)(2,1)} %get-tuple-element.7), channel_id=1, source_target_pairs={{0,16},{8,24},{16,0},{24,8},{1,17},{9,25},{17,1},{25,9},{2,18},{10... | collective-permute-start | bytes 442376 | tf_op jit(solution)/shard_map/ppermute | solution.py:51
  67.9 15.8 %collective-permute-start.21 = (bf16[48,1536]{1,0:T(8,128)(2,1)}, bf16[48,1536]{1,0:T(8,128)(2,1)}, u32[]{:S(2)}, u32[]{:S(2)}) collective-permute-start(bf16[48,1536]{1,0:T(8,128)(2,1)} %collective-permute-done.19.refs_2_), channel_id=1, source_target_pairs={{0,1},{1,0},{2,3},{3,2},{4,5},{5,4},{6,7},{7,6},{8,9},{9,8},{10,11... | collective-permute-start | bytes 442376 | tf_op jit(solution)/shard_map/ppermute | solution.py:51
  68.7 15.5 %collective-permute-start.23 = (bf16[48,1536]{1,0:T(8,128)(2,1)}, bf16[48,1536]{1,0:T(8,128)(2,1)}, u32[]{:S(2)}, u32[]{:S(2)}) collective-permute-start(bf16[48,1536]{1,0:T(8,128)(2,1)} %collective-permute-done.19.refs_2_), channel_id=1, source_target_pairs={{0,2},{1,3},{2,0},{3,1},{4,6},{5,7},{6,4},{7,5},{8,10},{9,11},{10,... | collective-permute-start | bytes 442376 | tf_op jit(solution)/shard_map/ppermute | solution.py:51
  83.7 15.5 %collective-permute-start.20 = (bf16[48,1536]{1,0:T(8,128)(2,1)}, bf16[48,1536]{1,0:T(8,128)(2,1)}, u32[]{:S(2)}, u32[]{:S(2)}) collective-permute-start(bf16[48,1536]{1,0:T(8,128)(2,1)} %collective-permute-done.19.refs_2_), channel_id=1, source_target_pairs={{0,8},{8,0},{16,24},{24,16},{1,9},{9,1},{17,25},{25,17},{2,10},{10... | collective-permute-start | bytes 442376 | tf_op jit(solution)/shard_map/ppermute | solution.py:51
  83.7 27.6 %collective-permute-start.26 = (bf16[48,1536]{1,0:T(8,128)(2,1)}, bf16[48,1536]{1,0:T(8,128)(2,1)}, u32[]{:S(2)}, u32[]{:S(2)}) collective-permute-start(bf16[48,1536]{1,0:T(8,128)(2,1)} %collective-permute-done.25.refs_8_), channel_id=1, source_target_pairs={{0,8},{8,0},{16,24},{24,16},{1,9},{9,1},{17,25},{25,17},{2,10},{10... | collective-permute-start | bytes 442376 | tf_op jit(solution)/shard_map/ppermute | solution.py:51
  84.2 27.1 %collective-permute-start.22 = (bf16[48,1536]{1,0:T(8,128)(2,1)}, bf16[48,1536]{1,0:T(8,128)(2,1)}, u32[]{:S(2)}, u32[]{:S(2)}) collective-permute-start(bf16[48,1536]{1,0:T(8,128)(2,1)} %collective-permute-done.21.refs_4_), channel_id=1, source_target_pairs={{0,8},{8,0},{16,24},{24,16},{1,9},{9,1},{17,25},{25,17},{2,10},{10... | collective-permute-start | bytes 442376 | tf_op jit(solution)/shard_map/ppermute | solution.py:51
  84.3 27.0 %collective-permute-start.24 = (bf16[48,1536]{1,0:T(8,128)(2,1)}, bf16[48,1536]{1,0:T(8,128)(2,1)}, u32[]{:S(2)}, u32[]{:S(2)}) collective-permute-start(bf16[48,1536]{1,0:T(8,128)(2,1)} %collective-permute-done.23.refs_6_), channel_id=1, source_target_pairs={{0,8},{8,0},{16,24},{24,16},{1,9},{9,1},{17,25},{25,17},{2,10},{10... | collective-permute-start | bytes 442376 | tf_op jit(solution)/shard_map/ppermute | solution.py:51
  99.1 12.2 %collective-permute-start.17 = (bf16[128,768]{1,0:T(8,128)(2,1)}, bf16[128,768]{1,0:T(8,128)(2,1)S(1)}, u32[]{:S(2)}, u32[]{:S(2)}) collective-permute-start(bf16[128,768]{1,0:T(8,128)(2,1)} %attend_tail.1), channel_id=1, source_target_pairs={{0,1},{1,2},{2,3},{3,4},{4,5},{5,6},{6,7},{8,9},{9,10},{10,11},{11... | collective-permute-start | bytes 589832 | tf_op jit(solution)/shard_map/ppermute | solution.py:57
  (9 other events, 20.6 us)

commit v2 on v0

v2 whole, which is shorter than its diff:
```python
import functools
import math

import jax
import jax.numpy as jnp
from jax import lax
from jax.experimental import pallas as pl
from jax.experimental.pallas import tpu as pltpu
from jax.sharding import PartitionSpec as P

HEADS = 12
HS = 64
SEAM = 128
BLK = 128
TSTEPS = 1000
STRIDE = 200
LANES = 128

epsilon = 1e-06
MASKED = -1e30
MICROSECOND = 10**9
VMEM_LIMIT = 18 * 1024 * 1024

BF16 = jnp.bfloat16
F32 = jnp.float32


def plan(moment):
    return jnp.cos((moment / TSTEPS + 0.008) / 1.008 * (math.pi / 2.0)) ** 2


def coefficients(timestep):
    current = timestep[0].astype(jnp.float32)
    abar_now = plan(current)
    abar_prev = plan(current - STRIDE)
    spread = jnp.sqrt((1.0 - abar_prev) / (1.0 - abar_now) * (1.0 - abar_now / abar_prev))
    carried = jnp.sqrt((1.0 - abar_prev) * (abar_now / abar_prev - abar_now) / (1.0 - abar_now))
    coef_pred = carried - jnp.sqrt(abar_prev) * jnp.sqrt(1.0 - abar_now) / jnp.sqrt(abar_now)
    coef_latent = jnp.sqrt(abar_prev / abar_now)
    return (current, coef_latent, coef_pred, spread)


def time_embedding(current, model_width):
    half_width = model_width // 2
    frequency = jnp.exp(-math.log(10000.0) * jnp.arange(half_width, dtype=jnp.float32) / half_width)
    angles = current * frequency
    return jnp.concatenate([jnp.cos(angles), jnp.sin(angles)])


def swapped(block, axis, bit):
    route = [(i, i ^ bit) for i in range(lax.axis_size(axis))]
    return lax.ppermute(block, axis, route)


def shifted(block, axis, distance):
    devices = range(lax.axis_size(axis))
    route = [(i - distance, i) for i in devices if i - distance in devices]
    return lax.ppermute(block, axis, route)


def vmem():
    return pl.BlockSpec(memory_space=pltpu.VMEM)


def smem():
    return pl.BlockSpec(memory_space=pltpu.SMEM)


def params():
    return pltpu.CompilerParams(vmem_limit_bytes=VMEM_LIMIT)


def anywhere():
    return pl.BlockSpec(memory_space=pl.ANY)


def hbm():
    return pl.BlockSpec(memory_space=pltpu.HBM)


def in_hbm(value):
    return pltpu.with_memory_space_constraint(value, pltpu.HBM)


def cost(flops):
    return pl.CostEstimate(flops=flops, bytes_accessed=1, transcendentals=0)


def everyones(row):
    var_count, tm_count = lax.axis_size("var"), lax.axis_size("tm")
    sent = jnp.broadcast_to(row, (var_count * tm_count, row.shape[1]))
    arrived = lax.all_to_all(sent, ("var", "tm"), 0, 0, tiled=True)
    return arrived.reshape(var_count, tm_count * row.shape[1])


def first_kernel(places_ref, ids_ref, table_ref, query_ref, keyval_ref, latent_ref, *refs):
    pooled_ref, halo_ref, *cut_refs, columns, sems = refs
    head_width = query_ref.shape[1]
    copies = [
        pltpu.make_async_copy(table_ref, columns, sems.at[0]),
        pltpu.make_async_copy(latent_ref.at[: halo_ref.shape[0], :], halo_ref, sems.at[1]),
    ]
    for k, target in enumerate(cut_refs):
        rows = target.shape[0]
        at = pl.ds(aligned(places_ref[k] * rows, 16), rows)
        copies += [
            pltpu.make_async_copy(
                query_ref.at[at, :], target.at[:, :head_width], sems.at[2 + 2 * k]
            ),
            pltpu.make_async_copy(
                keyval_ref.at[at, :], target.at[:, head_width:], sems.at[3 + 2 * k]
            ),
        ]
    for copy in copies:
        copy.start()
    lane = lax.broadcasted_iota(jnp.int32, (1, LANES), 1)
    copies[0].wait()

    def body(j, total):
        token = ids_ref[0, j]
        start = pl.multiple_of((token >> 7) * LANES, LANES)
        block = columns[:, pl.ds(start, LANES)].astype(F32)
        return total + jnp.where(lane == (token & (LANES - 1)), block, 0.0)

    count = ids_ref.shape[1]
    total = lax.fori_loop(0, count, body, jnp.zeros((columns.shape[0], LANES), F32), unroll=8)
    ones = jnp.full((8, LANES), 1.0 / count, F32)
    pooled_ref[...] = lax.dot_general(
        ones,
        total,
        (((1,), (1,)), ((), ())),
        precision=lax.Precision.HIGHEST,
        preferred_element_type=F32,
    )
    for copy in copies[1:]:
        copy.wait()


def first_rows(places, prompt_ids, prompt_table, w_query, w_keyval, latent):
    table_columns = prompt_table.T
    quarter = w_query.shape[0] // 4
    columns = w_query.shape[1] + w_keyval.shape[1]
    return pl.pallas_call(
        first_kernel,
        out_shape=[
            jax.ShapeDtypeStruct((8, table_columns.shape[0]), F32),
            jax.ShapeDtypeStruct((SEAM, latent.shape[1]), BF16),
        ]
        + [jax.ShapeDtypeStruct((quarter, columns), BF16)] * len(places),
        in_specs=[smem(), smem()] + [hbm()] * 4,
        out_specs=[vmem()] * (2 + len(places)),
        scratch_shapes=[
            pltpu.VMEM(table_columns.shape, BF16),
            pltpu.SemaphoreType.DMA((2 + 2 * len(places),)),
        ],
        compiler_params=params(),
        cost_estimate=cost(4 * MICROSECOND),
        name="pool_and_first_rows",
    )(
        numbers(*(places or (0,))),
        prompt_ids,
        *[in_hbm(value) for value in (table_columns, w_query, w_keyval, latent)],
    )


def joined(parts):
    return parts[0] if len(parts) == 1 else jnp.concatenate(parts, axis=1)


def can_route(rows):
    return lax.axis_size("var") == 4 and lax.axis_size("tm") % 4 == 0 and rows % 128 == 0


def cut(weights, which, count):
    rows = weights[0].shape[0] // count
    return joined([lax.dynamic_slice_in_dim(w, which * rows, rows, 0) for w in weights])


def gate_kernel(*refs):
    del refs


def together(*values):
    return pl.pallas_call(
        gate_kernel,
        out_shape=[jax.ShapeDtypeStruct(v.shape, v.dtype) for v in values],
        in_specs=[anywhere()] * len(values),
        out_specs=[anywhere()] * len(values),
        input_output_aliases={k: k for k in range(len(values))},
        compiler_params=params(),
        cost_estimate=cost(1),
        name="gate",
    )(*values)


def numbers(*values):
    return jnp.stack([jnp.asarray(value, jnp.int32) for value in values])


def aligned(value, multiple):
    return pl.multiple_of(value, multiple)


def normalize(target, begin, ref, scale, width):
    for row in range(0, ref.shape[0], 32):
        values = ref[row : row + 32, :].astype(F32)
        inv_norm = lax.rsqrt(jnp.sum(values * values, axis=-1, keepdims=True) / width + epsilon)
        target[begin + row : begin + row + 32, :] = (values * inv_norm * scale).astype(BF16)


def attend_rows(query, keyval_ref, bias, own_block, pair):
    head_width = keyval_ref.shape[1] // 2
    key_rows = keyval_ref.shape[0]
    blocks = len(bias)
    at = pl.ds(pair * LANES, LANES)
    value_at = pl.ds(head_width + pair * LANES, LANES)
    left = lax.broadcasted_iota(jnp.int32, (1, LANES), 1) < HS
    zero = jnp.zeros((), BF16)
    query = query * BF16(1.0 / math.sqrt(HS))
    both = jnp.concatenate([jnp.where(left, query, zero), jnp.where(left, zero, query)], axis=0)
    scores = lax.dot_general(
        both, keyval_ref[:, at], (((1,), (1,)), ((), ())), preferred_element_type=F32
    )
    cut_block = lambda j: scores[:, j * BLK : (j + 1) * BLK]
    peak = None
    for j in range(blocks):
        top = jnp.maximum(cut_block(j), cut_block(blocks + j))
        if j not in (0, own_block):
            top = top + bias[j]
        peak = top if peak is None else jnp.maximum(peak, top)
    peak = jnp.max(peak, axis=-1, keepdims=True)
    offsets = [peak if j in (0, own_block) else peak - bias[j] for j in range(blocks)]
    weights = jnp.concatenate(
        [jnp.exp(cut_block(j) - offsets[j % blocks]).astype(BF16) for j in range(2 * blocks)],
        axis=1,
    )
    ones = jnp.ones((key_rows, LANES), BF16)
    values = jnp.concatenate([keyval_ref[:, value_at], ones], axis=1)
    total = jnp.dot(weights, values, preferred_element_type=F32)
    mixed = total[:, :LANES] / total[:, LANES:]
    return jnp.where(left, mixed[:BLK], mixed[BLK:])


def own_kernel(n_wide, n_pairs, places_ref, latent_ref, halo_ref, scale_ref, *refs):
    wide_pieces = refs[:n_wide]
    query_pieces = refs[n_wide : n_wide + n_pairs]
    keyval_pieces = refs[n_wide + n_pairs : n_wide + 2 * n_pairs]
    query_ref, keyval_ref, weights_ref, normed, query_weights, sems = refs[n_wide + 2 * n_pairs :]
    head_width = query_weights.shape[1]
    copies = []

    def copy(source, target):
        copies.append(pltpu.make_async_copy(source, target, sems.at[len(copies)]))

    for k in range(n_pairs):
        at = pl.ds(aligned(places_ref[n_wide + k], 16), query_pieces[k].shape[0])
        copy(query_pieces[k], query_weights.at[at, :])
        copy(keyval_pieces[k], weights_ref.at[at, :])
    for k, piece in enumerate(wide_pieces):
        at = pl.ds(aligned(places_ref[k], 16), piece.shape[0])
        copy(piece.at[:, :head_width], query_weights.at[at, :])
        copy(piece.at[:, head_width:], weights_ref.at[at, :])
    for c in copies:
        c.start()
    scale = 1.0 + scale_ref[...]
    normalize(normed, 0, latent_ref, scale, latent_ref.shape[1])
    normalize(normed, latent_ref.shape[0], halo_ref, scale, latent_ref.shape[1])
    for c in copies:
        c.wait()
    step = 256
    for target, weights in ((query_ref, query_weights), (keyval_ref, weights_ref)):
        for begin in range(0, target.shape[1], step):
            at = pl.ds(begin, step)
            target[:, at] = jnp.dot(
                normed[...], weights[:, at], preferred_element_type=F32
            ).astype(BF16)


def project_own(latent, halo, condition, wide, wide_places, queries, keyvals, pair_places):
    window_rows = latent.shape[0] + halo.shape[0]
    width = latent.shape[1]
    keyval_width = keyvals[0].shape[1]
    head_width = keyval_width // 2
    n_copies = 2 * (len(wide) + len(queries))
    return pl.pallas_call(
        functools.partial(own_kernel, len(wide), len(queries)),
        out_shape=[
            jax.ShapeDtypeStruct((window_rows, head_width), BF16),
            jax.ShapeDtypeStruct((window_rows, keyval_width), BF16),
            jax.ShapeDtypeStruct((width, keyval_width), BF16),
        ],
        in_specs=[smem()] + [vmem()] * 3 + [hbm()] * n_copies_refs(wide, queries),
        out_specs=[vmem()] * 3,
        scratch_shapes=[
            pltpu.VMEM((window_rows, width), BF16),
            pltpu.VMEM((width, head_width), BF16),
            pltpu.SemaphoreType.DMA((n_copies,)),
        ],
        compiler_params=params(),
        cost_estimate=cost(6 * MICROSECOND),
        name="project_own",
    )(
        numbers(*wide_places, *pair_places),
        latent,
        halo,
        condition,
        *[in_hbm(piece) for piece in (*wide, *queries, *keyvals)],
    )


def n_copies_refs(wide, queries):
    return len(wide) + 2 * len(queries)


def source_kernel(
    n_sources, places_ref, bias_ref, query_ref, own_ref, weights_ref, scale_ref, *refs
):
    sources = refs[:n_sources]
    keyval_ref, tail_ref, normed = refs[n_sources:]
    window_rows, width = normed.shape
    main_rows = window_rows - SEAM
    scale = 1.0 + scale_ref[...]
    mine = jnp.where(places_ref[0] == 0, 1.0, 0.0)
    for row in range(0, window_rows, 32):
        at = pl.ds(row, 32)
        values = sources[0][at, :].astype(F32) * mine
        for ref in sources[1:]:
            values += ref[at, :].astype(F32)
        square = jnp.sum(values * values, axis=-1, keepdims=True)
        inv_norm = lax.rsqrt(square / width + epsilon)
        normed[at, :] = (values * inv_norm * scale).astype(BF16)
    keyval_ref[:window_rows, :] = own_ref[...]
    step = 256
    for begin in range(0, keyval_ref.shape[1], step):
        at = pl.ds(begin, step)
        keyval_ref[window_rows:, at] = jnp.dot(
            normed[...], weights_ref[:, at], preferred_element_type=F32
        ).astype(BF16)
    blocks = window_rows // BLK
    row = lax.broadcasted_iota(jnp.int32, (BLK, 1), 0).astype(F32)
    fade = 1.0 - (row + 0.5) / SEAM
    bias = [bias_ref[blocks - 1, j] for j in range(blocks)]
    for pair in range(HEADS // 2):
        at = pl.ds(pair * LANES, LANES)
        mixed = attend_rows(query_ref[main_rows:, at], keyval_ref, bias, blocks - 1, pair)
        tail_ref[:, at] = (mixed * fade).astype(BF16)


def project_source(place, bias, query, own, weights, scale, sources):
    window_rows, head_width = query.shape
    return pl.pallas_call(
        functools.partial(source_kernel, len(sources)),
        out_shape=[
            jax.ShapeDtypeStruct((2 * window_rows, 2 * head_width), BF16),
            jax.ShapeDtypeStruct((SEAM, head_width), BF16),
        ],
        in_specs=[smem(), smem()] + [vmem()] * (4 + len(sources)),
        out_specs=[vmem()] * 2,
        scratch_shapes=[pltpu.VMEM(sources[0].shape, BF16)],
        compiler_params=params(),
        cost_estimate=cost(5 * MICROSECOND),
        name="project_source_attend_tail",
    )(numbers(place), bias, query, own, weights, scale, *sources)


def main_kernel(bias_ref, query_ref, keyval_ref, out_ref):
    blocks = keyval_ref.shape[0] // (2 * BLK)
    for i in range(blocks - 1):
        bias = [bias_ref[i, j] for j in range(blocks)]
        rows = pl.ds(i * BLK, BLK)
        for pair in range(HEADS // 2):
            at = pl.ds(pair * LANES, LANES)
            out_ref[rows, at] = attend_rows(query_ref[rows, at], keyval_ref, bias, i, pair)


def attend_main(bias, query, keyval):
    rows, width = query.shape[0] - SEAM, query.shape[1]
    return pl.pallas_call(
        main_kernel,
        out_shape=jax.ShapeDtypeStruct((rows, width), F32),
        in_specs=[smem(), vmem(), vmem()],
        out_specs=vmem(),
        compiler_params=params(),
        cost_estimate=cost(4 * MICROSECOND),
        name="attend_main",
    )(bias, query, keyval)


def finish_kernel(
    n_pieces, places_ref, coef_ref, attended_ref, received_ref, latent_ref, noise_ref, *refs
):
    pieces, (out_ref, weights) = refs[:n_pieces], refs[n_pieces:]
    for k, piece in enumerate(pieces):
        weights[pl.ds(aligned(places_ref[k], 16), piece.shape[0]), :] = piece[...]
    row = lax.broadcasted_iota(jnp.int32, (SEAM, 1), 0).astype(F32)
    ramp_up = jnp.where(coef_ref[3] > 0.5, 1.0, (row + 0.5) / SEAM)
    lead = attended_ref[:SEAM, :] * ramp_up + received_ref[...].astype(F32)
    blended = jnp.concatenate([lead, attended_ref[SEAM:, :]], axis=0).astype(BF16)
    step = 256
    for begin in range(0, out_ref.shape[1], step):
        at = pl.ds(begin, step)
        prediction = jnp.dot(blended, weights[:, at], preferred_element_type=F32)
        result = (
            coef_ref[0] * latent_ref[:, at].astype(F32)
            + coef_ref[1] * prediction
            + coef_ref[2] * noise_ref[:, at].astype(F32)
        )
        out_ref[:, at] = result.astype(BF16)


def finish(coefs, attended, received, latent, noise, pieces, places):
    return pl.pallas_call(
        functools.partial(finish_kernel, len(pieces)),
        out_shape=jax.ShapeDtypeStruct(latent.shape, BF16),
        in_specs=[smem(), smem()] + [vmem()] * (4 + len(pieces)),
        out_specs=vmem(),
        scratch_shapes=[pltpu.VMEM((attended.shape[1], latent.shape[1]), BF16)],
        compiler_params=params(),
        cost_estimate=cost(3 * MICROSECOND),
        name="blend_and_step",
    )(
        numbers(*places),
        coefs,
        attended,
        received,
        latent,
        noise,
        *pieces,
    )


def from_source(value):
    bits = []
    bit = lax.axis_size("var") // 2
    while bit:
        bits.append(bit)
        bit //= 2
    return [(lax.ppermute(value, "var", [(0, bit)]), bit) for bit in bits]


def passed_on(arrivals):
    count = lax.axis_size("var")
    arrays = [arrivals[0][0]]
    for array, bit in arrivals[1:]:
        route = [(i, i + bit) for i in range(2 * bit, count, 2 * bit)]
        payload = functools.reduce(jnp.add, arrays)
        arrays += [array, lax.ppermute(payload, "var", route)]
    return arrays


def local(
    latent, fresh_noise, timestep, prompt_ids, block_table, prompt_table, w_query, w_keyval, w_out
):
    latent = latent[0]
    own_rows, model_width = latent.shape
    tm_count = lax.axis_size("tm")
    tm_place = lax.axis_index("tm")
    var_place = lax.axis_index("var")
    rows = w_query.shape[0]
    routed = can_route(rows)
    corner = tm_place & 3

    pooled, halo_rows, *cuts = first_rows(
        (corner, corner ^ 3) if routed else (),
        prompt_ids,
        prompt_table,
        w_query,
        w_keyval,
        latent,
    )
    if routed:
        quarter = rows // 4
        first = swapped(cuts[0], "var", 2)
        fourth = swapped(cuts[1], "var", 2)
        partner_query = swapped(w_query, "var", 1)
        partner_keyval = swapped(w_keyval, "var", 1)
    halo = shifted(halo_rows, "tm", -1)
    pooled = everyones(pooled[:1])
    if routed:
        halo, first = together(halo, first)
        second = swapped(first, "tm", 1)
        third = swapped(first, "tm", 2)
        first_over = swapped(first, "var", 1)
        fourth_over = swapped(fourth, "var", 1)
    window = jnp.concatenate([latent, halo], axis=0)
    sources = from_source(window)
    source_pooled = pooled[:1]
    pooled = lax.dynamic_slice_in_dim(pooled, var_place, 1, 0)
    current, coef_latent, coef_pred, spread = coefficients(timestep)
    embedded = time_embedding(current, model_width)[None, :]

    if routed:
        second, third = together(second, third)
        wide = [first, second, third, fourth]
        wide += [first_over, swapped(second, "var", 1), swapped(third, "var", 1), fourth_over]
        offsets = [(corner ^ k) * quarter for k in range(4)]
        wide_places = [(var_place ^ 2) * rows + offset for offset in offsets]
        wide_places += [(var_place ^ 3) * rows + offset for offset in offsets]
        queries, keyvals = [w_query, partner_query], [w_keyval, partner_keyval]
        pair_places = [var_place * rows, (var_place ^ 1) * rows]
        out_far = swapped(w_out, "var", 2)
    else:
        wide, wide_places, pair_places = [], [], [0]
        queries = [lax.all_gather(w_query, "var", axis=0, tiled=True)]
        keyvals = [lax.all_gather(w_keyval, "var", axis=0, tiled=True)]
    query, own, weights = project_own(
        latent, halo, embedded + pooled, wide, wide_places, queries, keyvals, pair_places
    )

    sources = [window] + passed_on(sources)
    blocks = block_table.shape[0]
    present = (jnp.arange(blocks) < own_rows // BLK) | (tm_place != tm_count - 1)
    bias = jnp.where((block_table > 0) & present[None, :], 0.0, MASKED).astype(F32)
    keyval, tail = project_source(
        var_place, bias, query, own, weights, embedded + source_pooled, sources
    )
    if routed:
        tail, out_far = together(tail, out_far)
        out_rows = w_out.shape[0]
        out_pieces = [w_out, swapped(w_out, "var", 1), out_far, swapped(out_far, "var", 1)]
        out_places = [(var_place ^ k) * out_rows for k in range(4)]
    else:
        out_pieces, out_places = [lax.all_gather(w_out, "var", axis=0, tiled=True)], [0]
    received = shifted(tail, "tm", 1)
    attended = attend_main(bias, query, keyval)
    coefs = jnp.stack([coef_latent, coef_pred, spread, (tm_place == 0).astype(F32)])
    return finish(coefs, attended, received, latent, fresh_noise[0], out_pieces, out_places)[None]


def solution(mesh):
    placed = (
        P("var", "tm", None),
        P("var", "tm", None),
        P(),
        P("var", None),
        P(),
        P(None, "tm"),
        P("var", None),
        P("var", None),
        P("var", None),
    )
    return jax.shard_map(
        local, mesh=mesh, in_specs=placed, out_specs=P("var", "tm", None), check_vma=False
    )
```

time: 183 us -> 88.4 us (0.48)
  matrix products: 51.4 us -> 0 us
  waiting for transfers between devices: 59.1 us -> 29.9 us
  Pallas kernels: 0 us -> 25.2 us
  local copies, waits for them, and re-layouts: 24.6 us -> 2.53 us
  starting transfers between devices: 6.05 us -> 27.8 us
  blocking collectives: 19.1 us -> 0 us
  between operations: 15.3 us -> 1.57 us
  other arithmetic: 5.4 us -> 0.47 us
    dot_general x27 -> x0, matrix products: 51.4 us -> none  [the longest x12 24.1 us: one_head(): return jnp.dot(probs, head_value, preferred_element_type=jnp.float32)]
    psum x1 -> x0, waiting for transfers between devices: 35.5 us -> none  [broadcast(): return lax.psum(kept, axis)]
    pallas_call x0 -> x8, Pallas kernels: none -> 25.2 us  [the longest x1 6.89 us: project_own(): pl.pallas_call(functools.partial(own_kernel, len(wide), len(queries)), ou...]
    ppermute x0 -> x16, waiting for transfers between devices: none -> 19.3 us  [the longest x13 19.3 us: swapped(): return lax.ppermute(block, axis, route)]
    unnamed x1 -> x0, blocking collectives: 19.1 us -> none
    ppermute x0 -> x16, starting transfers between devices: none -> 14.3 us  [the longest x13 8.98 us: swapped(): return lax.ppermute(block, axis, route)]
    all_gather x3 -> x0, waiting for transfers between devices: 9.87 us -> none  [the longest x1 9.85 us: local(): lax.all_gather(w_query, 'var', axis=0, tiled=True)]
    unnamed x19 -> x18, local copies, waits for them, and re-layouts: 11.3 us -> 1.61 us
  transfers between devices with their start and end apart: 6 -> 19, of which waited for: 4 -> 6; matrix products, arithmetic and copies ran while one was open for 43% -> 1% of each run, Pallas kernels for 0% -> 20%
where the time goes in v2:
time: 88.4 us; the launch traced here: 87.5 us
  waiting for transfers between devices  29.9 us (34%)
  starting transfers between devices  27.8 us (31%)
  Pallas kernels  25.2 us (29%)
  local copies, waits for them, and re-layouts  2.53 us (3%)
  between operations  1.57 us (2%)
    ppermute x13, waiting for transfers between devices, swapped(): return lax.ppermute(block, axis, route)  19.3 us
    ppermute x2, waiting for transfers between devices, shifted(): return lax.ppermute(block, axis, route)  10.5 us
    ppermute x13, starting transfers between devices, swapped(): return lax.ppermute(block, axis, route)  8.98 us
    ppermute x2, starting transfers between devices, shifted(): return lax.ppermute(block, axis, route)  7.69 us
    pallas_call x1, Pallas kernels, project_own(): pl.pallas_call(functools.partial(own_kernel, len(wide), len(queries)), ou...  6.89 us
    pallas_call x1, Pallas kernels, project_source(): pl.pallas_call(functools.partial(source_kernel, len(sources)), out_shape=...  6.65 us
    all_to_all x1, starting transfers between devices, everyones(): arrived = lax.all_to_all(sent, ('var', 'tm'), 0, 0, tiled=True)  5.9 us
    pallas_call x1, Pallas kernels, first_rows(): pl.pallas_call(first_kernel, out_shape=[jax.ShapeDtypeStruct((8, table_co...  5.34 us
  transfers between devices with their start and end apart: 19, of which 6 were waited for; matrix products, arithmetic and copies ran while one was open for 1% of the time, Pallas kernels for 20%

profile of v2, /device:TPU:10, one launch (start us, length us, event | category | flops | bytes accessed | tf_op | source)
XLA Modules:
  0.0 87.5 jit_solution(14208855458151511555)
XLA Ops:
  0.1 0.7 copy-done.5
  0.7 5.3 %pool_and_first_rows.1 = (f32[8,192]{1,0:T(8,128)S(1)}, bf16[128,1536]{1,0:T(8,128)(2,1)S(1)}, bf16[96,2304]{1,0:T(8,128)(2,1)S(1)}, bf16[96,2304]{1,0:T(8,128)(2,1)}) custom-call(s32[2]{0:T(128)S(1)} %pad_add_fusion.1.places_ref, s32[1,64]{1,0:T(1,128)S(1)} %copy-done.5, bf16[192,16384]{1,0:T(8,128)(2,1)} %bitcast.33, bf16[384,768]{1,0:T(8,128)(2,1)} %refs_8_.1, ...), custom_call_target="tpu_custom_call" | custom-call | flops 4000000000 | bytes 1 | tf_op jit(solution)/shard_map/pool_and_first_rows/pallas_call | solution.py:143
  6.1 0.6 collective-permute-start.1
  6.7 3.3 %collective-permute-start = (bf16[128,1536]{1,0:T(8,128)(2,1)S(1)}, bf16[128,1536]{1,0:T(8,128)(2,1)S(1)}, u32[]{:S(2)}, u32[]{:S(2)}) collective-permute-start(bf16[128,1536]{1,0:T(8,128)(2,1)S(1)} %get-tuple-element.20), channel_id=1, source_target_pairs={{1,0},{2,1},{3,2},{4,3},{5,4},{6,5},{7,6},{9,8},{10,9},{11,10},{12... | collective-permute-start | bytes 1179656 | tf_op jit(solution)/shard_map/ppermute | solution.py:58
  10.0 9.1 %collective-permute-done.refs_0_ = bf16[128,1536]{1,0:T(8,128)(2,1)S(1)} collective-permute-done((bf16[128,1536]{1,0:T(8,128)(2,1)S(1)}, bf16[128,1536]{1,0:T(8,128)(2,1)S(1)}, u32[]{:S(2)}, u32[]{:S(2)}) %collective-permute-start) | collective-permute-done | bytes 393248 | tf_op jit(solution)/shard_map/ppermute | solution.py:58
  19.2 1.3 %collective-permute-start.11 = (bf16[384,1536]{1,0:T(8,128)(2,1)S(1)}, bf16[384,1536]{1,0:T(8,128)(2,1)}, u32[]{:S(2)}, u32[]{:S(2)}) collective-permute-start(bf16[384,1536]{1,0:T(8,128)(2,1)S(1)} %pad_maximum_fusion.refs_0_), channel_id=1, source_target_pairs={{0,16},{1,17},{2,18},{3,19},{4,20},{5,21},{6,22},{7,23}} | collective-permute-start | bytes 3538952 | tf_op jit(solution)/shard_map/ppermute | solution.py:438
  20.5 3.7 %collective-permute-start.4 = (bf16[96,2304]{1,0:T(8,128)(2,1)}, bf16[96,2304]{1,0:T(8,128)(2,1)}, u32[]{:S(2)}, u32[]{:S(2)}) collective-permute-start(bf16[96,2304]{1,0:T(8,128)(2,1)} %get-tuple-element.27), channel_id=1, source_target_pairs={{0,16},{8,24},{16,0},{24,8},{1,17},{9,25},{17,1},{25,9},{2,18},{10... | collective-permute-start | bytes 1327112 | tf_op jit(solution)/shard_map/ppermute | solution.py:52
  24.2 0.5 collective-permute-start.10
  24.7 0.6 broadcast_in_dim.23
  25.3 5.9 %all-to-all-start = ((f32[32,1,192]{2,1,0:T(1,128)}), f32[32,1,192]{2,1,0:T(1,128)S(1)}, u32[]{:S(2)}, u32[]{:S(2)}) async-start(f32[32,1,192]{2,1,0:T(1,128)} %broadcast_in_dim.23), calls=%async_computation | async-start | bytes 65536 | tf_op jit(solution)/shard_map/all_to_all | solution.py:92
  31.9 1.5 %collective-permute-start.2 = (bf16[96,2304]{1,0:T(8,128)(2,1)}, bf16[96,2304]{1,0:T(8,128)(2,1)S(1)}, u32[]{:S(2)}, u32[]{:S(2)}) collective-permute-start(bf16[96,2304]{1,0:T(8,128)(2,1)} %get-tuple-element.24.refs_0_), channel_id=1, source_target_pairs={{0,1},{1,0},{2,3},{3,2},{4,5},{5,4},{6,7},{7,6},{8,9},{9,8},{10,11... | collective-permute-start | bytes 1327112 | tf_op jit(solution)/shard_map/ppermute | solution.py:52
  33.5 11.5 %collective-permute-done.4.refs_3_ = bf16[96,2304]{1,0:T(8,128)(2,1)} collective-permute-done((bf16[96,2304]{1,0:T(8,128)(2,1)}, bf16[96,2304]{1,0:T(8,128)(2,1)}, u32[]{:S(2)}, u32[]{:S(2)}) %collective-permute-start.4) | collective-permute-done | bytes 442400 | tf_op jit(solution)/shard_map/ppermute | solution.py:52
  45.0 0.7 collective-permute-start.3
  45.8 0.5 collective-permute-start.8
  47.0 0.1 stack.99.places_ref
  47.2 0.1 reshape.51
  47.3 6.3 %collective-permute-done.3.refs_1_ = bf16[96,2304]{1,0:T(8,128)(2,1)S(1)} collective-permute-done((bf16[96,2304]{1,0:T(8,128)(2,1)}, bf16[96,2304]{1,0:T(8,128)(2,1)S(1)}, u32[]{:S(2)}, u32[]{:S(2)}) %collective-permute-start.3) | collective-permute-done | bytes 442400 | tf_op jit(solution)/shard_map/ppermute | solution.py:52
  53.5 1.7 %collective-permute-start.12 = (bf16[384,1536]{1,0:T(8,128)(2,1)S(1)}, bf16[384,1536]{1,0:T(8,128)(2,1)}, u32[]{:S(2)}, u32[]{:S(2)}) collective-permute-start(bf16[384,1536]{1,0:T(8,128)(2,1)S(1)} %pad_maximum_fusion.refs_0_), channel_id=1, source_target_pairs={{0,8},{1,9},{2,10},{3,11},{4,12},{5,13},{6,14},{7,15}} | collective-permute-start | bytes 3538952 | tf_op jit(solution)/shard_map/ppermute | solution.py:438
  55.2 2.3 %collective-permute-start.13 = (bf16[384,1536]{1,0:T(8,128)(2,1)}, bf16[384,1536]{1,0:T(8,128)(2,1)}, u32[]{:S(2)}, u32[]{:S(2)}) collective-permute-start(bf16[384,1536]{1,0:T(8,128)(2,1)} %collective-permute-done.11.refs_1_), channel_id=1, source_target_pairs={{16,24},{17,25},{18,26},{19,27},{20,28},{21,29},{22,30},{23,31}} | collective-permute-start | bytes 3538952 | tf_op jit(solution)/shard_map/ppermute | solution.py:447
  57.8 0.5 collective-permute-start.7
  58.3 1.2 %collective-permute-done.6.refs_5_ = bf16[96,2304]{1,0:T(8,128)(2,1)S(1)} collective-permute-done((bf16[96,2304]{1,0:T(8,128)(2,1)S(1)}, bf16[96,2304]{1,0:T(8,128)(2,1)S(1)}, u32[]{:S(2)}, u32[]{:S(2)}) %collective-permute-start.6) | collective-permute-done | bytes 442400 | tf_op jit(solution)/shard_map/ppermute | solution.py:52
  59.6 0.4 collective-permute-start.16
  60.0 0.3 collective-permute-done.7.refs_6_
  60.2 0.1 copy-done.7
  60.3 0.8 copy-done.8
  61.1 6.9 %project_own.1 = (bf16[384,768]{1,0:T(8,128)(2,1)S(1)}, bf16[384,1536]{1,0:T(8,128)(2,1)S(1)}, bf16[1536,1536]{1,0:T(8,128)(2,1)S(1)}) custom-call(s32[10]{0:T(128)S(1)} %stack.99.places_ref, bf16[256,1536]{1,0:T(8,128)(2,1)S(1)} %bitcast.29, bf16[128,1536]{1,0:T(8,128)(2,1)S(1)} %get-tuple-element.22.halo_ref, ...), custom_call_target="tpu_custom_call" | custom-call | flops 6000000000 | bytes 1 | tf_op jit(solution)/shard_map/project_own/pallas_call | solution.py:285
  68.1 6.7 %project_source_attend_tail.1 = (bf16[768,1536]{1,0:T(8,128)(2,1)S(1)}, bf16[128,768]{1,0:T(8,128)(2,1)S(1)}) custom-call(s32[1]{0:T(128)} %bitcast.24.places_ref, f32[3,3]{1,0:T(4,128)S(1)} %and_select_fusion.bias_ref, bf16[384,768]{1,0:T(8,128)(2,1)S(1)} %get-tuple-element.28.query_ref, bf16[384,1536]{1,0:T(8,128)(2,1)S(1)} %get-tuple-element.29.own_ref, ...), custom_call_target="tpu_custom_call" | custom-call | flops 5000000000 | bytes 1 | tf_op jit(solution)/shard_map/project_source_attend_tail/pallas_call | solution.py:351
  74.7 0.4 collective-permute-start.17
  75.3 4.4 %collective-permute-start.15 = (bf16[128,768]{1,0:T(8,128)(2,1)S(1)}, bf16[128,768]{1,0:T(8,128)(2,1)S(1)}, u32[]{:S(2)}, u32[]{:S(2)}) collective-permute-start(bf16[128,768]{1,0:T(8,128)(2,1)S(1)} %get-tuple-element.33), channel_id=1, source_target_pairs={{0,1},{1,2},{2,3},{3,4},{4,5},{5,6},{6,7},{8,9},{9,10},{10,11},{11... | collective-permute-start | bytes 589832 | tf_op jit(solution)/shard_map/ppermute | solution.py:58
  79.8 3.9 %attend_main.1.attended_ref = f32[256,768]{1,0:T(8,128)S(1)} custom-call(f32[3,3]{1,0:T(4,128)S(1)} %and_select_fusion.bias_ref, bf16[384,768]{1,0:T(8,128)(2,1)S(1)} %get-tuple-element.28.query_ref, bf16[768,1536]{1,0:T(8,128)(2,1)S(1)} %get-tuple-element.31.keyval_ref), custom_call_target="tpu_custom_call" | custom-call | flops 4000000000 | bytes 1 | tf_op jit(solution)/shard_map/attend_main/pallas_call | solution.py:378
  83.7 1.4 %collective-permute-done.15.received_ref = bf16[128,768]{1,0:T(8,128)(2,1)S(1)} collective-permute-done((bf16[128,768]{1,0:T(8,128)(2,1)S(1)}, bf16[128,768]{1,0:T(8,128)(2,1)S(1)}, u32[]{:S(2)}, u32[]{:S(2)}) %collective-permute-start.15) | collective-permute-done | bytes 196640 | tf_op jit(solution)/shard_map/ppermute | solution.py:58
  85.1 2.4 %blend_and_step.1 = bf16[256,1536]{1,0:T(8,128)(2,1)} custom-call(s32[4]{0:T(128)S(1)} %pad_add_fusion.places_ref, f32[4]{0:T(128)S(1)} %pad_maximum_fusion.2.coef_ref, f32[256,768]{1,0:T(8,128)S(1)} %attend_main.1.attended_ref, bf16[128,768]{1,0:T(8,128)(2,1)S(1)} %collective-permute-done.15.received_ref, bf16[256,1536]{1,0:T(8,128)(2,1)S(1)} %bitcast.30, ...), custom_call_target="tpu_custom_call" | custom-call | flops 3000000000 | bytes 1 | tf_op jit(solution)/shard_map/blend_and_step/pallas_call | solution.py:412
  (51 shorter events, 0.9 us)
Async XLA Ops:
  0.1 0.7 copy-start.5
  6.1 13.1 %copy-start = (bf16[1,256,1536]{2,1,0:T(8,128)(2,1)S(1)}, bf16[1,256,1536]{2,1,0:T(8,128)(2,1)}, u32[]{:S(2)}) copy-start(bf16[1,256,1536]{2,1,0:T(8,128)(2,1)} %param.9) | copy-start | bytes 2359300
  6.1 13.1 %collective-permute-start.1 = (bf16[96,2304]{1,0:T(8,128)(2,1)S(1)}, bf16[96,2304]{1,0:T(8,128)(2,1)}, u32[]{:S(2)}, u32[]{:S(2)}) collective-permute-start(bf16[96,2304]{1,0:T(8,128)(2,1)S(1)} %get-tuple-element.21), channel_id=1, source_target_pairs={{0,16},{8,24},{16,0},{24,8},{1,17},{9,25},{17,1},{25,9},{2,18},{10... | collective-permute-start | bytes 1327112 | tf_op jit(solution)/shard_map/ppermute | solution.py:52
  6.7 12.5 %collective-permute-start = (bf16[128,1536]{1,0:T(8,128)(2,1)S(1)}, bf16[128,1536]{1,0:T(8,128)(2,1)S(1)}, u32[]{:S(2)}, u32[]{:S(2)}) collective-permute-start(bf16[128,1536]{1,0:T(8,128)(2,1)S(1)} %get-tuple-element.20), channel_id=1, source_target_pairs={{1,0},{2,1},{3,2},{4,3},{5,4},{6,5},{7,6},{9,8},{10,9},{11,10},{12... | collective-permute-start | bytes 1179656 | tf_op jit(solution)/shard_map/ppermute | solution.py:58
  19.2 26.6 %copy-start.6 = (s32[3,3]{1,0:T(4,128)S(1)}, s32[3,3]{1,0:T(4,128)}, u32[]{:S(2)}) copy-start(s32[3,3]{1,0:T(4,128)} %param.13) | copy-start | bytes 112
  19.2 36.0 %collective-permute-start.11 = (bf16[384,1536]{1,0:T(8,128)(2,1)S(1)}, bf16[384,1536]{1,0:T(8,128)(2,1)}, u32[]{:S(2)}, u32[]{:S(2)}) collective-permute-start(bf16[384,1536]{1,0:T(8,128)(2,1)S(1)} %pad_maximum_fusion.refs_0_), channel_id=1, source_target_pairs={{0,16},{1,17},{2,18},{3,19},{4,20},{5,21},{6,22},{7,23}} | collective-permute-start | bytes 3538952 | tf_op jit(solution)/shard_map/ppermute | solution.py:438
  20.5 24.5 %collective-permute-start.4 = (bf16[96,2304]{1,0:T(8,128)(2,1)}, bf16[96,2304]{1,0:T(8,128)(2,1)}, u32[]{:S(2)}, u32[]{:S(2)}) collective-permute-start(bf16[96,2304]{1,0:T(8,128)(2,1)} %get-tuple-element.27), channel_id=1, source_target_pairs={{0,16},{8,24},{16,0},{24,8},{1,17},{9,25},{17,1},{25,9},{2,18},{10... | collective-permute-start | bytes 1327112 | tf_op jit(solution)/shard_map/ppermute | solution.py:52
  24.2 21.5 %collective-permute-start.9 = (bf16[384,768]{1,0:T(8,128)(2,1)}, bf16[384,768]{1,0:T(8,128)(2,1)}, u32[]{:S(2)}, u32[]{:S(2)}) collective-permute-start(bf16[384,768]{1,0:T(8,128)(2,1)} %refs_8_.1), channel_id=1, source_target_pairs={{0,8},{8,0},{16,24},{24,16},{1,9},{9,1},{17,25},{25,17},{2,10},{10... | collective-permute-start | bytes 1769480 | tf_op jit(solution)/shard_map/ppermute | solution.py:52
  24.2 34.0 %collective-permute-start.10 = (bf16[384,1536]{1,0:T(8,128)(2,1)}, bf16[384,1536]{1,0:T(8,128)(2,1)}, u32[]{:S(2)}, u32[]{:S(2)}) collective-permute-start(bf16[384,1536]{1,0:T(8,128)(2,1)} %refs_10_.1), channel_id=1, source_target_pairs={{0,8},{8,0},{16,24},{24,16},{1,9},{9,1},{17,25},{25,17},{2,10},{10... | collective-permute-start | bytes 3538952 | tf_op jit(solution)/shard_map/ppermute | solution.py:52
  25.3 21.7 %all-to-all-start = ((f32[32,1,192]{2,1,0:T(1,128)}), f32[32,1,192]{2,1,0:T(1,128)S(1)}, u32[]{:S(2)}, u32[]{:S(2)}) async-start(f32[32,1,192]{2,1,0:T(1,128)} %broadcast_in_dim.23), calls=%async_computation | async-start | bytes 65536 | tf_op jit(solution)/shard_map/all_to_all | solution.py:92
  31.9 13.9 %collective-permute-start.2 = (bf16[96,2304]{1,0:T(8,128)(2,1)}, bf16[96,2304]{1,0:T(8,128)(2,1)S(1)}, u32[]{:S(2)}, u32[]{:S(2)}) collective-permute-start(bf16[96,2304]{1,0:T(8,128)(2,1)} %get-tuple-element.24.refs_0_), channel_id=1, source_target_pairs={{0,1},{1,0},{2,3},{3,2},{4,5},{5,4},{6,7},{7,6},{8,9},{9,8},{10,11... | collective-permute-start | bytes 1327112 | tf_op jit(solution)/shard_map/ppermute | solution.py:52
  45.0 8.5 %collective-permute-start.3 = (bf16[96,2304]{1,0:T(8,128)(2,1)}, bf16[96,2304]{1,0:T(8,128)(2,1)S(1)}, u32[]{:S(2)}, u32[]{:S(2)}) collective-permute-start(bf16[96,2304]{1,0:T(8,128)(2,1)} %get-tuple-element.24.refs_0_), channel_id=1, source_target_pairs={{0,2},{1,3},{2,0},{3,1},{4,6},{5,7},{6,4},{7,5},{8,10},{9,11},{10,... | collective-permute-start | bytes 1327112 | tf_op jit(solution)/shard_map/ppermute | solution.py:52
  45.7 11.9 %collective-permute-start.5 = (bf16[96,2304]{1,0:T(8,128)(2,1)}, bf16[96,2304]{1,0:T(8,128)(2,1)}, u32[]{:S(2)}, u32[]{:S(2)}) collective-permute-start(bf16[96,2304]{1,0:T(8,128)(2,1)} %get-tuple-element.24.refs_0_), channel_id=1, source_target_pairs={{0,8},{8,0},{16,24},{24,16},{1,9},{9,1},{17,25},{25,17},{2,10},{10... | collective-permute-start | bytes 1327112 | tf_op jit(solution)/shard_map/ppermute | solution.py:52
  45.8 11.9 %collective-permute-start.8 = (bf16[96,2304]{1,0:T(8,128)(2,1)}, bf16[96,2304]{1,0:T(8,128)(2,1)}, u32[]{:S(2)}, u32[]{:S(2)}) collective-permute-start(bf16[96,2304]{1,0:T(8,128)(2,1)} %collective-permute-done.4.refs_3_), channel_id=1, source_target_pairs={{0,8},{8,0},{16,24},{24,16},{1,9},{9,1},{17,25},{25,17},{2,10},{10... | collective-permute-start | bytes 1327112 | tf_op jit(solution)/shard_map/ppermute | solution.py:52
  53.5 14.5 %collective-permute-start.12 = (bf16[384,1536]{1,0:T(8,128)(2,1)S(1)}, bf16[384,1536]{1,0:T(8,128)(2,1)}, u32[]{:S(2)}, u32[]{:S(2)}) collective-permute-start(bf16[384,1536]{1,0:T(8,128)(2,1)S(1)} %pad_maximum_fusion.refs_0_), channel_id=1, source_target_pairs={{0,8},{1,9},{2,10},{3,11},{4,12},{5,13},{6,14},{7,15}} | collective-permute-start | bytes 3538952 | tf_op jit(solution)/shard_map/ppermute | solution.py:438
  55.2 12.9 %collective-permute-start.13 = (bf16[384,1536]{1,0:T(8,128)(2,1)}, bf16[384,1536]{1,0:T(8,128)(2,1)}, u32[]{:S(2)}, u32[]{:S(2)}) collective-permute-start(bf16[384,1536]{1,0:T(8,128)(2,1)} %collective-permute-done.11.refs_1_), channel_id=1, source_target_pairs={{16,24},{17,25},{18,26},{19,27},{20,28},{21,29},{22,30},{23,31}} | collective-permute-start | bytes 3538952 | tf_op jit(solution)/shard_map/ppermute | solution.py:447
  57.6 2.6 %copy-start.1 = (bf16[96,2304]{1,0:T(8,128)(2,1)}, bf16[96,2304]{1,0:T(8,128)(2,1)S(1)}, u32[]{:S(2)}) copy-start(bf16[96,2304]{1,0:T(8,128)(2,1)S(1)} %get-tuple-element.25.refs_1_) | copy-start | bytes 1327108
  57.7 2.6 %copy-start.2 = (bf16[96,2304]{1,0:T(8,128)(2,1)}, bf16[96,2304]{1,0:T(8,128)(2,1)S(1)}, u32[]{:S(2)}) copy-start(bf16[96,2304]{1,0:T(8,128)(2,1)S(1)} %get-tuple-element.26.refs_2_) | copy-start | bytes 1327108
  57.7 1.9 %collective-permute-start.6 = (bf16[96,2304]{1,0:T(8,128)(2,1)S(1)}, bf16[96,2304]{1,0:T(8,128)(2,1)S(1)}, u32[]{:S(2)}, u32[]{:S(2)}) collective-permute-start(bf16[96,2304]{1,0:T(8,128)(2,1)S(1)} %get-tuple-element.25.refs_1_), channel_id=1, source_target_pairs={{0,8},{8,0},{16,24},{24,16},{1,9},{9,1},{17,25},{25,17},{2,10},{10... | collective-permute-start | bytes 1327112 | tf_op jit(solution)/shard_map/ppermute | solution.py:52
  57.8 2.5 %collective-permute-start.7 = (bf16[96,2304]{1,0:T(8,128)(2,1)S(1)}, bf16[96,2304]{1,0:T(8,128)(2,1)S(1)}, u32[]{:S(2)}, u32[]{:S(2)}) collective-permute-start(bf16[96,2304]{1,0:T(8,128)(2,1)S(1)} %get-tuple-element.26.refs_2_), channel_id=1, source_target_pairs={{0,8},{8,0},{16,24},{24,16},{1,9},{9,1},{17,25},{25,17},{2,10},{10... | collective-permute-start | bytes 1327112 | tf_op jit(solution)/shard_map/ppermute | solution.py:52
  58.3 16.5 %collective-permute-start.14 = (bf16[192,1536]{1,0:T(8,128)(2,1)}, bf16[192,1536]{1,0:T(8,128)(2,1)S(1)}, u32[]{:S(2)}, u32[]{:S(2)}) collective-permute-start(bf16[192,1536]{1,0:T(8,128)(2,1)} %refs_0_.1), channel_id=1, source_target_pairs={{0,16},{8,24},{16,0},{24,8},{1,17},{9,25},{17,1},{25,9},{2,18},{10... | collective-permute-start | bytes 1769480 | tf_op jit(solution)/shard_map/ppermute | solution.py:52
  59.6 0.8 copy-start.7
  59.6 24.1 %collective-permute-start.16 = (bf16[192,1536]{1,0:T(8,128)(2,1)}, bf16[192,1536]{1,0:T(8,128)(2,1)S(1)}, u32[]{:S(2)}, u32[]{:S(2)}) collective-permute-start(bf16[192,1536]{1,0:T(8,128)(2,1)} %refs_0_.1), channel_id=1, source_target_pairs={{0,8},{8,0},{16,24},{24,16},{1,9},{9,1},{17,25},{25,17},{2,10},{10... | collective-permute-start | bytes 1769480 | tf_op jit(solution)/shard_map/ppermute | solution.py:52
  60.3 0.8 copy-start.8
  74.7 10.3 %collective-permute-start.17 = (bf16[192,1536]{1,0:T(8,128)(2,1)S(1)}, bf16[192,1536]{1,0:T(8,128)(2,1)S(1)}, u32[]{:S(2)}, u32[]{:S(2)}) collective-permute-start(bf16[192,1536]{1,0:T(8,128)(2,1)S(1)} %get-tuple-element.34.refs_2_), channel_id=1, source_target_pairs={{0,8},{8,0},{16,24},{24,16},{1,9},{9,1},{17,25},{25,17},{2,10},{10... | collective-permute-start | bytes 1769480 | tf_op jit(solution)/shard_map/ppermute | solution.py:52
  75.3 9.7 %collective-permute-start.15 = (bf16[128,768]{1,0:T(8,128)(2,1)S(1)}, bf16[128,768]{1,0:T(8,128)(2,1)S(1)}, u32[]{:S(2)}, u32[]{:S(2)}) collective-permute-start(bf16[128,768]{1,0:T(8,128)(2,1)S(1)} %get-tuple-element.33), channel_id=1, source_target_pairs={{0,1},{1,2},{2,3},{3,4},{4,5},{5,6},{6,7},{8,9},{9,10},{10,11},{11... | collective-permute-start | bytes 589832 | tf_op jit(solution)/shard_map/ppermute | solution.py:58
  79.7 5.3 %copy-start.3 = (bf16[1,256,1536]{2,1,0:T(8,128)(2,1)S(1)}, bf16[1,256,1536]{2,1,0:T(8,128)(2,1)}, u32[]{:S(2)}) copy-start(bf16[1,256,1536]{2,1,0:T(8,128)(2,1)} %param.10) | copy-start | bytes 2359300
  79.8 5.3 %copy-start.4 = (bf16[192,1536]{1,0:T(8,128)(2,1)S(1)}, bf16[192,1536]{1,0:T(8,128)(2,1)}, u32[]{:S(2)}) copy-start(bf16[192,1536]{1,0:T(8,128)(2,1)} %refs_0_.1) | copy-start | bytes 1769476

commit v3 on v2

v3 whole, which is shorter than its diff:
```python
import functools
import math

import jax
import jax.numpy as jnp
from jax import lax
from jax.experimental import pallas as pl
from jax.experimental.pallas import tpu as pltpu
from jax.sharding import PartitionSpec as P

HEADS = 12
HS = 64
SEAM = 128
BLK = 128
TSTEPS = 1000
STRIDE = 200
LANES = 128

epsilon = 1e-06
MASKED = -1e30
MICROSECOND = 10**9
VMEM_LIMIT = 18 * 1024 * 1024
ALL_VMEM = 62 * 1024 * 1024

BF16 = jnp.bfloat16
F32 = jnp.float32


def plan(moment):
    return jnp.cos((moment / TSTEPS + 0.008) / 1.008 * (math.pi / 2.0)) ** 2


def coefficients(timestep):
    current = timestep[0].astype(jnp.float32)
    abar_now = plan(current)
    abar_prev = plan(current - STRIDE)
    spread = jnp.sqrt((1.0 - abar_prev) / (1.0 - abar_now) * (1.0 - abar_now / abar_prev))
    carried = jnp.sqrt((1.0 - abar_prev) * (abar_now / abar_prev - abar_now) / (1.0 - abar_now))
    coef_pred = carried - jnp.sqrt(abar_prev) * jnp.sqrt(1.0 - abar_now) / jnp.sqrt(abar_now)
    coef_latent = jnp.sqrt(abar_prev / abar_now)
    return (current, coef_latent, coef_pred, spread)


def time_waves(current, model_width):
    half_width = model_width // 2
    frequency = jnp.exp(-math.log(10000.0) * jnp.arange(half_width, dtype=jnp.float32) / half_width)
    angles = current * frequency
    return (jnp.cos(angles)[None, :], jnp.sin(angles)[None, :])


def swapped(block, axis, bit):
    route = [(i, i ^ bit) for i in range(lax.axis_size(axis))]
    return lax.ppermute(block, axis, route)


def shifted(block, axis, distance):
    devices = range(lax.axis_size(axis))
    route = [(i - distance, i) for i in devices if i - distance in devices]
    return lax.ppermute(block, axis, route)


def vmem():
    return pl.BlockSpec(memory_space=pltpu.VMEM)


def smem():
    return pl.BlockSpec(memory_space=pltpu.SMEM)


def params(limit=VMEM_LIMIT):
    return pltpu.CompilerParams(vmem_limit_bytes=limit)


def anywhere():
    return pl.BlockSpec(memory_space=pl.ANY)


def hbm():
    return pl.BlockSpec(memory_space=pltpu.HBM)


def in_hbm(value):
    return pltpu.with_memory_space_constraint(value, pltpu.HBM)


def cost(flops):
    return pl.CostEstimate(flops=flops, bytes_accessed=1, transcendentals=0)


def whole_rows(row):
    tm_count = lax.axis_size("tm")
    sent = jnp.broadcast_to(row, (tm_count, row.shape[1]))
    arrived = lax.all_to_all(sent, "tm", 0, 0, tiled=True)
    if row.shape[1] % HS or tm_count % 8:
        arrived = arrived.reshape(1, tm_count * row.shape[1])
    return arrived


def first_kernel(
    places_ref, ids_ref, table_ref, query_ref, keyval_ref, out_weights_ref, latent_ref, *refs
):
    pooled_ref, halo_ref, out_cut_ref, *cut_refs, columns, sems = refs
    head_width = query_ref.shape[1]
    copies = [
        pltpu.make_async_copy(table_ref, columns, sems.at[0]),
        pltpu.make_async_copy(latent_ref.at[: halo_ref.shape[0], :], halo_ref, sems.at[1]),
    ]
    out_rows = out_cut_ref.shape[0]
    at = pl.ds(aligned(places_ref[0] * out_rows, 16), out_rows)
    copies.append(pltpu.make_async_copy(out_weights_ref.at[at, :], out_cut_ref, sems.at[2]))
    for k, target in enumerate(cut_refs):
        rows = target.shape[0]
        at = pl.ds(aligned(places_ref[1 + k] * rows, 16), rows)
        copies += [
            pltpu.make_async_copy(
                query_ref.at[at, :], target.at[:, :head_width], sems.at[3 + 2 * k]
            ),
            pltpu.make_async_copy(
                keyval_ref.at[at, :], target.at[:, head_width:], sems.at[4 + 2 * k]
            ),
        ]
    for copy in copies:
        copy.start()
    lane = lax.broadcasted_iota(jnp.int32, (1, LANES), 1)
    copies[0].wait()

    def body(j, total):
        token = ids_ref[0, j]
        start = pl.multiple_of((token >> 7) * LANES, LANES)
        block = columns[:, pl.ds(start, LANES)].astype(F32)
        return total + jnp.where(lane == (token & (LANES - 1)), block, 0.0)

    count = ids_ref.shape[1]
    total = lax.fori_loop(0, count, body, jnp.zeros((columns.shape[0], LANES), F32), unroll=8)
    ones = jnp.full((8, LANES), 1.0 / count, F32)
    pooled_ref[...] = lax.dot_general(
        ones,
        total,
        (((1,), (1,)), ((), ())),
        precision=lax.Precision.HIGHEST,
        preferred_element_type=F32,
    )
    for copy in copies[1:]:
        copy.wait()


def first_rows(side, places, prompt_ids, prompt_table, w_query, w_keyval, w_out, latent):
    table_columns = prompt_table.T
    quarter = w_query.shape[0] // 4
    columns = w_query.shape[1] + w_keyval.shape[1]
    return pl.pallas_call(
        first_kernel,
        out_shape=[
            jax.ShapeDtypeStruct((8, table_columns.shape[0]), F32),
            jax.ShapeDtypeStruct((SEAM, latent.shape[1]), BF16),
            jax.ShapeDtypeStruct((w_out.shape[0] // 2, w_out.shape[1]), BF16),
        ]
        + [jax.ShapeDtypeStruct((quarter, columns), BF16)] * len(places),
        in_specs=[smem(), smem()] + [hbm()] * 5,
        out_specs=[vmem()] * (3 + len(places)),
        scratch_shapes=[
            pltpu.VMEM(table_columns.shape, BF16),
            pltpu.SemaphoreType.DMA((3 + 2 * len(places),)),
        ],
        compiler_params=params(),
        cost_estimate=cost(4 * MICROSECOND),
        name="pool_and_first_rows",
    )(
        numbers(side, *places),
        prompt_ids,
        *[in_hbm(value) for value in (table_columns, w_query, w_keyval, w_out, latent)],
    )


def joined(parts):
    return parts[0] if len(parts) == 1 else jnp.concatenate(parts, axis=1)


def can_route(rows):
    return lax.axis_size("var") == 4 and lax.axis_size("tm") % 4 == 0 and rows % 128 == 0


def cut(weights, which, count):
    rows = weights[0].shape[0] // count
    return joined([lax.dynamic_slice_in_dim(w, which * rows, rows, 0) for w in weights])


def gate_kernel(*refs):
    del refs


def together(*values, limit=VMEM_LIMIT):
    return pl.pallas_call(
        gate_kernel,
        out_shape=[jax.ShapeDtypeStruct(v.shape, v.dtype) for v in values],
        in_specs=[anywhere()] * len(values),
        out_specs=[anywhere()] * len(values),
        input_output_aliases={k: k for k in range(len(values))},
        compiler_params=params(limit),
        cost_estimate=cost(1),
        name="gate",
    )(*values)


def numbers(*values):
    return jnp.stack([jnp.asarray(value, jnp.int32) for value in values])


def aligned(value, multiple):
    return pl.multiple_of(value, multiple)


def scale_of(rows_ref, cos_ref, sin_ref):
    rows = rows_ref[...]
    row = jnp.concatenate([rows[k : k + 1, :] for k in range(rows.shape[0])], axis=1)
    return 1.0 + (jnp.concatenate([cos_ref[...], sin_ref[...]], axis=1) + row)


def bias_of(table_ref, last, query_block):
    blocks = table_ref.shape[0]
    biases = []
    for j in range(blocks):
        allowed = table_ref[query_block, j] > 0
        if j == blocks - 1:
            allowed = jnp.logical_and(allowed, last == 0)
        biases.append(jnp.where(allowed, 0.0, MASKED))
    return biases


def normalize(target, begin, ref, scale, width):
    for row in range(0, ref.shape[0], 32):
        values = ref[row : row + 32, :].astype(F32)
        inv_norm = lax.rsqrt(jnp.sum(values * values, axis=-1, keepdims=True) / width + epsilon)
        target[begin + row : begin + row + 32, :] = (values * inv_norm * scale).astype(BF16)


def normalize_kernel(
    latent_ref, halo_ref, rows_ref, cos_ref, sin_ref, normed_ref, window, normed, rows, sems
):
    main_rows = latent_ref.shape[0]
    copies = [
        pltpu.make_async_copy(latent_ref, window.at[:main_rows, :], sems.at[0]),
        pltpu.make_async_copy(halo_ref, window.at[main_rows:, :], sems.at[1]),
        pltpu.make_async_copy(rows_ref, rows, sems.at[2]),
    ]
    for copy in copies:
        copy.start()
    for copy in copies:
        copy.wait()
    normalize(normed, 0, window, scale_of(rows, cos_ref, sin_ref), window.shape[1])
    copy = pltpu.make_async_copy(normed, normed_ref, sems.at[3])
    copy.start()
    copy.wait()


def normalized(latent, halo, rows, waves):
    shape = (latent.shape[0] + SEAM, latent.shape[1])
    return pl.pallas_call(
        normalize_kernel,
        out_shape=pltpu.HBM(shape, BF16),
        in_specs=[anywhere()] * 3 + [vmem()] * 2,
        out_specs=hbm(),
        scratch_shapes=[
            pltpu.VMEM(shape, BF16),
            pltpu.VMEM(shape, BF16),
            pltpu.VMEM(rows.shape, F32),
            pltpu.SemaphoreType.DMA((4,)),
        ],
        compiler_params=params(),
        cost_estimate=cost(MICROSECOND),
        name="normalize",
    )(latent, halo, rows, *waves)


def attend_rows(query, keyval_ref, bias, own_block, pair):
    head_width = keyval_ref.shape[1] // 2
    key_rows = keyval_ref.shape[0]
    blocks = len(bias)
    at = pl.ds(pair * LANES, LANES)
    value_at = pl.ds(head_width + pair * LANES, LANES)
    left = lax.broadcasted_iota(jnp.int32, (1, LANES), 1) < HS
    zero = jnp.zeros((), BF16)
    query = query * BF16(1.0 / math.sqrt(HS))
    both = jnp.concatenate([jnp.where(left, query, zero), jnp.where(left, zero, query)], axis=0)
    scores = lax.dot_general(
        both, keyval_ref[:, at], (((1,), (1,)), ((), ())), preferred_element_type=F32
    )
    cut_block = lambda j: scores[:, j * BLK : (j + 1) * BLK]
    peak = None
    for j in range(blocks):
        top = jnp.maximum(cut_block(j), cut_block(blocks + j))
        if j not in (0, own_block):
            top = top + bias[j]
        peak = top if peak is None else jnp.maximum(peak, top)
    peak = jnp.max(peak, axis=-1, keepdims=True)
    offsets = [peak if j in (0, own_block) else peak - bias[j] for j in range(blocks)]
    weights = jnp.concatenate(
        [jnp.exp(cut_block(j) - offsets[j % blocks]).astype(BF16) for j in range(2 * blocks)],
        axis=1,
    )
    ones = jnp.ones((key_rows, LANES), BF16)
    values = jnp.concatenate([keyval_ref[:, value_at], ones], axis=1)
    total = jnp.dot(weights, values, preferred_element_type=F32)
    mixed = total[:, :LANES] / total[:, LANES:]
    return jnp.where(left, mixed[:BLK], mixed[BLK:])


def project_kernel(n_wide, n_pairs, n_sources, places_ref, table_ref, normed_hbm, *refs):
    wide_pieces, refs = refs[:n_wide], refs[n_wide:]
    query_pieces, refs = refs[:n_pairs], refs[n_pairs:]
    keyval_pieces, refs = refs[:n_pairs], refs[n_pairs:]
    sources, refs = refs[:n_sources], refs[n_sources:]
    query_ref, keyval_ref, tail_ref, query_weights, keyval_weights, normed, tail_query, sems = refs
    head_width = query_weights.shape[1]
    window_rows = normed.shape[0] // 2
    main_rows = window_rows - SEAM
    own_rows = pl.ds(0, window_rows)
    source_rows = pl.ds(window_rows, window_rows)
    choice, last = places_ref[0], places_ref[1]

    rows_of = [(places_ref[2 + n_wide + k], p.shape[0]) for k, p in enumerate(query_pieces)]
    rows_of += [(places_ref[2 + k], p.shape[0]) for k, p in enumerate(wide_pieces)]
    rows_of = [pl.ds(aligned(start, 16), count) for start, count in rows_of]
    query_parts = list(query_pieces) + [p.at[:, :head_width] for p in wide_pieces]
    keyval_parts = list(keyval_pieces) + [p.at[:, head_width:] for p in wide_pieces]
    copies = [(normed_hbm, normed.at[own_rows, :])]
    copies += [(p, query_weights.at[at, :]) for p, at in zip(query_parts, rows_of)]
    copies += [(p, keyval_weights.at[at, :]) for p, at in zip(keyval_parts, rows_of)]
    copies = [
        pltpu.make_async_copy(source, target, sems.at[k])
        for k, (source, target) in enumerate(copies)
    ]
    for copy in copies:
        copy.start()
    source_copies = [
        pltpu.make_async_copy(source, normed.at[source_rows, :], sems.at[len(copies)])
        for source in sources
    ]
    for k, copy in enumerate(source_copies):
        pl.when(choice == k)(copy.start)
    for copy in copies[: 1 + len(rows_of)]:
        copy.wait()
    step = 256
    for begin in range(0, head_width, step):
        at = pl.ds(begin, step)
        result = jnp.dot(
            normed[own_rows, :], query_weights[:, at], preferred_element_type=F32
        ).astype(BF16)
        query_ref[:, at] = result[:main_rows]
        tail_query[:, at] = result[main_rows:]
    for k, copy in enumerate(source_copies):
        pl.when(choice == k)(copy.wait)
    for copy in copies[1 + len(rows_of) :]:
        copy.wait()
    for begin in range(0, 2 * head_width, step):
        at = pl.ds(begin, step)
        keyval_ref[:, at] = jnp.dot(
            normed[...], keyval_weights[:, at], preferred_element_type=F32
        ).astype(BF16)
    blocks = window_rows // BLK
    row = lax.broadcasted_iota(jnp.int32, (BLK, 1), 0).astype(F32)
    fade = 1.0 - (row + 0.5) / SEAM
    bias = bias_of(table_ref, last, blocks - 1)
    for pair in range(HEADS // 2):
        at = pl.ds(pair * LANES, LANES)
        mixed = attend_rows(tail_query[:, at], keyval_ref, bias, blocks - 1, pair)
        tail_ref[:, at] = (mixed * fade).astype(BF16)


def project(
    choice, last, block_table, normed, wide, wide_places, queries, keyvals, pair_places, sources
):
    window_rows, width = normed.shape
    keyval_width = keyvals[0].shape[1]
    head_width = keyval_width // 2
    n_copies = 1 + 2 * (len(wide) + len(queries))
    arrays = (normed, *wide, *queries, *keyvals, *sources)
    late = (*wide[6:], sources[-1])
    specs = [anywhere() if any(a is b for b in late) else hbm() for a in arrays]
    arrays = [a if any(a is b for b in late) else in_hbm(a) for a in arrays]
    return pl.pallas_call(
        functools.partial(project_kernel, len(wide), len(queries), len(sources)),
        out_shape=[
            jax.ShapeDtypeStruct((window_rows - SEAM, head_width), BF16),
            jax.ShapeDtypeStruct((2 * window_rows, keyval_width), BF16),
            jax.ShapeDtypeStruct((SEAM, head_width), BF16),
        ],
        in_specs=[smem(), smem()] + specs,
        out_specs=[vmem()] * 3,
        scratch_shapes=[
            pltpu.VMEM((width, head_width), BF16),
            pltpu.VMEM((width, keyval_width), BF16),
            pltpu.VMEM((2 * window_rows, width), BF16),
            pltpu.VMEM((SEAM, head_width), BF16),
            pltpu.SemaphoreType.DMA((n_copies + 1,)),
        ],
        compiler_params=params(),
        cost_estimate=cost(10 * MICROSECOND),
        name="project_attend_tail",
    )(
        numbers(choice, last, *wide_places, *pair_places),
        block_table,
        *arrays,
    )


def main_kernel(places_ref, table_ref, query_ref, keyval_ref, out_ref):
    blocks = keyval_ref.shape[0] // (2 * BLK)
    for i in range(blocks - 1):
        bias = bias_of(table_ref, places_ref[0], i)
        rows = pl.ds(i * BLK, BLK)
        for pair in range(HEADS // 2):
            at = pl.ds(pair * LANES, LANES)
            out_ref[rows, at] = attend_rows(query_ref[rows, at], keyval_ref, bias, i, pair)


def attend_main(last, block_table, query, keyval):
    rows, width = query.shape
    return pl.pallas_call(
        main_kernel,
        out_shape=jax.ShapeDtypeStruct((rows, width), F32),
        in_specs=[smem(), smem(), vmem(), vmem()],
        out_specs=vmem(),
        compiler_params=params(),
        cost_estimate=cost(4 * MICROSECOND),
        name="attend_main",
    )(numbers(last), block_table, query, keyval)


def finish_kernel(
    n_pieces, places_ref, coef_ref, attended_ref, received_ref, latent_ref, noise_ref, *refs
):
    pieces, (out_ref, weights) = refs[:n_pieces], refs[n_pieces:]
    for k, piece in enumerate(pieces):
        weights[pl.ds(aligned(places_ref[k], 16), piece.shape[0]), :] = piece[...]
    row = lax.broadcasted_iota(jnp.int32, (SEAM, 1), 0).astype(F32)
    ramp_up = jnp.where(coef_ref[3] > 0.5, 1.0, (row + 0.5) / SEAM)
    lead = attended_ref[:SEAM, :] * ramp_up + received_ref[...].astype(F32)
    blended = jnp.concatenate([lead, attended_ref[SEAM:, :]], axis=0).astype(BF16)
    step = 256
    for begin in range(0, out_ref.shape[1], step):
        at = pl.ds(begin, step)
        prediction = jnp.dot(blended, weights[:, at], preferred_element_type=F32)
        result = (
            coef_ref[0] * latent_ref[:, at].astype(F32)
            + coef_ref[1] * prediction
            + coef_ref[2] * noise_ref[:, at].astype(F32)
        )
        out_ref[:, at] = result.astype(BF16)


def finish(coefs, attended, received, latent, noise, pieces, places):
    return pl.pallas_call(
        functools.partial(finish_kernel, len(pieces)),
        out_shape=jax.ShapeDtypeStruct(latent.shape, BF16),
        in_specs=[smem(), smem()] + [vmem()] * (4 + len(pieces)),
        out_specs=vmem(),
        scratch_shapes=[pltpu.VMEM((attended.shape[1], latent.shape[1]), BF16)],
        compiler_params=params(),
        cost_estimate=cost(3 * MICROSECOND),
        name="blend_and_step",
    )(
        numbers(*places),
        coefs,
        attended,
        received,
        latent,
        noise,
        *pieces,
    )


def from_source(value):
    bits = []
    bit = lax.axis_size("var") // 2
    while bit:
        bits.append(bit)
        bit //= 2
    return [(lax.ppermute(value, "var", [(0, bit)]), bit) for bit in bits]


def passed_on(value, arrivals):
    count = lax.axis_size("var")
    place = lax.axis_index("var")
    arrays, choice = [value, arrivals[0][0]], (place == arrivals[0][1]).astype(jnp.int32)
    for array, bit in arrivals[1:]:
        payload = functools.reduce(jnp.add, arrays[1:])
        route = [(i, i + bit) for i in range(2 * bit, count, 2 * bit)]
        choice = jnp.where(place == bit, len(arrays), choice)
        arrays.append(array)
        choice = jnp.where((place > bit) & (place % (2 * bit) == bit), len(arrays), choice)
        arrays.append(lax.ppermute(payload, "var", route))
    return arrays, choice


def local(
    latent, fresh_noise, timestep, prompt_ids, block_table, prompt_table, w_query, w_keyval, w_out
):
    latent = latent[0]
    own_rows, model_width = latent.shape
    tm_count = lax.axis_size("tm")
    tm_place = lax.axis_index("tm")
    var_place = lax.axis_index("var")
    rows = w_query.shape[0]
    routed = can_route(rows)
    corner = tm_place & 3

    side = tm_place & 1
    pooled, halo_rows, out_cut, *cuts = first_rows(
        side if routed else 0,
        (corner, corner ^ 3) if routed else (),
        prompt_ids,
        prompt_table,
        w_query,
        w_keyval,
        w_out,
        latent,
    )
    halo = shifted(halo_rows, "tm", -1)
    pooled = whole_rows(pooled[:1])
    if routed:
        quarter = rows // 4
        first = swapped(cuts[0], "var", 2)
        fourth = swapped(cuts[1], "var", 2)
        halo, pooled, first, fourth = together(
            halo, pooled, first, fourth, limit=ALL_VMEM
        )

    current, coef_latent, coef_pred, spread = coefficients(timestep)
    normed = normalized(latent, halo, pooled, time_waves(current, model_width))
    sources = from_source(normed)
    if routed:
        second = swapped(first, "tm", 1)
        third = swapped(first, "tm", 2)
        queries, keyvals = [w_query], [w_keyval]
        fetched = [second, third]
        fetched += [swapped(piece, "var", 1) for piece in (first, fourth, w_query, w_keyval)]
        fetched += [swapped(out_cut, "var", 2)] + [array for array, _ in sources]
        second, third, first_over, fourth_over, partner_query, partner_keyval, *fetched = together(
            *fetched, limit=ALL_VMEM
        )
        out_first, *fetched = fetched
        sources = [(array, bit) for array, (_, bit) in zip(fetched, sources)]

        wide = [first, second, third, fourth, first_over, fourth_over]
        wide += [swapped(second, "var", 1), swapped(third, "var", 1)]
        here, there = (var_place ^ 2) * rows, (var_place ^ 3) * rows
        wide_places = [here + (corner ^ k) * quarter for k in range(4)]
        wide_places += [there + (corner ^ k) * quarter for k in (0, 3, 1, 2)]
        queries, keyvals = [w_query, partner_query], [w_keyval, partner_keyval]
        pair_places = [var_place * rows, (var_place ^ 1) * rows]
    else:
        wide, wide_places, pair_places = [], [], [0]
        queries = [lax.all_gather(w_query, "var", axis=0, tiled=True)]
        keyvals = [lax.all_gather(w_keyval, "var", axis=0, tiled=True)]
    sources, choice = passed_on(normed, sources)
    last = tm_place == tm_count - 1
    query, keyval, tail = project(
        choice,
        last,
        block_table,
        normed,
        wide,
        wide_places,
        queries,
        keyvals,
        pair_places,
        sources,
    )
    if routed:
        tail, out_second = together(tail, swapped(out_first, "tm", 1))
        out_rows = w_out.shape[0]
        half = out_rows // 2
        out_pieces = [w_out, swapped(w_out, "var", 1), out_first, out_second]
        out_pieces += [swapped(out_first, "var", 1), swapped(out_second, "var", 1)]
        out_places = [var_place * out_rows, (var_place ^ 1) * out_rows]
        out_places += [(var_place ^ 2) * out_rows + place * half for place in (side, 1 - side)]
        out_places += [(var_place ^ 3) * out_rows + place * half for place in (side, 1 - side)]
    else:
        out_pieces, out_places = [lax.all_gather(w_out, "var", axis=0, tiled=True)], [0]
    received = shifted(tail, "tm", 1)
    attended = attend_main(last, block_table, query, keyval)
    coefs = jnp.stack([coef_latent, coef_pred, spread, (tm_place == 0).astype(F32)])
    return finish(coefs, attended, received, latent, fresh_noise[0], out_pieces, out_places)[None]


def solution(mesh):
    placed = (
        P("var", "tm", None),
        P("var", "tm", None),
        P(),
        P("var", None),
        P(),
        P(None, "tm"),
        P("var", None),
        P("var", None),
        P("var", None),
    )
    return jax.shard_map(
        local, mesh=mesh, in_specs=placed, out_specs=P("var", "tm", None), check_vma=False
    )
```

time: 88.4 us -> 77.8 us (0.88)
  waiting for transfers between devices: 29.9 us -> 24.6 us
  starting transfers between devices: 27.8 us -> 24.4 us
  Pallas kernels: 25.2 us -> 22.9 us
  local copies, waits for them, and re-layouts: 2.53 us -> 3.74 us
    ppermute x2, waiting for transfers between devices: 10.5 us -> 1.92 us  [shifted(): return lax.ppermute(block, axis, route)]
    all_to_all x1, waiting for transfers between devices: 0.01 us -> 4.24 us  [whole_rows(): arrived = lax.all_to_all(sent, 'tm', 0, 0, tiled=True)]
    ppermute x13 -> x15, waiting for transfers between devices: 19.3 us -> 16.9 us  [swapped(): return lax.ppermute(block, axis, route)]
    ppermute x2, waiting for transfers between devices: 0.01 us -> 1.59 us  [from_source(): return [(lax.ppermute(value, 'var', [(0, bit)]), bit) for bit in bits]]
    pallas_call x2, Pallas kernels: 13.5 us -> 12 us  [the longest x1 10.2 us: project(): pl.pallas_call(functools.partial(project_kernel, len(wide), len(queries),...]
    unnamed x18 -> x25, local copies, waits for them, and re-layouts: 1.61 us -> 2.96 us
    ppermute x13 -> x15, starting transfers between devices: 8.98 us -> 7.78 us  [swapped(): return lax.ppermute(block, axis, route)]
    ppermute x1, starting transfers between devices: 2.32 us -> 1.36 us  [passed_on(): arrays.append(lax.ppermute(payload, 'var', route))]
  transfers between devices with their start and end apart: 19 -> 21, of which waited for: 6 -> 10; matrix products, arithmetic and copies ran while one was open for 1% -> 2% of each run, Pallas kernels for 20% -> 21%
where the time goes in v3:
time: 77.8 us; the launch traced here: 77.5 us
  waiting for transfers between devices  24.6 us (32%)
  starting transfers between devices  24.4 us (31%)
  Pallas kernels  22.9 us (29%)
  local copies, waits for them, and re-layouts  3.74 us (5%)
  between operations  1.51 us (2%)
    ppermute x15, waiting for transfers between devices, swapped(): return lax.ppermute(block, axis, route)  16.9 us
    pallas_call x1, Pallas kernels, project(): pl.pallas_call(functools.partial(project_kernel, len(wide), len(queries),...  10.2 us
    ppermute x15, starting transfers between devices, swapped(): return lax.ppermute(block, axis, route)  7.78 us
    ppermute x2, starting transfers between devices, shifted(): return lax.ppermute(block, axis, route)  6.91 us
    all_to_all x1, starting transfers between devices, whole_rows(): arrived = lax.all_to_all(sent, 'tm', 0, 0, tiled=True)  5.4 us
    pallas_call x1, Pallas kernels, first_rows(): pl.pallas_call(first_kernel, out_shape=[jax.ShapeDtypeStruct((8, table_co...  4.59 us
    all_to_all x1, waiting for transfers between devices, whole_rows(): arrived = lax.all_to_all(sent, 'tm', 0, 0, tiled=True)  4.24 us
    pallas_call x1, Pallas kernels, attend_main(): pl.pallas_call(main_kernel, out_shape=jax.ShapeDtypeStruct((rows, width),...  3.93 us
  transfers between devices with their start and end apart: 21, of which 10 were waited for; matrix products, arithmetic and copies ran while one was open for 2% of the time, Pallas kernels for 21%

profile of v3, /device:TPU:10, one launch (start us, length us, event | category | flops | bytes accessed | tf_op | source)
XLA Modules:
  0.0 77.5 jit_solution(15078135644587216215)
XLA Ops:
  0.1 0.7 copy-done.9
  0.7 4.6 %pool_and_first_rows.1 = (f32[8,192]{1,0:T(8,128)S(1)}, bf16[128,1536]{1,0:T(8,128)(2,1)S(1)}, bf16[96,1536]{1,0:T(8,128)(2,1)S(1)}, bf16[96,2304]{1,0:T(8,128)(2,1)S(1)}, bf16[96,2304]{1,0:T(8,128)(2,1)S(1)}) custom-call(s32[3]{0:T(128)S(1)} %pad_add_fusion.places_ref, s32[1,64]{1,0:T(1,128)S(1)} %copy-done.9, bf16[192,16384]{1,0:T(8,128)(2,1)} %bitcast.40, ...), custom_call_target="tpu_custom_call" | custom-call | flops 4000000000 | bytes 1 | tf_op jit(solution)/shard_map/pool_and_first_rows/pallas_call | solution.py:151
  5.3 0.6 collective-permute-start.1
  5.9 1.5 %collective-permute-start.2 = (bf16[96,2304]{1,0:T(8,128)(2,1)S(1)}, bf16[96,2304]{1,0:T(8,128)(2,1)}, u32[]{:S(2)}, u32[]{:S(2)}) collective-permute-start(bf16[96,2304]{1,0:T(8,128)(2,1)S(1)} %get-tuple-element.31), channel_id=1, source_target_pairs={{0,16},{8,24},{16,0},{24,8},{1,17},{9,25},{17,1},{25,9},{2,18},{10... | collective-permute-start | bytes 1327112 | tf_op jit(solution)/shard_map/ppermute | solution.py:53
  7.4 3.3 %collective-permute-start = (bf16[128,1536]{1,0:T(8,128)(2,1)S(1)}, bf16[128,1536]{1,0:T(8,128)(2,1)S(1)}, u32[]{:S(2)}, u32[]{:S(2)}) collective-permute-start(bf16[128,1536]{1,0:T(8,128)(2,1)S(1)} %get-tuple-element.28), channel_id=1, source_target_pairs={{1,0},{2,1},{3,2},{4,3},{5,4},{6,5},{7,6},{9,8},{10,9},{11,10},{12... | collective-permute-start | bytes 1179656 | tf_op jit(solution)/shard_map/ppermute | solution.py:59
  10.8 0.5 collective-permute-start.8
  11.3 0.6 broadcast_in_dim.4
  11.9 5.4 %all-to-all-start = ((f32[8,1,192]{2,1,0:T(1,128)}), f32[8,1,192]{2,1,0:T(1,128)S(1)}, u32[]{:S(2)}, u32[]{:S(2)}) async-start(f32[8,1,192]{2,1,0:T(1,128)} %broadcast_in_dim.4), calls=%async_computation | async-start | bytes 16384 | tf_op jit(solution)/shard_map/all_to_all | solution.py:93
  18.1 4.2 %all-to-all-done = f32[8,1,192]{2,1,0:T(1,128)S(1)} async-done(((f32[8,1,192]{2,1,0:T(1,128)}), f32[8,1,192]{2,1,0:T(1,128)S(1)}, u32[]{:S(2)}, u32[]{:S(2)}) %all-to-all-start) | async-done | bytes 6176 | tf_op jit(solution)/shard_map/all_to_all | solution.py:93
  22.3 0.6 copy.27
  22.9 0.5 collective-permute-start.9
  23.5 4.6 %collective-permute-done.2.refs_3_ = bf16[96,2304]{1,0:T(8,128)(2,1)} collective-permute-done((bf16[96,2304]{1,0:T(8,128)(2,1)S(1)}, bf16[96,2304]{1,0:T(8,128)(2,1)}, u32[]{:S(2)}, u32[]{:S(2)}) %collective-permute-start.2) | collective-permute-done | bytes 442400 | tf_op jit(solution)/shard_map/ppermute | solution.py:53
  28.1 1.0 %copy-done.1 = bf16[128,1536]{1,0:T(8,128)(2,1)S(1)} copy-done((bf16[128,1536]{1,0:T(8,128)(2,1)S(1)}, bf16[128,1536]{1,0:T(8,128)(2,1)}, u32[]{:S(2)}) %copy-start.1) | copy-done | bytes 393240
  29.1 0.7 copy-done.4
  29.7 1.8 %normalize.1.normed_hbm.refs_12_ = bf16[384,1536]{1,0:T(8,128)(2,1)} custom-call(bf16[256,1536]{1,0:T(8,128)(2,1)S(1)} %bitcast.36, bf16[128,1536]{1,0:T(8,128)(2,1)S(1)} %copy-done.1, f32[8,192]{1,0:T(8,128)S(1)} %copy-done.4, f32[1,768]{1,0:T(1,128)S(1)} %get-tuple-element.52.cos_ref, f32[1,768]{1,0:T(1,128)S(1)} %get-tuple-element.51.sin_ref), custom_call_target="tpu_custom_call" | custom-call | flops 1000000000 | bytes 1 | tf_op jit(solution)/shard_map/normalize/pallas_call | solution.py:258
  31.5 1.3 %collective-permute-start.10 = (bf16[384,1536]{1,0:T(8,128)(2,1)}, bf16[384,1536]{1,0:T(8,128)(2,1)}, u32[]{:S(2)}, u32[]{:S(2)}) collective-permute-start(bf16[384,1536]{1,0:T(8,128)(2,1)} %normalize.1.normed_hbm.refs_12_), channel_id=1, source_target_pairs={{0,16},{1,17},{2,18},{3,19},{4,20},{5,21},{6,22},{7,23}} | collective-permute-start | bytes 3538952 | tf_op jit(solution)/shard_map/ppermute | solution.py:479
  32.8 1.7 %collective-permute-start.11 = (bf16[384,1536]{1,0:T(8,128)(2,1)}, bf16[384,1536]{1,0:T(8,128)(2,1)}, u32[]{:S(2)}, u32[]{:S(2)}) collective-permute-start(bf16[384,1536]{1,0:T(8,128)(2,1)} %normalize.1.normed_hbm.refs_12_), channel_id=1, source_target_pairs={{0,8},{1,9},{2,10},{3,11},{4,12},{5,13},{6,14},{7,15}} | collective-permute-start | bytes 3538952 | tf_op jit(solution)/shard_map/ppermute | solution.py:479
  34.5 1.5 %collective-permute-start.3 = (bf16[96,2304]{1,0:T(8,128)(2,1)}, bf16[96,2304]{1,0:T(8,128)(2,1)}, u32[]{:S(2)}, u32[]{:S(2)}) collective-permute-start(bf16[96,2304]{1,0:T(8,128)(2,1)} %get-tuple-element.34.refs_0_), channel_id=1, source_target_pairs={{0,1},{1,0},{2,3},{3,2},{4,5},{5,4},{6,7},{7,6},{8,9},{9,8},{10,11... | collective-permute-start | bytes 1327112 | tf_op jit(solution)/shard_map/ppermute | solution.py:53
  36.0 0.5 collective-permute-start.4
  36.5 8.6 %collective-permute-done.3.refs_0_ = bf16[96,2304]{1,0:T(8,128)(2,1)} collective-permute-done((bf16[96,2304]{1,0:T(8,128)(2,1)}, bf16[96,2304]{1,0:T(8,128)(2,1)}, u32[]{:S(2)}, u32[]{:S(2)}) %collective-permute-start.3) | collective-permute-done | bytes 442400 | tf_op jit(solution)/shard_map/ppermute | solution.py:53
  45.1 1.2 %collective-permute-done.4.refs_1_ = bf16[96,2304]{1,0:T(8,128)(2,1)} collective-permute-done((bf16[96,2304]{1,0:T(8,128)(2,1)}, bf16[96,2304]{1,0:T(8,128)(2,1)}, u32[]{:S(2)}, u32[]{:S(2)}) %collective-permute-start.4) | collective-permute-done | bytes 442400 | tf_op jit(solution)/shard_map/ppermute | solution.py:53
  46.4 0.8 collective-permute-done.5.refs_2_
  47.1 1.2 %collective-permute-done.6.refs_3_ = bf16[96,2304]{1,0:T(8,128)(2,1)S(1)} collective-permute-done((bf16[96,2304]{1,0:T(8,128)(2,1)}, bf16[96,2304]{1,0:T(8,128)(2,1)S(1)}, u32[]{:S(2)}, u32[]{:S(2)}) %collective-permute-start.6) | collective-permute-done | bytes 442400 | tf_op jit(solution)/shard_map/ppermute | solution.py:53
  48.4 1.6 %collective-permute-done.10.refs_7_ = bf16[384,1536]{1,0:T(8,128)(2,1)} collective-permute-done((bf16[384,1536]{1,0:T(8,128)(2,1)}, bf16[384,1536]{1,0:T(8,128)(2,1)}, u32[]{:S(2)}, u32[]{:S(2)}) %collective-permute-start.10) | collective-permute-done | bytes 1179680 | tf_op jit(solution)/shard_map/ppermute | solution.py:479
  50.0 1.4 %collective-permute-start.14 = (bf16[384,1536]{1,0:T(8,128)(2,1)}, bf16[384,1536]{1,0:T(8,128)(2,1)S(1)}, u32[]{:S(2)}, u32[]{:S(2)}) collective-permute-start(bf16[384,1536]{1,0:T(8,128)(2,1)} %get-tuple-element.43.refs_13_), channel_id=1, source_target_pairs={{16,24},{17,25},{18,26},{19,27},{20,28},{21,29},{22,30},{23,31}} | collective-permute-start | bytes 3538952 | tf_op jit(solution)/shard_map/ppermute | solution.py:492
  51.4 0.5 collective-permute-start.13
  52.9 1.5 %collective-permute-start.15 = (bf16[96,1536]{1,0:T(8,128)(2,1)}, bf16[96,1536]{1,0:T(8,128)(2,1)S(1)}, u32[]{:S(2)}, u32[]{:S(2)}) collective-permute-start(bf16[96,1536]{1,0:T(8,128)(2,1)} %get-tuple-element.48.refs_2_), channel_id=1, source_target_pairs={{0,1},{1,0},{2,3},{3,2},{4,5},{5,4},{6,7},{7,6},{8,9},{9,8},{10,11... | collective-permute-start | bytes 884744 | tf_op jit(solution)/shard_map/ppermute | solution.py:53
  55.2 10.2 %project_attend_tail.1 = (bf16[256,768]{1,0:T(8,128)(2,1)S(1)}, bf16[768,1536]{1,0:T(8,128)(2,1)S(1)}, bf16[128,768]{1,0:T(8,128)(2,1)S(1)}) custom-call(s32[12]{0:T(128)S(1)} %stack.119.places_ref, s32[3,3]{1,0:T(4,128)S(1)} %copy-done.8, bf16[384,1536]{1,0:T(8,128)(2,1)} %normalize.1.normed_hbm.refs_12_, bf16[96,2304]{1,0:T(8,128)(2,1)} %get-tuple-element.34.refs_0_, ...), custom_call_target="tpu_custom_call" | custom-call | flops 10000000000 | bytes 1 | tf_op jit(solution)/shard_map/project_attend_tail/pallas_call | solution.py:381
  65.5 3.6 %collective-permute-start.16 = (bf16[128,768]{1,0:T(8,128)(2,1)S(1)}, bf16[128,768]{1,0:T(8,128)(2,1)S(1)}, u32[]{:S(2)}, u32[]{:S(2)}) collective-permute-start(bf16[128,768]{1,0:T(8,128)(2,1)S(1)} %get-tuple-element.49), channel_id=1, source_target_pairs={{0,1},{1,2},{2,3},{3,4},{4,5},{5,6},{6,7},{8,9},{9,10},{10,11},{11... | collective-permute-start | bytes 589832 | tf_op jit(solution)/shard_map/ppermute | solution.py:59
  69.2 3.9 %attend_main.1.attended_ref = f32[256,768]{1,0:T(8,128)S(1)} custom-call(s32[1]{0:T(128)} %bitcast.11.places_ref, s32[3,3]{1,0:T(4,128)S(1)} %copy-done.8, bf16[256,768]{1,0:T(8,128)(2,1)S(1)} %get-tuple-element.45.query_ref, bf16[768,1536]{1,0:T(8,128)(2,1)S(1)} %get-tuple-element.46.keyval_ref), custom_call_target="tpu_custom_call" | custom-call | flops 4000000000 | bytes 1 | tf_op jit(solution)/shard_map/attend_main/pallas_call | solution.py:419
  73.2 1.9 %collective-permute-done.16.received_ref = bf16[128,768]{1,0:T(8,128)(2,1)S(1)} collective-permute-done((bf16[128,768]{1,0:T(8,128)(2,1)S(1)}, bf16[128,768]{1,0:T(8,128)(2,1)S(1)}, u32[]{:S(2)}, u32[]{:S(2)}) %collective-permute-start.16) | collective-permute-done | bytes 196640 | tf_op jit(solution)/shard_map/ppermute | solution.py:59
  75.1 2.4 %blend_and_step.1 = bf16[256,1536]{1,0:T(8,128)(2,1)} custom-call(s32[6]{0:T(128)S(1)} %stack.99.places_ref, f32[4]{0:T(128)S(1)} %pad_maximum_fusion.coef_ref, f32[256,768]{1,0:T(8,128)S(1)} %attend_main.1.attended_ref, bf16[128,768]{1,0:T(8,128)(2,1)S(1)} %collective-permute-done.16.received_ref, bf16[256,1536]{1,0:T(8,128)(2,1)S(1)} %bitcast.37, ...), custom_call_target="tpu_custom_call" | custom-call | flops 3000000000 | bytes 1 | tf_op jit(solution)/shard_map/blend_and_step/pallas_call | solution.py:453
  (50 shorter events, 1.6 us)
Async XLA Ops:
  5.3 22.7 %copy-start.5 = (bf16[1,256,1536]{2,1,0:T(8,128)(2,1)S(1)}, bf16[1,256,1536]{2,1,0:T(8,128)(2,1)}, u32[]{:S(2)}) copy-start(bf16[1,256,1536]{2,1,0:T(8,128)(2,1)} %param.9) | copy-start | bytes 2359300
  5.3 18.1 %collective-permute-start.1 = (bf16[96,2304]{1,0:T(8,128)(2,1)S(1)}, bf16[96,2304]{1,0:T(8,128)(2,1)}, u32[]{:S(2)}, u32[]{:S(2)}) collective-permute-start(bf16[96,2304]{1,0:T(8,128)(2,1)S(1)} %get-tuple-element.30), channel_id=1, source_target_pairs={{0,16},{8,24},{16,0},{24,8},{1,17},{9,25},{17,1},{25,9},{2,18},{10... | collective-permute-start | bytes 1327112 | tf_op jit(solution)/shard_map/ppermute | solution.py:53
  5.9 22.1 %collective-permute-start.2 = (bf16[96,2304]{1,0:T(8,128)(2,1)S(1)}, bf16[96,2304]{1,0:T(8,128)(2,1)}, u32[]{:S(2)}, u32[]{:S(2)}) collective-permute-start(bf16[96,2304]{1,0:T(8,128)(2,1)S(1)} %get-tuple-element.31), channel_id=1, source_target_pairs={{0,16},{8,24},{16,0},{24,8},{1,17},{9,25},{17,1},{25,9},{2,18},{10... | collective-permute-start | bytes 1327112 | tf_op jit(solution)/shard_map/ppermute | solution.py:53
  7.4 15.5 %collective-permute-start = (bf16[128,1536]{1,0:T(8,128)(2,1)S(1)}, bf16[128,1536]{1,0:T(8,128)(2,1)S(1)}, u32[]{:S(2)}, u32[]{:S(2)}) collective-permute-start(bf16[128,1536]{1,0:T(8,128)(2,1)S(1)} %get-tuple-element.28), channel_id=1, source_target_pairs={{1,0},{2,1},{3,2},{4,3},{5,4},{6,5},{7,6},{9,8},{10,9},{11,10},{12... | collective-permute-start | bytes 1179656 | tf_op jit(solution)/shard_map/ppermute | solution.py:59
  10.7 25.3 %collective-permute-start.7 = (bf16[384,768]{1,0:T(8,128)(2,1)}, bf16[384,768]{1,0:T(8,128)(2,1)}, u32[]{:S(2)}, u32[]{:S(2)}) collective-permute-start(bf16[384,768]{1,0:T(8,128)(2,1)} %refs_8_.1), channel_id=1, source_target_pairs={{0,8},{8,0},{16,24},{24,16},{1,9},{9,1},{17,25},{25,17},{2,10},{10... | collective-permute-start | bytes 1769480 | tf_op jit(solution)/shard_map/ppermute | solution.py:53
  10.8 37.5 %collective-permute-start.8 = (bf16[384,1536]{1,0:T(8,128)(2,1)}, bf16[384,1536]{1,0:T(8,128)(2,1)}, u32[]{:S(2)}, u32[]{:S(2)}) collective-permute-start(bf16[384,1536]{1,0:T(8,128)(2,1)} %refs_10_.1), channel_id=1, source_target_pairs={{0,8},{8,0},{16,24},{24,16},{1,9},{9,1},{17,25},{25,17},{2,10},{10... | collective-permute-start | bytes 3538952 | tf_op jit(solution)/shard_map/ppermute | solution.py:53
  11.9 10.4 %all-to-all-start = ((f32[8,1,192]{2,1,0:T(1,128)}), f32[8,1,192]{2,1,0:T(1,128)S(1)}, u32[]{:S(2)}, u32[]{:S(2)}) async-start(f32[8,1,192]{2,1,0:T(1,128)} %broadcast_in_dim.4), calls=%async_computation | async-start | bytes 16384 | tf_op jit(solution)/shard_map/all_to_all | solution.py:93
  22.9 5.1 %copy-start = (bf16[128,1536]{1,0:T(8,128)(2,1)}, bf16[128,1536]{1,0:T(8,128)(2,1)S(1)}, u32[]{:S(2)}) copy-start(bf16[128,1536]{1,0:T(8,128)(2,1)S(1)} %collective-permute-done.refs_0_) | copy-start | bytes 1179652
  22.9 11.6 %collective-permute-start.9 = (bf16[96,1536]{1,0:T(8,128)(2,1)S(1)}, bf16[96,1536]{1,0:T(8,128)(2,1)S(1)}, u32[]{:S(2)}, u32[]{:S(2)}) collective-permute-start(bf16[96,1536]{1,0:T(8,128)(2,1)S(1)} %get-tuple-element.36), channel_id=1, source_target_pairs={{0,16},{8,24},{16,0},{24,8},{1,17},{9,25},{17,1},{25,9},{2,18},{10... | collective-permute-start | bytes 884744 | tf_op jit(solution)/shard_map/ppermute | solution.py:53
  28.1 1.0 %copy-start.1 = (bf16[128,1536]{1,0:T(8,128)(2,1)S(1)}, bf16[128,1536]{1,0:T(8,128)(2,1)}, u32[]{:S(2)}) copy-start(bf16[128,1536]{1,0:T(8,128)(2,1)} %get-tuple-element.32.halo_ref) | copy-start | bytes 1179652
  29.0 0.7 copy-start.4
  31.5 18.4 %collective-permute-start.10 = (bf16[384,1536]{1,0:T(8,128)(2,1)}, bf16[384,1536]{1,0:T(8,128)(2,1)}, u32[]{:S(2)}, u32[]{:S(2)}) collective-permute-start(bf16[384,1536]{1,0:T(8,128)(2,1)} %normalize.1.normed_hbm.refs_12_), channel_id=1, source_target_pairs={{0,16},{1,17},{2,18},{3,19},{4,20},{5,21},{6,22},{7,23}} | collective-permute-start | bytes 3538952 | tf_op jit(solution)/shard_map/ppermute | solution.py:479
  32.8 17.1 %collective-permute-start.11 = (bf16[384,1536]{1,0:T(8,128)(2,1)}, bf16[384,1536]{1,0:T(8,128)(2,1)}, u32[]{:S(2)}, u32[]{:S(2)}) collective-permute-start(bf16[384,1536]{1,0:T(8,128)(2,1)} %normalize.1.normed_hbm.refs_12_), channel_id=1, source_target_pairs={{0,8},{1,9},{2,10},{3,11},{4,12},{5,13},{6,14},{7,15}} | collective-permute-start | bytes 3538952 | tf_op jit(solution)/shard_map/ppermute | solution.py:479
  34.5 15.4 %copy-start.2 = (bf16[96,1536]{1,0:T(8,128)(2,1)}, bf16[96,1536]{1,0:T(8,128)(2,1)S(1)}, u32[]{:S(2)}) copy-start(bf16[96,1536]{1,0:T(8,128)(2,1)S(1)} %collective-permute-done.9.refs_6_) | copy-start | bytes 884740
  34.5 10.6 %collective-permute-start.3 = (bf16[96,2304]{1,0:T(8,128)(2,1)}, bf16[96,2304]{1,0:T(8,128)(2,1)}, u32[]{:S(2)}, u32[]{:S(2)}) collective-permute-start(bf16[96,2304]{1,0:T(8,128)(2,1)} %get-tuple-element.34.refs_0_), channel_id=1, source_target_pairs={{0,1},{1,0},{2,3},{3,2},{4,5},{5,4},{6,7},{7,6},{8,9},{9,8},{10,11... | collective-permute-start | bytes 1327112 | tf_op jit(solution)/shard_map/ppermute | solution.py:53
  36.0 10.3 %collective-permute-start.4 = (bf16[96,2304]{1,0:T(8,128)(2,1)}, bf16[96,2304]{1,0:T(8,128)(2,1)}, u32[]{:S(2)}, u32[]{:S(2)}) collective-permute-start(bf16[96,2304]{1,0:T(8,128)(2,1)} %get-tuple-element.34.refs_0_), channel_id=1, source_target_pairs={{0,2},{1,3},{2,0},{3,1},{4,6},{5,7},{6,4},{7,5},{8,10},{9,11},{10,... | collective-permute-start | bytes 1327112 | tf_op jit(solution)/shard_map/ppermute | solution.py:53
  45.1 2.0 %collective-permute-start.5 = (bf16[96,2304]{1,0:T(8,128)(2,1)}, bf16[96,2304]{1,0:T(8,128)(2,1)S(1)}, u32[]{:S(2)}, u32[]{:S(2)}) collective-permute-start(bf16[96,2304]{1,0:T(8,128)(2,1)} %get-tuple-element.34.refs_0_), channel_id=1, source_target_pairs={{0,8},{8,0},{16,24},{24,16},{1,9},{9,1},{17,25},{25,17},{2,10},{10... | collective-permute-start | bytes 1327112 | tf_op jit(solution)/shard_map/ppermute | solution.py:53
  46.4 8.9 %copy-start.8 = (s32[3,3]{1,0:T(4,128)S(1)}, s32[3,3]{1,0:T(4,128)}, u32[]{:S(2)}) copy-start(s32[3,3]{1,0:T(4,128)} %table_ref.3) | copy-start | bytes 112
  46.4 2.0 %collective-permute-start.6 = (bf16[96,2304]{1,0:T(8,128)(2,1)}, bf16[96,2304]{1,0:T(8,128)(2,1)S(1)}, u32[]{:S(2)}, u32[]{:S(2)}) collective-permute-start(bf16[96,2304]{1,0:T(8,128)(2,1)} %get-tuple-element.35.refs_3_), channel_id=1, source_target_pairs={{0,8},{8,0},{16,24},{24,16},{1,9},{9,1},{17,25},{25,17},{2,10},{10... | collective-permute-start | bytes 1327112 | tf_op jit(solution)/shard_map/ppermute | solution.py:53
  47.1 2.9 %copy-start.10 = (bf16[96,2304]{1,0:T(8,128)(2,1)}, bf16[96,2304]{1,0:T(8,128)(2,1)S(1)}, u32[]{:S(2)}) copy-start(bf16[96,2304]{1,0:T(8,128)(2,1)S(1)} %collective-permute-done.5.refs_2_) | copy-start | bytes 1327108
  48.4 1.6 %copy-start.11 = (bf16[96,2304]{1,0:T(8,128)(2,1)}, bf16[96,2304]{1,0:T(8,128)(2,1)S(1)}, u32[]{:S(2)}) copy-start(bf16[96,2304]{1,0:T(8,128)(2,1)S(1)} %collective-permute-done.6.refs_3_) | copy-start | bytes 1327108
  50.0 5.2 %collective-permute-start.14 = (bf16[384,1536]{1,0:T(8,128)(2,1)}, bf16[384,1536]{1,0:T(8,128)(2,1)S(1)}, u32[]{:S(2)}, u32[]{:S(2)}) collective-permute-start(bf16[384,1536]{1,0:T(8,128)(2,1)} %get-tuple-element.43.refs_13_), channel_id=1, source_target_pairs={{16,24},{17,25},{18,26},{19,27},{20,28},{21,29},{22,30},{23,31}} | collective-permute-start | bytes 3538952 | tf_op jit(solution)/shard_map/ppermute | solution.py:492
  51.4 3.2 %collective-permute-start.12 = (bf16[96,2304]{1,0:T(8,128)(2,1)}, bf16[96,2304]{1,0:T(8,128)(2,1)S(1)}, u32[]{:S(2)}, u32[]{:S(2)}) collective-permute-start(bf16[96,2304]{1,0:T(8,128)(2,1)} %get-tuple-element.37.refs_1_), channel_id=1, source_target_pairs={{0,8},{8,0},{16,24},{24,16},{1,9},{9,1},{17,25},{25,17},{2,10},{10... | collective-permute-start | bytes 1327112 | tf_op jit(solution)/shard_map/ppermute | solution.py:53
  51.4 3.8 %collective-permute-start.13 = (bf16[96,2304]{1,0:T(8,128)(2,1)}, bf16[96,2304]{1,0:T(8,128)(2,1)S(1)}, u32[]{:S(2)}, u32[]{:S(2)}) collective-permute-start(bf16[96,2304]{1,0:T(8,128)(2,1)} %get-tuple-element.38.refs_2_), channel_id=1, source_target_pairs={{0,8},{8,0},{16,24},{24,16},{1,9},{9,1},{17,25},{25,17},{2,10},{10... | collective-permute-start | bytes 1327112 | tf_op jit(solution)/shard_map/ppermute | solution.py:53
  51.9 21.2 %collective-permute-start.17 = (bf16[192,1536]{1,0:T(8,128)(2,1)}, bf16[192,1536]{1,0:T(8,128)(2,1)S(1)}, u32[]{:S(2)}, u32[]{:S(2)}) collective-permute-start(bf16[192,1536]{1,0:T(8,128)(2,1)} %refs_0_.1), channel_id=1, source_target_pairs={{0,8},{8,0},{16,24},{24,16},{1,9},{9,1},{17,25},{25,17},{2,10},{10... | collective-permute-start | bytes 1769480 | tf_op jit(solution)/shard_map/ppermute | solution.py:53
  52.9 12.5 %collective-permute-start.15 = (bf16[96,1536]{1,0:T(8,128)(2,1)}, bf16[96,1536]{1,0:T(8,128)(2,1)S(1)}, u32[]{:S(2)}, u32[]{:S(2)}) collective-permute-start(bf16[96,1536]{1,0:T(8,128)(2,1)} %get-tuple-element.48.refs_2_), channel_id=1, source_target_pairs={{0,1},{1,0},{2,3},{3,2},{4,5},{5,4},{6,7},{7,6},{8,9},{9,8},{10,11... | collective-permute-start | bytes 884744 | tf_op jit(solution)/shard_map/ppermute | solution.py:53
  54.6 18.6 %collective-permute-start.18 = (bf16[96,1536]{1,0:T(8,128)(2,1)}, bf16[96,1536]{1,0:T(8,128)(2,1)S(1)}, u32[]{:S(2)}, u32[]{:S(2)}) collective-permute-start(bf16[96,1536]{1,0:T(8,128)(2,1)} %get-tuple-element.48.refs_2_), channel_id=1, source_target_pairs={{0,8},{8,0},{16,24},{24,16},{1,9},{9,1},{17,25},{25,17},{2,10},{10... | collective-permute-start | bytes 884744 | tf_op jit(solution)/shard_map/ppermute | solution.py:53
  65.5 9.6 %collective-permute-start.16 = (bf16[128,768]{1,0:T(8,128)(2,1)S(1)}, bf16[128,768]{1,0:T(8,128)(2,1)S(1)}, u32[]{:S(2)}, u32[]{:S(2)}) collective-permute-start(bf16[128,768]{1,0:T(8,128)(2,1)S(1)} %get-tuple-element.49), channel_id=1, source_target_pairs={{0,1},{1,2},{2,3},{3,4},{4,5},{5,6},{6,7},{8,9},{9,10},{10,11},{11... | collective-permute-start | bytes 589832 | tf_op jit(solution)/shard_map/ppermute | solution.py:59
  69.1 6.0 %collective-permute-start.19 = (bf16[96,1536]{1,0:T(8,128)(2,1)S(1)}, bf16[96,1536]{1,0:T(8,128)(2,1)S(1)}, u32[]{:S(2)}, u32[]{:S(2)}) collective-permute-start(bf16[96,1536]{1,0:T(8,128)(2,1)S(1)} %get-tuple-element.50.refs_3_), channel_id=1, source_target_pairs={{0,8},{8,0},{16,24},{24,16},{1,9},{9,1},{17,25},{25,17},{2,10},{10... | collective-permute-start | bytes 884744 | tf_op jit(solution)/shard_map/ppermute | solution.py:53
  69.2 5.9 %copy-start.3 = (bf16[96,1536]{1,0:T(8,128)(2,1)S(1)}, bf16[96,1536]{1,0:T(8,128)(2,1)}, u32[]{:S(2)}) copy-start(bf16[96,1536]{1,0:T(8,128)(2,1)} %get-tuple-element.48.refs_2_) | copy-start | bytes 884740
  69.2 5.9 %copy-start.6 = (bf16[1,256,1536]{2,1,0:T(8,128)(2,1)S(1)}, bf16[1,256,1536]{2,1,0:T(8,128)(2,1)}, u32[]{:S(2)}) copy-start(bf16[1,256,1536]{2,1,0:T(8,128)(2,1)} %param.10) | copy-start | bytes 2359300
  69.2 5.9 %copy-start.7 = (bf16[192,1536]{1,0:T(8,128)(2,1)S(1)}, bf16[192,1536]{1,0:T(8,128)(2,1)}, u32[]{:S(2)}) copy-start(bf16[192,1536]{1,0:T(8,128)(2,1)} %refs_0_.1) | copy-start | bytes 1769476
  (1 other events, 0.7 us)

commit v4 on v3

--- a/solution.py
+++ b/solution.py
@@ -96,33 +96,12 @@
     return arrived
 
 
-def first_kernel(
-    places_ref, ids_ref, table_ref, query_ref, keyval_ref, out_weights_ref, latent_ref, *refs
-):
-    pooled_ref, halo_ref, out_cut_ref, *cut_refs, columns, sems = refs
-    head_width = query_ref.shape[1]
-    copies = [
-        pltpu.make_async_copy(table_ref, columns, sems.at[0]),
-        pltpu.make_async_copy(latent_ref.at[: halo_ref.shape[0], :], halo_ref, sems.at[1]),
-    ]
-    out_rows = out_cut_ref.shape[0]
-    at = pl.ds(aligned(places_ref[0] * out_rows, 16), out_rows)
-    copies.append(pltpu.make_async_copy(out_weights_ref.at[at, :], out_cut_ref, sems.at[2]))
-    for k, target in enumerate(cut_refs):
-        rows = target.shape[0]
-        at = pl.ds(aligned(places_ref[1 + k] * rows, 16), rows)
-        copies += [
-            pltpu.make_async_copy(
-                query_ref.at[at, :], target.at[:, :head_width], sems.at[3 + 2 * k]
-            ),
-            pltpu.make_async_copy(
-                keyval_ref.at[at, :], target.at[:, head_width:], sems.at[4 + 2 * k]
-            ),
-        ]
-    for copy in copies:
-        copy.start()
+def pool_kernel(ids_ref, table_ref, after_ref, pooled_ref, columns, sem):
+    del after_ref
+    whole = pltpu.make_async_copy(table_ref, columns, sem)
+    whole.start()
     lane = lax.broadcasted_iota(jnp.int32, (1, LANES), 1)
-    copies[0].wait()
+    whole.wait()
 
     def body(j, total):
         token = ids_ref[0, j]
@@ -140,35 +119,69 @@
         precision=lax.Precision.HIGHEST,
         preferred_element_type=F32,
     )
-    for copy in copies[1:]:
+
+
+def pool(prompt_ids, prompt_table, after):
+    table_columns = prompt_table.T
+    return pl.pallas_call(
+        pool_kernel,
+        out_shape=jax.ShapeDtypeStruct((8, table_columns.shape[0]), F32),
+        in_specs=[smem(), hbm(), anywhere()],
+        out_specs=vmem(),
+        scratch_shapes=[pltpu.VMEM(table_columns.shape, BF16), pltpu.SemaphoreType.DMA],
+        compiler_params=params(),
+        cost_estimate=cost(1),
+        name="pool_prompt",
+    )(prompt_ids, in_hbm(table_columns), after)
+
+
+def first_kernel(
+    places_ref, query_ref, keyval_ref, out_weights_ref, latent_ref, halo_ref, out_cut_ref, *refs
+):
+    *cut_refs, sems = refs
+    head_width = query_ref.shape[1]
+    copies = [
+        pltpu.make_async_copy(latent_ref.at[: halo_ref.shape[0], :], halo_ref, sems.at[0]),
+    ]
+    out_rows = out_cut_ref.shape[0]
+    at = pl.ds(aligned(places_ref[0] * out_rows, 16), out_rows)
+    copies.append(pltpu.make_async_copy(out_weights_ref.at[at, :], out_cut_ref, sems.at[1]))
+    for k, target in enumerate(cut_refs):
+        rows = target.shape[0]
+        at = pl.ds(aligned(places_ref[1 + k] * rows, 16), rows)
+        copies += [
+            pltpu.make_async_copy(
+                query_ref.at[at, :], target.at[:, :head_width], sems.at[2 + 2 * k]
+            ),
+            pltpu.make_async_copy(
+                keyval_ref.at[at, :], target.at[:, head_width:], sems.at[3 + 2 * k]
+            ),
+        ]
+    for copy in copies:
+        copy.start()
+    for copy in copies:
         copy.wait()
 
 
-def first_rows(side, places, prompt_ids, prompt_table, w_query, w_keyval, w_out, latent):
-    table_columns = prompt_table.T
+def first_rows(side, places, w_query, w_keyval, w_out, latent):
     quarter = w_query.shape[0] // 4
     columns = w_query.shape[1] + w_keyval.shape[1]
     return pl.pallas_call(
         first_kernel,
         out_shape=[
-            jax.ShapeDtypeStruct((8, table_columns.shape[0]), F32),
             jax.ShapeDtypeStruct((SEAM, latent.shape[1]), BF16),
             jax.ShapeDtypeStruct((w_out.shape[0] // 2, w_out.shape[1]), BF16),
         ]
         + [jax.ShapeDtypeStruct((quarter, columns), BF16)] * len(places),
-        in_specs=[smem(), smem()] + [hbm()] * 5,
-        out_specs=[vmem()] * (3 + len(places)),
-        scratch_shapes=[
-            pltpu.VMEM(table_columns.shape, BF16),
-            pltpu.SemaphoreType.DMA((3 + 2 * len(places),)),
-        ],
+        in_specs=[smem()] + [hbm()] * 4,
+        out_specs=[vmem()] * (2 + len(places)),
+        scratch_shapes=[pltpu.SemaphoreType.DMA((2 + 2 * len(places),))],
         compiler_params=params(),
-        cost_estimate=cost(4 * MICROSECOND),
-        name="pool_and_first_rows",
+        cost_estimate=cost(1),
+        name="first_rows",
     )(
         numbers(side, *places),
-        prompt_ids,
-        *[in_hbm(value) for value in (table_columns, w_query, w_keyval, w_out, latent)],
+        *[in_hbm(value) for value in (w_query, w_keyval, w_out, latent)],
     )
 
 
@@ -258,7 +271,7 @@
     return pl.pallas_call(
         normalize_kernel,
         out_shape=pltpu.HBM(shape, BF16),
-        in_specs=[anywhere()] * 3 + [vmem()] * 2,
+        in_specs=[hbm()] * 3 + [vmem()] * 2,
         out_specs=hbm(),
         scratch_shapes=[
             pltpu.VMEM(shape, BF16),
@@ -269,7 +282,7 @@
         compiler_params=params(),
         cost_estimate=cost(MICROSECOND),
         name="normalize",
-    )(latent, halo, rows, *waves)
+    )(in_hbm(latent), in_hbm(halo), in_hbm(rows), *waves)
 
 
 def attend_rows(query, keyval_ref, bias, own_block, pair):
@@ -506,16 +519,15 @@
     corner = tm_place & 3
 
     side = tm_place & 1
-    pooled, halo_rows, out_cut, *cuts = first_rows(
+    halo_rows, out_cut, *cuts = first_rows(
         side if routed else 0,
         (corner, corner ^ 3) if routed else (),
-        prompt_ids,
-        prompt_table,
         w_query,
         w_keyval,
         w_out,
         latent,
     )
+    pooled = pool(prompt_ids, prompt_table, halo_rows)
     halo = shifted(halo_rows, "tm", -1)
     pooled = whole_rows(pooled[:1])
     if routed:

time: 77.8 us -> 76.1 us (0.978)
  Pallas kernels: 22.9 us -> 25.6 us
  waiting for transfers between devices: 24.6 us -> 22.4 us
  starting transfers between devices: 24.4 us -> 23 us
  local copies, waits for them, and re-layouts: 3.74 us -> 2.96 us
    ppermute x15, waiting for transfers between devices: 16.9 us -> 13.5 us  [swapped(): return lax.ppermute(block, axis, route)]
    pallas_call x1 -> x2, Pallas kernels: 4.59 us -> 6.46 us  [the longest x1 4.52 us: pool(): pl.pallas_call(pool_kernel, out_shape=jax.ShapeDtypeStruct((8, table_colu...]
    pallas_call x1, Pallas kernels: 1.79 us -> 2.83 us  [normalized(): pl.pallas_call(normalize_kernel, out_shape=pltpu.HBM(shape, BF16), in_spe...]
    ppermute x2, starting transfers between devices: 6.91 us -> 5.96 us  [shifted(): return lax.ppermute(block, axis, route)]
    ppermute x2, waiting for transfers between devices: 1.92 us -> 2.83 us  [shifted(): return lax.ppermute(block, axis, route)]
    unnamed x25, local copies, waits for them, and re-layouts: 2.96 us -> 2.18 us
  transfers between devices with their start and end apart: 21 -> 21, of which waited for: 10 -> 9; matrix products, arithmetic and copies ran while one was open for 2% -> 2% of each run, Pallas kernels for 21% -> 28%
where the time goes in v4:
time: 76.1 us; the launch traced here: 75.8 us
  Pallas kernels  25.6 us (34%)
  starting transfers between devices  23 us (30%)
  waiting for transfers between devices  22.4 us (29%)
  local copies, waits for them, and re-layouts  2.96 us (4%)
  between operations  1.51 us (2%)
    ppermute x15, waiting for transfers between devices, swapped(): return lax.ppermute(block, axis, route)  13.5 us
    pallas_call x1, Pallas kernels, project(): pl.pallas_call(functools.partial(project_kernel, len(wide), len(queries),...  10.2 us
    ppermute x15, starting transfers between devices, swapped(): return lax.ppermute(block, axis, route)  7.33 us
    ppermute x2, starting transfers between devices, shifted(): return lax.ppermute(block, axis, route)  5.96 us
    all_to_all x1, starting transfers between devices, whole_rows(): arrived = lax.all_to_all(sent, 'tm', 0, 0, tiled=True)  5.4 us
    pallas_call x1, Pallas kernels, pool(): pl.pallas_call(pool_kernel, out_shape=jax.ShapeDtypeStruct((8, table_colu...  4.52 us
    all_to_all x1, waiting for transfers between devices, whole_rows(): arrived = lax.all_to_all(sent, 'tm', 0, 0, tiled=True)  4.24 us
    pallas_call x1, Pallas kernels, attend_main(): pl.pallas_call(main_kernel, out_shape=jax.ShapeDtypeStruct((rows, width),...  3.67 us
  transfers between devices with their start and end apart: 21, of which 9 were waited for; matrix products, arithmetic and copies ran while one was open for 2% of the time, Pallas kernels for 28%

profile of v4, /device:TPU:10, one launch (start us, length us, event | category | flops | bytes accessed | tf_op | source)
XLA Modules:
  0.0 75.8 jit_solution(12844116701593880419)
XLA Ops:
  0.1 1.9 %first_rows.1 = (bf16[128,1536]{1,0:T(8,128)(2,1)S(1)}, bf16[96,1536]{1,0:T(8,128)(2,1)S(1)}, bf16[96,2304]{1,0:T(8,128)(2,1)S(1)}, bf16[96,2304]{1,0:T(8,128)(2,1)S(1)}) custom-call(s32[3]{0:T(128)S(1)} %pad_add_fusion.places_ref, bf16[384,768]{1,0:T(8,128)(2,1)} %refs_8_.1, bf16[384,1536]{1,0:T(8,128)(2,1)} %refs_10_.1, bf16[192,1536]{1,0:T(8,128)(2,1)} %refs_0_.1, ...), custom_call_target="tpu_custom_call" | custom-call | flops 1 | bytes 1 | tf_op jit(solution)/shard_map/first_rows/pallas_call | solution.py:169
  2.0 0.6 collective-permute-start.1
  2.6 1.5 %collective-permute-start.2 = (bf16[96,2304]{1,0:T(8,128)(2,1)S(1)}, bf16[96,2304]{1,0:T(8,128)(2,1)}, u32[]{:S(2)}, u32[]{:S(2)}) collective-permute-start(bf16[96,2304]{1,0:T(8,128)(2,1)S(1)} %get-tuple-element.29), channel_id=1, source_target_pairs={{0,16},{8,24},{16,0},{24,8},{1,17},{9,25},{17,1},{25,9},{2,18},{10... | collective-permute-start | bytes 1327112 | tf_op jit(solution)/shard_map/ppermute | solution.py:53
  4.1 3.3 %collective-permute-start = (bf16[128,1536]{1,0:T(8,128)(2,1)S(1)}, bf16[128,1536]{1,0:T(8,128)(2,1)S(1)}, u32[]{:S(2)}, u32[]{:S(2)}) collective-permute-start(bf16[128,1536]{1,0:T(8,128)(2,1)S(1)} %get-tuple-element.27.after_ref), channel_id=1, source_target_pairs={{1,0},{2,1},{3,2},{4,3},{5,4},{6,5},{7,6},{9,8},{10,9},{11,10},{12... | collective-permute-start | bytes 1179656 | tf_op jit(solution)/shard_map/ppermute | solution.py:59
  7.5 0.5 collective-permute-start.8
  8.0 4.5 %pool_prompt.1 = f32[8,192]{1,0:T(8,128)S(1)} custom-call(s32[1,64]{1,0:T(1,128)S(1)} %copy-done.4, bf16[192,16384]{1,0:T(8,128)(2,1)} %bitcast.38, bf16[128,1536]{1,0:T(8,128)(2,1)S(1)} %get-tuple-element.27.after_ref), custom_call_target="tpu_custom_call" | custom-call | flops 1 | bytes 1 | tf_op jit(solution)/shard_map/pool_prompt/pallas_call | solution.py:126
  12.5 0.6 broadcast_in_dim.4
  13.2 5.4 %all-to-all-start = ((f32[8,1,192]{2,1,0:T(1,128)}), f32[8,1,192]{2,1,0:T(1,128)S(1)}, u32[]{:S(2)}, u32[]{:S(2)}) async-start(f32[8,1,192]{2,1,0:T(1,128)} %broadcast_in_dim.4), calls=%async_computation | async-start | bytes 16384 | tf_op jit(solution)/shard_map/all_to_all | solution.py:93
  19.3 4.2 %all-to-all-done = f32[8,1,192]{2,1,0:T(1,128)S(1)} async-done(((f32[8,1,192]{2,1,0:T(1,128)}), f32[8,1,192]{2,1,0:T(1,128)S(1)}, u32[]{:S(2)}, u32[]{:S(2)}) %all-to-all-start) | async-done | bytes 6176 | tf_op jit(solution)/shard_map/all_to_all | solution.py:93
  23.6 0.6 copy.27
  24.2 0.7 copy-done.11
  24.9 0.5 collective-permute-start.9
  25.5 0.8 %copy-done.9 = bf16[96,2304]{1,0:T(8,128)(2,1)} copy-done((bf16[96,2304]{1,0:T(8,128)(2,1)}, bf16[96,2304]{1,0:T(8,128)(2,1)S(1)}, u32[]{:S(2)}) %copy-start.9) | copy-done | bytes 442392
  26.3 2.8 %normalize.1.normed_hbm.refs_12_ = bf16[384,1536]{1,0:T(8,128)(2,1)} custom-call(bf16[256,1536]{1,0:T(8,128)(2,1)} %bitcast.35, bf16[128,1536]{1,0:T(8,128)(2,1)} %get-tuple-element.30.halo_ref, f32[8,192]{1,0:T(8,128)} %get-tuple-element.31.rows_ref, f32[1,768]{1,0:T(1,128)S(1)} %get-tuple-element.50.cos_ref, f32[1,768]{1,0:T(1,128)S(1)} %get-tuple-element.49.sin_ref), custom_call_target="tpu_custom_call" | custom-call | flops 1000000000 | bytes 1 | tf_op jit(solution)/shard_map/normalize/pallas_call | solution.py:271
  29.1 1.3 %collective-permute-start.10 = (bf16[384,1536]{1,0:T(8,128)(2,1)}, bf16[384,1536]{1,0:T(8,128)(2,1)}, u32[]{:S(2)}, u32[]{:S(2)}) collective-permute-start(bf16[384,1536]{1,0:T(8,128)(2,1)} %normalize.1.normed_hbm.refs_12_), channel_id=1, source_target_pairs={{0,16},{1,17},{2,18},{3,19},{4,20},{5,21},{6,22},{7,23}} | collective-permute-start | bytes 3538952 | tf_op jit(solution)/shard_map/ppermute | solution.py:492
  30.4 1.7 %collective-permute-start.11 = (bf16[384,1536]{1,0:T(8,128)(2,1)}, bf16[384,1536]{1,0:T(8,128)(2,1)}, u32[]{:S(2)}, u32[]{:S(2)}) collective-permute-start(bf16[384,1536]{1,0:T(8,128)(2,1)} %normalize.1.normed_hbm.refs_12_), channel_id=1, source_target_pairs={{0,8},{1,9},{2,10},{3,11},{4,12},{5,13},{6,14},{7,15}} | collective-permute-start | bytes 3538952 | tf_op jit(solution)/shard_map/ppermute | solution.py:492
  32.1 0.4 collective-permute-done.9.refs_6_
  32.5 0.6 collective-permute-start.3
  33.1 1.4 %collective-permute-start.4 = (bf16[96,2304]{1,0:T(8,128)(2,1)S(1)}, bf16[96,2304]{1,0:T(8,128)(2,1)}, u32[]{:S(2)}, u32[]{:S(2)}) collective-permute-start(bf16[96,2304]{1,0:T(8,128)(2,1)S(1)} %copy-done.10), channel_id=1, source_target_pairs={{0,2},{1,3},{2,0},{3,1},{4,6},{5,7},{6,4},{7,5},{8,10},{9,11},{10,... | collective-permute-start | bytes 1327112 | tf_op jit(solution)/shard_map/ppermute | solution.py:53
  34.5 8.5 %collective-permute-done.3.refs_0_ = bf16[96,2304]{1,0:T(8,128)(2,1)} collective-permute-done((bf16[96,2304]{1,0:T(8,128)(2,1)S(1)}, bf16[96,2304]{1,0:T(8,128)(2,1)}, u32[]{:S(2)}, u32[]{:S(2)}) %collective-permute-start.3) | collective-permute-done | bytes 442400 | tf_op jit(solution)/shard_map/ppermute | solution.py:53
  43.6 1.3 %collective-permute-done.5.refs_2_ = bf16[96,2304]{1,0:T(8,128)(2,1)} collective-permute-done((bf16[96,2304]{1,0:T(8,128)(2,1)S(1)}, bf16[96,2304]{1,0:T(8,128)(2,1)}, u32[]{:S(2)}, u32[]{:S(2)}) %collective-permute-start.5) | collective-permute-done | bytes 442400 | tf_op jit(solution)/shard_map/ppermute | solution.py:53
  44.9 0.7 collective-permute-done.6.refs_3_
  45.6 1.9 %collective-permute-done.10.refs_7_ = bf16[384,1536]{1,0:T(8,128)(2,1)} collective-permute-done((bf16[384,1536]{1,0:T(8,128)(2,1)}, bf16[384,1536]{1,0:T(8,128)(2,1)}, u32[]{:S(2)}, u32[]{:S(2)}) %collective-permute-start.10) | collective-permute-done | bytes 1179680 | tf_op jit(solution)/shard_map/ppermute | solution.py:492
  47.5 1.4 %collective-permute-start.14 = (bf16[384,1536]{1,0:T(8,128)(2,1)}, bf16[384,1536]{1,0:T(8,128)(2,1)S(1)}, u32[]{:S(2)}, u32[]{:S(2)}) collective-permute-start(bf16[384,1536]{1,0:T(8,128)(2,1)} %get-tuple-element.41.refs_13_), channel_id=1, source_target_pairs={{16,24},{17,25},{18,26},{19,27},{20,28},{21,29},{22,30},{23,31}} | collective-permute-start | bytes 3538952 | tf_op jit(solution)/shard_map/ppermute | solution.py:505
  49.0 0.5 collective-permute-start.13
  50.4 0.8 collective-permute-start.15
  51.2 2.2 %collective-permute-done.12.refs_6_ = bf16[96,2304]{1,0:T(8,128)(2,1)S(1)} collective-permute-done((bf16[96,2304]{1,0:T(8,128)(2,1)}, bf16[96,2304]{1,0:T(8,128)(2,1)S(1)}, u32[]{:S(2)}, u32[]{:S(2)}) %collective-permute-start.12) | collective-permute-done | bytes 442400 | tf_op jit(solution)/shard_map/ppermute | solution.py:53
  53.8 10.2 %project_attend_tail.1 = (bf16[256,768]{1,0:T(8,128)(2,1)S(1)}, bf16[768,1536]{1,0:T(8,128)(2,1)S(1)}, bf16[128,768]{1,0:T(8,128)(2,1)S(1)}) custom-call(s32[12]{0:T(128)S(1)} %stack.119.places_ref, s32[3,3]{1,0:T(4,128)S(1)} %copy-done.6, bf16[384,1536]{1,0:T(8,128)(2,1)} %normalize.1.normed_hbm.refs_12_, bf16[96,2304]{1,0:T(8,128)(2,1)} %get-tuple-element.32.refs_0_, ...), custom_call_target="tpu_custom_call" | custom-call | flops 10000000000 | bytes 1 | tf_op jit(solution)/shard_map/project_attend_tail/pallas_call | solution.py:394
  64.1 2.7 %collective-permute-start.16 = (bf16[128,768]{1,0:T(8,128)(2,1)S(1)}, bf16[128,768]{1,0:T(8,128)(2,1)S(1)}, u32[]{:S(2)}, u32[]{:S(2)}) collective-permute-start(bf16[128,768]{1,0:T(8,128)(2,1)S(1)} %get-tuple-element.47), channel_id=1, source_target_pairs={{0,1},{1,2},{2,3},{3,4},{4,5},{5,6},{6,7},{8,9},{9,10},{10,11},{11... | collective-permute-start | bytes 589832 | tf_op jit(solution)/shard_map/ppermute | solution.py:59
  66.8 3.7 %attend_main.1.attended_ref = f32[256,768]{1,0:T(8,128)S(1)} custom-call(s32[1]{0:T(128)} %bitcast.11.places_ref, s32[3,3]{1,0:T(4,128)S(1)} %copy-done.6, bf16[256,768]{1,0:T(8,128)(2,1)S(1)} %get-tuple-element.43.query_ref, bf16[768,1536]{1,0:T(8,128)(2,1)S(1)} %get-tuple-element.44.keyval_ref), custom_call_target="tpu_custom_call" | custom-call | flops 4000000000 | bytes 1 | tf_op jit(solution)/shard_map/attend_main/pallas_call | solution.py:432
  70.5 2.8 %collective-permute-done.16.received_ref = bf16[128,768]{1,0:T(8,128)(2,1)S(1)} collective-permute-done((bf16[128,768]{1,0:T(8,128)(2,1)S(1)}, bf16[128,768]{1,0:T(8,128)(2,1)S(1)}, u32[]{:S(2)}, u32[]{:S(2)}) %collective-permute-start.16) | collective-permute-done | bytes 196640 | tf_op jit(solution)/shard_map/ppermute | solution.py:59
  73.4 2.4 %blend_and_step.1 = bf16[256,1536]{1,0:T(8,128)(2,1)} custom-call(s32[6]{0:T(128)S(1)} %stack.99.places_ref, f32[4]{0:T(128)S(1)} %pad_maximum_fusion.coef_ref, f32[256,768]{1,0:T(8,128)S(1)} %attend_main.1.attended_ref, bf16[128,768]{1,0:T(8,128)(2,1)S(1)} %collective-permute-done.16.received_ref, bf16[256,1536]{1,0:T(8,128)(2,1)S(1)} %bitcast.36, ...), custom_call_target="tpu_custom_call" | custom-call | flops 3000000000 | bytes 1 | tf_op jit(solution)/shard_map/blend_and_step/pallas_call | solution.py:466
  (51 shorter events, 1.8 us)
Async XLA Ops:
  0.1 7.9 %copy-start.4 = (s32[1,64]{1,0:T(1,128)S(1)}, s32[1,64]{1,0:T(1,128)}, u32[]{:S(2)}) copy-start(s32[1,64]{1,0:T(1,128)} %ids_ref.1) | copy-start | bytes 772
  2.0 23.4 %collective-permute-start.1 = (bf16[96,2304]{1,0:T(8,128)(2,1)S(1)}, bf16[96,2304]{1,0:T(8,128)(2,1)S(1)}, u32[]{:S(2)}, u32[]{:S(2)}) collective-permute-start(bf16[96,2304]{1,0:T(8,128)(2,1)S(1)} %get-tuple-element.28), channel_id=1, source_target_pairs={{0,16},{8,24},{16,0},{24,8},{1,17},{9,25},{17,1},{25,9},{2,18},{10... | collective-permute-start | bytes 1327112 | tf_op jit(solution)/shard_map/ppermute | solution.py:53
  2.6 22.8 %collective-permute-start.2 = (bf16[96,2304]{1,0:T(8,128)(2,1)S(1)}, bf16[96,2304]{1,0:T(8,128)(2,1)}, u32[]{:S(2)}, u32[]{:S(2)}) collective-permute-start(bf16[96,2304]{1,0:T(8,128)(2,1)S(1)} %get-tuple-element.29), channel_id=1, source_target_pairs={{0,16},{8,24},{16,0},{24,8},{1,17},{9,25},{17,1},{25,9},{2,18},{10... | collective-permute-start | bytes 1327112 | tf_op jit(solution)/shard_map/ppermute | solution.py:53
  4.1 20.0 %collective-permute-start = (bf16[128,1536]{1,0:T(8,128)(2,1)S(1)}, bf16[128,1536]{1,0:T(8,128)(2,1)S(1)}, u32[]{:S(2)}, u32[]{:S(2)}) collective-permute-start(bf16[128,1536]{1,0:T(8,128)(2,1)S(1)} %get-tuple-element.27.after_ref), channel_id=1, source_target_pairs={{1,0},{2,1},{3,2},{4,3},{5,4},{6,5},{7,6},{9,8},{10,9},{11,10},{12... | collective-permute-start | bytes 1179656 | tf_op jit(solution)/shard_map/ppermute | solution.py:59
  7.4 25.7 %collective-permute-start.7 = (bf16[384,768]{1,0:T(8,128)(2,1)}, bf16[384,768]{1,0:T(8,128)(2,1)S(1)}, u32[]{:S(2)}, u32[]{:S(2)}) collective-permute-start(bf16[384,768]{1,0:T(8,128)(2,1)} %refs_8_.1), channel_id=1, source_target_pairs={{0,8},{8,0},{16,24},{24,16},{1,9},{9,1},{17,25},{25,17},{2,10},{10... | collective-permute-start | bytes 1769480 | tf_op jit(solution)/shard_map/ppermute | solution.py:53
  7.5 38.1 %collective-permute-start.8 = (bf16[384,1536]{1,0:T(8,128)(2,1)}, bf16[384,1536]{1,0:T(8,128)(2,1)}, u32[]{:S(2)}, u32[]{:S(2)}) collective-permute-start(bf16[384,1536]{1,0:T(8,128)(2,1)} %refs_10_.1), channel_id=1, source_target_pairs={{0,8},{8,0},{16,24},{24,16},{1,9},{9,1},{17,25},{25,17},{2,10},{10... | collective-permute-start | bytes 3538952 | tf_op jit(solution)/shard_map/ppermute | solution.py:53
  13.2 10.4 %all-to-all-start = ((f32[8,1,192]{2,1,0:T(1,128)}), f32[8,1,192]{2,1,0:T(1,128)S(1)}, u32[]{:S(2)}, u32[]{:S(2)}) async-start(f32[8,1,192]{2,1,0:T(1,128)} %broadcast_in_dim.4), calls=%async_computation | async-start | bytes 16384 | tf_op jit(solution)/shard_map/all_to_all | solution.py:93
  24.9 7.6 %collective-permute-start.9 = (bf16[96,1536]{1,0:T(8,128)(2,1)S(1)}, bf16[96,1536]{1,0:T(8,128)(2,1)S(1)}, u32[]{:S(2)}, u32[]{:S(2)}) collective-permute-start(bf16[96,1536]{1,0:T(8,128)(2,1)S(1)} %get-tuple-element.34), channel_id=1, source_target_pairs={{0,16},{8,24},{16,0},{24,8},{1,17},{9,25},{17,1},{25,9},{2,18},{10... | collective-permute-start | bytes 884744 | tf_op jit(solution)/shard_map/ppermute | solution.py:53
  25.4 0.8 %copy-start.9 = (bf16[96,2304]{1,0:T(8,128)(2,1)}, bf16[96,2304]{1,0:T(8,128)(2,1)S(1)}, u32[]{:S(2)}) copy-start(bf16[96,2304]{1,0:T(8,128)(2,1)S(1)} %collective-permute-done.1.refs_2_) | copy-start | bytes 1327108
  26.3 6.2 %copy-start.10 = (bf16[96,2304]{1,0:T(8,128)(2,1)S(1)}, bf16[96,2304]{1,0:T(8,128)(2,1)}, u32[]{:S(2)}) copy-start(bf16[96,2304]{1,0:T(8,128)(2,1)} %get-tuple-element.32.refs_0_) | copy-start | bytes 1327108
  29.1 18.4 %collective-permute-start.10 = (bf16[384,1536]{1,0:T(8,128)(2,1)}, bf16[384,1536]{1,0:T(8,128)(2,1)}, u32[]{:S(2)}, u32[]{:S(2)}) collective-permute-start(bf16[384,1536]{1,0:T(8,128)(2,1)} %normalize.1.normed_hbm.refs_12_), channel_id=1, source_target_pairs={{0,16},{1,17},{2,18},{3,19},{4,20},{5,21},{6,22},{7,23}} | collective-permute-start | bytes 3538952 | tf_op jit(solution)/shard_map/ppermute | solution.py:492
  30.4 17.1 %collective-permute-start.11 = (bf16[384,1536]{1,0:T(8,128)(2,1)}, bf16[384,1536]{1,0:T(8,128)(2,1)}, u32[]{:S(2)}, u32[]{:S(2)}) collective-permute-start(bf16[384,1536]{1,0:T(8,128)(2,1)} %normalize.1.normed_hbm.refs_12_), channel_id=1, source_target_pairs={{0,8},{1,9},{2,10},{3,11},{4,12},{5,13},{6,14},{7,15}} | collective-permute-start | bytes 3538952 | tf_op jit(solution)/shard_map/ppermute | solution.py:492
  32.5 15.0 %copy-start.2 = (bf16[96,1536]{1,0:T(8,128)(2,1)}, bf16[96,1536]{1,0:T(8,128)(2,1)S(1)}, u32[]{:S(2)}) copy-start(bf16[96,1536]{1,0:T(8,128)(2,1)S(1)} %collective-permute-done.9.refs_6_) | copy-start | bytes 884740
  32.5 10.5 %collective-permute-start.3 = (bf16[96,2304]{1,0:T(8,128)(2,1)S(1)}, bf16[96,2304]{1,0:T(8,128)(2,1)}, u32[]{:S(2)}, u32[]{:S(2)}) collective-permute-start(bf16[96,2304]{1,0:T(8,128)(2,1)S(1)} %copy-done.10), channel_id=1, source_target_pairs={{0,1},{1,0},{2,3},{3,2},{4,5},{5,4},{6,7},{7,6},{8,9},{9,8},{10,11... | collective-permute-start | bytes 1327112 | tf_op jit(solution)/shard_map/ppermute | solution.py:53
  33.1 10.3 %copy-start.7 = (bf16[384,768]{1,0:T(8,128)(2,1)}, bf16[384,768]{1,0:T(8,128)(2,1)S(1)}, u32[]{:S(2)}) copy-start(bf16[384,768]{1,0:T(8,128)(2,1)S(1)} %collective-permute-done.7.refs_4_) | copy-start | bytes 1769476
  33.1 10.2 %collective-permute-start.4 = (bf16[96,2304]{1,0:T(8,128)(2,1)S(1)}, bf16[96,2304]{1,0:T(8,128)(2,1)}, u32[]{:S(2)}, u32[]{:S(2)}) collective-permute-start(bf16[96,2304]{1,0:T(8,128)(2,1)S(1)} %copy-done.10), channel_id=1, source_target_pairs={{0,2},{1,3},{2,0},{3,1},{4,6},{5,7},{6,4},{7,5},{8,10},{9,11},{10,... | collective-permute-start | bytes 1327112 | tf_op jit(solution)/shard_map/ppermute | solution.py:53
  43.0 1.9 %collective-permute-start.5 = (bf16[96,2304]{1,0:T(8,128)(2,1)S(1)}, bf16[96,2304]{1,0:T(8,128)(2,1)}, u32[]{:S(2)}, u32[]{:S(2)}) collective-permute-start(bf16[96,2304]{1,0:T(8,128)(2,1)S(1)} %copy-done.10), channel_id=1, source_target_pairs={{0,8},{8,0},{16,24},{24,16},{1,9},{9,1},{17,25},{25,17},{2,10},{10... | collective-permute-start | bytes 1327112 | tf_op jit(solution)/shard_map/ppermute | solution.py:53
  43.4 6.1 %copy-start.1 = (bf16[192,1536]{1,0:T(8,128)(2,1)S(1)}, bf16[192,1536]{1,0:T(8,128)(2,1)}, u32[]{:S(2)}) copy-start(bf16[192,1536]{1,0:T(8,128)(2,1)} %refs_0_.1) | copy-start | bytes 1769476
  43.4 10.4 %copy-start.6 = (s32[3,3]{1,0:T(4,128)S(1)}, s32[3,3]{1,0:T(4,128)}, u32[]{:S(2)}) copy-start(s32[3,3]{1,0:T(4,128)} %table_ref.3) | copy-start | bytes 112
  43.4 2.3 %collective-permute-start.6 = (bf16[96,2304]{1,0:T(8,128)(2,1)}, bf16[96,2304]{1,0:T(8,128)(2,1)S(1)}, u32[]{:S(2)}, u32[]{:S(2)}) collective-permute-start(bf16[96,2304]{1,0:T(8,128)(2,1)} %get-tuple-element.33.refs_3_), channel_id=1, source_target_pairs={{0,8},{8,0},{16,24},{24,16},{1,9},{9,1},{17,25},{25,17},{2,10},{10... | collective-permute-start | bytes 1327112 | tf_op jit(solution)/shard_map/ppermute | solution.py:53
  45.6 1.9 %copy-start.8 = (bf16[96,2304]{1,0:T(8,128)(2,1)}, bf16[96,2304]{1,0:T(8,128)(2,1)S(1)}, u32[]{:S(2)}) copy-start(bf16[96,2304]{1,0:T(8,128)(2,1)S(1)} %collective-permute-done.6.refs_3_) | copy-start | bytes 1327108
  47.5 6.2 %collective-permute-start.14 = (bf16[384,1536]{1,0:T(8,128)(2,1)}, bf16[384,1536]{1,0:T(8,128)(2,1)S(1)}, u32[]{:S(2)}, u32[]{:S(2)}) collective-permute-start(bf16[384,1536]{1,0:T(8,128)(2,1)} %get-tuple-element.41.refs_13_), channel_id=1, source_target_pairs={{16,24},{17,25},{18,26},{19,27},{20,28},{21,29},{22,30},{23,31}} | collective-permute-start | bytes 3538952 | tf_op jit(solution)/shard_map/ppermute | solution.py:505
  48.9 4.5 %collective-permute-start.12 = (bf16[96,2304]{1,0:T(8,128)(2,1)}, bf16[96,2304]{1,0:T(8,128)(2,1)S(1)}, u32[]{:S(2)}, u32[]{:S(2)}) collective-permute-start(bf16[96,2304]{1,0:T(8,128)(2,1)} %get-tuple-element.35.refs_1_), channel_id=1, source_target_pairs={{0,8},{8,0},{16,24},{24,16},{1,9},{9,1},{17,25},{25,17},{2,10},{10... | collective-permute-start | bytes 1327112 | tf_op jit(solution)/shard_map/ppermute | solution.py:53
  49.0 4.8 %collective-permute-start.13 = (bf16[96,2304]{1,0:T(8,128)(2,1)}, bf16[96,2304]{1,0:T(8,128)(2,1)}, u32[]{:S(2)}, u32[]{:S(2)}) collective-permute-start(bf16[96,2304]{1,0:T(8,128)(2,1)} %get-tuple-element.36.refs_2_), channel_id=1, source_target_pairs={{0,8},{8,0},{16,24},{24,16},{1,9},{9,1},{17,25},{25,17},{2,10},{10... | collective-permute-start | bytes 1327112 | tf_op jit(solution)/shard_map/ppermute | solution.py:53
  49.5 21.0 %collective-permute-start.17 = (bf16[192,1536]{1,0:T(8,128)(2,1)S(1)}, bf16[192,1536]{1,0:T(8,128)(2,1)S(1)}, u32[]{:S(2)}, u32[]{:S(2)}) collective-permute-start(bf16[192,1536]{1,0:T(8,128)(2,1)S(1)} %copy-done.1), channel_id=1, source_target_pairs={{0,8},{8,0},{16,24},{24,16},{1,9},{9,1},{17,25},{25,17},{2,10},{10... | collective-permute-start | bytes 1769480 | tf_op jit(solution)/shard_map/ppermute | solution.py:53
  50.4 13.6 %collective-permute-start.15 = (bf16[96,1536]{1,0:T(8,128)(2,1)}, bf16[96,1536]{1,0:T(8,128)(2,1)S(1)}, u32[]{:S(2)}, u32[]{:S(2)}) collective-permute-start(bf16[96,1536]{1,0:T(8,128)(2,1)} %get-tuple-element.46.refs_2_), channel_id=1, source_target_pairs={{0,1},{1,0},{2,3},{3,2},{4,5},{5,4},{6,7},{7,6},{8,9},{9,8},{10,11... | collective-permute-start | bytes 884744 | tf_op jit(solution)/shard_map/ppermute | solution.py:53
  53.4 17.1 %collective-permute-start.18 = (bf16[96,1536]{1,0:T(8,128)(2,1)}, bf16[96,1536]{1,0:T(8,128)(2,1)S(1)}, u32[]{:S(2)}, u32[]{:S(2)}) collective-permute-start(bf16[96,1536]{1,0:T(8,128)(2,1)} %get-tuple-element.46.refs_2_), channel_id=1, source_target_pairs={{0,8},{8,0},{16,24},{24,16},{1,9},{9,1},{17,25},{25,17},{2,10},{10... | collective-permute-start | bytes 884744 | tf_op jit(solution)/shard_map/ppermute | solution.py:53
  64.1 9.3 %collective-permute-start.16 = (bf16[128,768]{1,0:T(8,128)(2,1)S(1)}, bf16[128,768]{1,0:T(8,128)(2,1)S(1)}, u32[]{:S(2)}, u32[]{:S(2)}) collective-permute-start(bf16[128,768]{1,0:T(8,128)(2,1)S(1)} %get-tuple-element.47), channel_id=1, source_target_pairs={{0,1},{1,2},{2,3},{3,4},{4,5},{5,6},{6,7},{8,9},{9,10},{10,11},{11... | collective-permute-start | bytes 589832 | tf_op jit(solution)/shard_map/ppermute | solution.py:59
  66.7 6.7 %collective-permute-start.19 = (bf16[96,1536]{1,0:T(8,128)(2,1)S(1)}, bf16[96,1536]{1,0:T(8,128)(2,1)S(1)}, u32[]{:S(2)}, u32[]{:S(2)}) collective-permute-start(bf16[96,1536]{1,0:T(8,128)(2,1)S(1)} %get-tuple-element.48.refs_3_), channel_id=1, source_target_pairs={{0,8},{8,0},{16,24},{24,16},{1,9},{9,1},{17,25},{25,17},{2,10},{10... | collective-permute-start | bytes 884744 | tf_op jit(solution)/shard_map/ppermute | solution.py:53
  66.8 6.6 %copy-start = (bf16[1,256,1536]{2,1,0:T(8,128)(2,1)S(1)}, bf16[1,256,1536]{2,1,0:T(8,128)(2,1)}, u32[]{:S(2)}) copy-start(bf16[1,256,1536]{2,1,0:T(8,128)(2,1)} %param.9) | copy-start | bytes 2359300
  66.8 6.6 %copy-start.3 = (bf16[96,1536]{1,0:T(8,128)(2,1)S(1)}, bf16[96,1536]{1,0:T(8,128)(2,1)}, u32[]{:S(2)}) copy-start(bf16[96,1536]{1,0:T(8,128)(2,1)} %get-tuple-element.46.refs_2_) | copy-start | bytes 884740
  66.8 6.6 %copy-start.5 = (bf16[1,256,1536]{2,1,0:T(8,128)(2,1)S(1)}, bf16[1,256,1536]{2,1,0:T(8,128)(2,1)}, u32[]{:S(2)}) copy-start(bf16[1,256,1536]{2,1,0:T(8,128)(2,1)} %param.10) | copy-start | bytes 2359300
  (1 other events, 0.7 us)

commit v5 on v4

--- a/solution.py
+++ b/solution.py
@@ -89,7 +89,7 @@
 
 def whole_rows(row):
     tm_count = lax.axis_size("tm")
-    sent = jnp.broadcast_to(row, (tm_count, row.shape[1]))
+    sent = row if row.shape[0] == tm_count else jnp.broadcast_to(row[:1], (tm_count, row.shape[1]))
     arrived = lax.all_to_all(sent, "tm", 0, 0, tiled=True)
     if row.shape[1] % HS or tm_count % 8:
         arrived = arrived.reshape(1, tm_count * row.shape[1])
@@ -251,19 +251,29 @@
     latent_ref, halo_ref, rows_ref, cos_ref, sin_ref, normed_ref, window, normed, rows, sems
 ):
     main_rows = latent_ref.shape[0]
-    copies = [
-        pltpu.make_async_copy(latent_ref, window.at[:main_rows, :], sems.at[0]),
-        pltpu.make_async_copy(halo_ref, window.at[main_rows:, :], sems.at[1]),
-        pltpu.make_async_copy(rows_ref, rows, sems.at[2]),
+    part = SEAM
+    parts = [pl.ds(begin, part) for begin in range(0, window.shape[0], part)]
+    sources = [latent_ref.at[at, :] for at in parts[: main_rows // part]] + [halo_ref]
+    copies = [pltpu.make_async_copy(rows_ref, rows, sems.at[0])]
+    copies += [
+        pltpu.make_async_copy(source, window.at[at, :], sems.at[1 + k])
+        for k, (source, at) in enumerate(zip(sources, parts))
     ]
     for copy in copies:
         copy.start()
-    for copy in copies:
-        copy.wait()
-    normalize(normed, 0, window, scale_of(rows, cos_ref, sin_ref), window.shape[1])
-    copy = pltpu.make_async_copy(normed, normed_ref, sems.at[3])
-    copy.start()
-    copy.wait()
+    copies[0].wait()
+    scale = scale_of(rows, cos_ref, sin_ref)
+    stores = []
+    for k, at in enumerate(parts):
+        copies[1 + k].wait()
+        normalize(normed.at[at, :], 0, window.at[at, :], scale, window.shape[1])
+        store = pltpu.make_async_copy(
+            normed.at[at, :], normed_ref.at[at, :], sems.at[1 + len(parts) + k]
+        )
+        store.start()
+        stores.append(store)
+    for store in stores:
+        store.wait()
 
 
 def normalized(latent, halo, rows, waves):
@@ -277,7 +287,7 @@
             pltpu.VMEM(shape, BF16),
             pltpu.VMEM(shape, BF16),
             pltpu.VMEM(rows.shape, F32),
-            pltpu.SemaphoreType.DMA((4,)),
+            pltpu.SemaphoreType.DMA((1 + 2 * (shape[0] // SEAM),)),
         ],
         compiler_params=params(),
         cost_estimate=cost(MICROSECOND),
@@ -529,7 +539,7 @@
     )
     pooled = pool(prompt_ids, prompt_table, halo_rows)
     halo = shifted(halo_rows, "tm", -1)
-    pooled = whole_rows(pooled[:1])
+    pooled = whole_rows(pooled)
     if routed:
         quarter = rows // 4
         first = swapped(cuts[0], "var", 2)

time: 76.1 us -> 75.7 us (level)
  no operation moved by 1% of the time
where the time goes in v5:
time: 75.7 us; the launch traced here: 75.4 us
  Pallas kernels  25.2 us (33%)
  starting transfers between devices  23.2 us (31%)
  waiting for transfers between devices  22.2 us (29%)
  local copies, waits for them, and re-layouts  2.96 us (4%)
  between operations  1.5 us (2%)
    ppermute x15, waiting for transfers between devices, swapped(): return lax.ppermute(block, axis, route)  13.5 us
    pallas_call x1, Pallas kernels, project(): pl.pallas_call(functools.partial(project_kernel, len(wide), len(queries),...  10.2 us
    ppermute x15, starting transfers between devices, swapped(): return lax.ppermute(block, axis, route)  7.33 us
    ppermute x2, starting transfers between devices, shifted(): return lax.ppermute(block, axis, route)  6.14 us
    all_to_all x1, starting transfers between devices, whole_rows(): arrived = lax.all_to_all(sent, 'tm', 0, 0, tiled=True)  5.4 us
    pallas_call x1, Pallas kernels, pool(): pl.pallas_call(pool_kernel, out_shape=jax.ShapeDtypeStruct((8, table_colu...  4.52 us
    all_to_all x1, waiting for transfers between devices, whole_rows(): arrived = lax.all_to_all(sent, 'tm', 0, 0, tiled=True)  4.24 us
    pallas_call x1, Pallas kernels, attend_main(): pl.pallas_call(main_kernel, out_shape=jax.ShapeDtypeStruct((rows, width),...  3.67 us
  transfers between devices with their start and end apart: 21, of which 9 were waited for; matrix products, arithmetic and copies ran while one was open for 2% of the time, Pallas kernels for 28%

profile of v5, /device:TPU:10, one launch (start us, length us, event | category | flops | bytes accessed | tf_op | source)
XLA Modules:
  0.0 75.4 jit_solution(666315736860707880)
XLA Ops:
  0.1 1.9 %first_rows.1 = (bf16[128,1536]{1,0:T(8,128)(2,1)S(1)}, bf16[96,1536]{1,0:T(8,128)(2,1)S(1)}, bf16[96,2304]{1,0:T(8,128)(2,1)S(1)}, bf16[96,2304]{1,0:T(8,128)(2,1)S(1)}) custom-call(s32[3]{0:T(128)S(1)} %pad_add_fusion.places_ref, bf16[384,768]{1,0:T(8,128)(2,1)} %refs_8_.1, bf16[384,1536]{1,0:T(8,128)(2,1)} %refs_10_.1, bf16[192,1536]{1,0:T(8,128)(2,1)} %refs_0_.1, ...), custom_call_target="tpu_custom_call" | custom-call | flops 1 | bytes 1 | tf_op jit(solution)/shard_map/first_rows/pallas_call | solution.py:169
  2.0 0.6 collective-permute-start.1
  2.6 1.5 %collective-permute-start.2 = (bf16[96,2304]{1,0:T(8,128)(2,1)S(1)}, bf16[96,2304]{1,0:T(8,128)(2,1)}, u32[]{:S(2)}, u32[]{:S(2)}) collective-permute-start(bf16[96,2304]{1,0:T(8,128)(2,1)S(1)} %get-tuple-element.29), channel_id=1, source_target_pairs={{0,16},{8,24},{16,0},{24,8},{1,17},{9,25},{17,1},{25,9},{2,18},{10... | collective-permute-start | bytes 1327112 | tf_op jit(solution)/shard_map/ppermute | solution.py:53
  4.1 3.3 %collective-permute-start = (bf16[128,1536]{1,0:T(8,128)(2,1)S(1)}, bf16[128,1536]{1,0:T(8,128)(2,1)S(1)}, u32[]{:S(2)}, u32[]{:S(2)}) collective-permute-start(bf16[128,1536]{1,0:T(8,128)(2,1)S(1)} %get-tuple-element.27.after_ref), channel_id=1, source_target_pairs={{1,0},{2,1},{3,2},{4,3},{5,4},{6,5},{7,6},{9,8},{10,9},{11,10},{12... | collective-permute-start | bytes 1179656 | tf_op jit(solution)/shard_map/ppermute | solution.py:59
  7.5 0.5 collective-permute-start.8
  8.0 4.5 %pool_prompt.1 = f32[8,192]{1,0:T(8,128)S(1)} custom-call(s32[1,64]{1,0:T(1,128)S(1)} %copy-done.4, bf16[192,16384]{1,0:T(8,128)(2,1)} %bitcast.39, bf16[128,1536]{1,0:T(8,128)(2,1)S(1)} %get-tuple-element.27.after_ref), custom_call_target="tpu_custom_call" | custom-call | flops 1 | bytes 1 | tf_op jit(solution)/shard_map/pool_prompt/pallas_call | solution.py:126
  12.5 0.6 copy.25
  13.1 5.4 %all-to-all-start = ((f32[8,1,192]{2,1,0:T(1,128)}), f32[8,1,192]{2,1,0:T(1,128)S(1)}, u32[]{:S(2)}, u32[]{:S(2)}) async-start(f32[8,1,192]{2,1,0:T(1,128)} %copy.25), calls=%async_computation | async-start | bytes 16384 | tf_op jit(solution)/shard_map/all_to_all | solution.py:93
  19.3 4.2 %all-to-all-done = f32[8,1,192]{2,1,0:T(1,128)S(1)} async-done(((f32[8,1,192]{2,1,0:T(1,128)}), f32[8,1,192]{2,1,0:T(1,128)S(1)}, u32[]{:S(2)}, u32[]{:S(2)}) %all-to-all-start) | async-done | bytes 6176 | tf_op jit(solution)/shard_map/all_to_all | solution.py:93
  23.6 0.6 copy.28
  24.2 0.7 copy-done.11
  24.9 0.5 collective-permute-start.9
  25.4 0.8 %copy-done.9 = bf16[96,2304]{1,0:T(8,128)(2,1)} copy-done((bf16[96,2304]{1,0:T(8,128)(2,1)}, bf16[96,2304]{1,0:T(8,128)(2,1)S(1)}, u32[]{:S(2)}) %copy-start.9) | copy-done | bytes 442392
  26.2 2.4 %normalize.1.normed_hbm.refs_12_ = bf16[384,1536]{1,0:T(8,128)(2,1)} custom-call(bf16[256,1536]{1,0:T(8,128)(2,1)} %bitcast.35, bf16[128,1536]{1,0:T(8,128)(2,1)} %get-tuple-element.30.halo_ref, f32[8,192]{1,0:T(8,128)} %get-tuple-element.31.rows_ref, f32[1,768]{1,0:T(1,128)S(1)} %get-tuple-element.50.cos_ref, f32[1,768]{1,0:T(1,128)S(1)} %get-tuple-element.49.sin_ref), custom_call_target="tpu_custom_call" | custom-call | flops 1000000000 | bytes 1 | tf_op jit(solution)/shard_map/normalize/pallas_call | solution.py:281
  28.7 1.3 %collective-permute-start.10 = (bf16[384,1536]{1,0:T(8,128)(2,1)}, bf16[384,1536]{1,0:T(8,128)(2,1)}, u32[]{:S(2)}, u32[]{:S(2)}) collective-permute-start(bf16[384,1536]{1,0:T(8,128)(2,1)} %normalize.1.normed_hbm.refs_12_), channel_id=1, source_target_pairs={{0,16},{1,17},{2,18},{3,19},{4,20},{5,21},{6,22},{7,23}} | collective-permute-start | bytes 3538952 | tf_op jit(solution)/shard_map/ppermute | solution.py:502
  30.0 1.7 %collective-permute-start.11 = (bf16[384,1536]{1,0:T(8,128)(2,1)}, bf16[384,1536]{1,0:T(8,128)(2,1)}, u32[]{:S(2)}, u32[]{:S(2)}) collective-permute-start(bf16[384,1536]{1,0:T(8,128)(2,1)} %normalize.1.normed_hbm.refs_12_), channel_id=1, source_target_pairs={{0,8},{1,9},{2,10},{3,11},{4,12},{5,13},{6,14},{7,15}} | collective-permute-start | bytes 3538952 | tf_op jit(solution)/shard_map/ppermute | solution.py:502
  31.7 0.8 %collective-permute-done.9.refs_6_ = bf16[96,1536]{1,0:T(8,128)(2,1)S(1)} collective-permute-done((bf16[96,1536]{1,0:T(8,128)(2,1)S(1)}, bf16[96,1536]{1,0:T(8,128)(2,1)S(1)}, u32[]{:S(2)}, u32[]{:S(2)}) %collective-permute-start.9) | collective-permute-done | bytes 294944 | tf_op jit(solution)/shard_map/ppermute | solution.py:53
  32.5 0.6 collective-permute-start.3
  33.1 1.4 %collective-permute-start.4 = (bf16[96,2304]{1,0:T(8,128)(2,1)S(1)}, bf16[96,2304]{1,0:T(8,128)(2,1)}, u32[]{:S(2)}, u32[]{:S(2)}) collective-permute-start(bf16[96,2304]{1,0:T(8,128)(2,1)S(1)} %copy-done.10), channel_id=1, source_target_pairs={{0,2},{1,3},{2,0},{3,1},{4,6},{5,7},{6,4},{7,5},{8,10},{9,11},{10,... | collective-permute-start | bytes 1327112 | tf_op jit(solution)/shard_map/ppermute | solution.py:53
  34.5 8.1 %collective-permute-done.3.refs_0_ = bf16[96,2304]{1,0:T(8,128)(2,1)} collective-permute-done((bf16[96,2304]{1,0:T(8,128)(2,1)S(1)}, bf16[96,2304]{1,0:T(8,128)(2,1)}, u32[]{:S(2)}, u32[]{:S(2)}) %collective-permute-start.3) | collective-permute-done | bytes 442400 | tf_op jit(solution)/shard_map/ppermute | solution.py:53
  43.2 1.3 %collective-permute-done.5.refs_2_ = bf16[96,2304]{1,0:T(8,128)(2,1)} collective-permute-done((bf16[96,2304]{1,0:T(8,128)(2,1)S(1)}, bf16[96,2304]{1,0:T(8,128)(2,1)}, u32[]{:S(2)}, u32[]{:S(2)}) %collective-permute-start.5) | collective-permute-done | bytes 442400 | tf_op jit(solution)/shard_map/ppermute | solution.py:53
  44.5 0.7 collective-permute-done.6.refs_3_
  45.3 1.9 %collective-permute-done.10.refs_7_ = bf16[384,1536]{1,0:T(8,128)(2,1)} collective-permute-done((bf16[384,1536]{1,0:T(8,128)(2,1)}, bf16[384,1536]{1,0:T(8,128)(2,1)}, u32[]{:S(2)}, u32[]{:S(2)}) %collective-permute-start.10) | collective-permute-done | bytes 1179680 | tf_op jit(solution)/shard_map/ppermute | solution.py:502
  47.1 1.4 %collective-permute-start.14 = (bf16[384,1536]{1,0:T(8,128)(2,1)}, bf16[384,1536]{1,0:T(8,128)(2,1)S(1)}, u32[]{:S(2)}, u32[]{:S(2)}) collective-permute-start(bf16[384,1536]{1,0:T(8,128)(2,1)} %get-tuple-element.41.refs_13_), channel_id=1, source_target_pairs={{16,24},{17,25},{18,26},{19,27},{20,28},{21,29},{22,30},{23,31}} | collective-permute-start | bytes 3538952 | tf_op jit(solution)/shard_map/ppermute | solution.py:515
  48.6 0.5 collective-permute-start.13
  50.1 0.8 %collective-permute-start.15 = (bf16[96,1536]{1,0:T(8,128)(2,1)}, bf16[96,1536]{1,0:T(8,128)(2,1)S(1)}, u32[]{:S(2)}, u32[]{:S(2)}) collective-permute-start(bf16[96,1536]{1,0:T(8,128)(2,1)} %get-tuple-element.46.refs_2_), channel_id=1, source_target_pairs={{0,1},{1,0},{2,3},{3,2},{4,5},{5,4},{6,7},{7,6},{8,9},{9,8},{10,11... | collective-permute-start | bytes 884744 | tf_op jit(solution)/shard_map/ppermute | solution.py:53
  50.8 2.2 %collective-permute-done.12.refs_6_ = bf16[96,2304]{1,0:T(8,128)(2,1)S(1)} collective-permute-done((bf16[96,2304]{1,0:T(8,128)(2,1)}, bf16[96,2304]{1,0:T(8,128)(2,1)S(1)}, u32[]{:S(2)}, u32[]{:S(2)}) %collective-permute-start.12) | collective-permute-done | bytes 442400 | tf_op jit(solution)/shard_map/ppermute | solution.py:53
  53.4 10.2 %project_attend_tail.1 = (bf16[256,768]{1,0:T(8,128)(2,1)S(1)}, bf16[768,1536]{1,0:T(8,128)(2,1)S(1)}, bf16[128,768]{1,0:T(8,128)(2,1)S(1)}) custom-call(s32[12]{0:T(128)S(1)} %stack.119.places_ref, s32[3,3]{1,0:T(4,128)S(1)} %copy-done.6, bf16[384,1536]{1,0:T(8,128)(2,1)} %normalize.1.normed_hbm.refs_12_, bf16[96,2304]{1,0:T(8,128)(2,1)} %get-tuple-element.32.refs_0_, ...), custom_call_target="tpu_custom_call" | custom-call | flops 10000000000 | bytes 1 | tf_op jit(solution)/shard_map/project_attend_tail/pallas_call | solution.py:404
  63.7 2.8 %collective-permute-start.16 = (bf16[128,768]{1,0:T(8,128)(2,1)S(1)}, bf16[128,768]{1,0:T(8,128)(2,1)S(1)}, u32[]{:S(2)}, u32[]{:S(2)}) collective-permute-start(bf16[128,768]{1,0:T(8,128)(2,1)S(1)} %get-tuple-element.47), channel_id=1, source_target_pairs={{0,1},{1,2},{2,3},{3,4},{4,5},{5,6},{6,7},{8,9},{9,10},{10,11},{11... | collective-permute-start | bytes 589832 | tf_op jit(solution)/shard_map/ppermute | solution.py:59
  66.6 3.7 %attend_main.1.attended_ref = f32[256,768]{1,0:T(8,128)S(1)} custom-call(s32[1]{0:T(128)} %bitcast.11.places_ref, s32[3,3]{1,0:T(4,128)S(1)} %copy-done.6, bf16[256,768]{1,0:T(8,128)(2,1)S(1)} %get-tuple-element.43.query_ref, bf16[768,1536]{1,0:T(8,128)(2,1)S(1)} %get-tuple-element.44.keyval_ref), custom_call_target="tpu_custom_call" | custom-call | flops 4000000000 | bytes 1 | tf_op jit(solution)/shard_map/attend_main/pallas_call | solution.py:442
  70.3 2.6 %collective-permute-done.16.received_ref = bf16[128,768]{1,0:T(8,128)(2,1)S(1)} collective-permute-done((bf16[128,768]{1,0:T(8,128)(2,1)S(1)}, bf16[128,768]{1,0:T(8,128)(2,1)S(1)}, u32[]{:S(2)}, u32[]{:S(2)}) %collective-permute-start.16) | collective-permute-done | bytes 196640 | tf_op jit(solution)/shard_map/ppermute | solution.py:59
  73.0 2.4 %blend_and_step.1 = bf16[256,1536]{1,0:T(8,128)(2,1)} custom-call(s32[6]{0:T(128)S(1)} %stack.99.places_ref, f32[4]{0:T(128)S(1)} %pad_maximum_fusion.coef_ref, f32[256,768]{1,0:T(8,128)S(1)} %attend_main.1.attended_ref, bf16[128,768]{1,0:T(8,128)(2,1)S(1)} %collective-permute-done.16.received_ref, bf16[256,1536]{1,0:T(8,128)(2,1)S(1)} %bitcast.36, ...), custom_call_target="tpu_custom_call" | custom-call | flops 3000000000 | bytes 1 | tf_op jit(solution)/shard_map/blend_and_step/pallas_call | solution.py:476
  (50 shorter events, 1.8 us)
Async XLA Ops:
  0.1 7.9 %copy-start.4 = (s32[1,64]{1,0:T(1,128)S(1)}, s32[1,64]{1,0:T(1,128)}, u32[]{:S(2)}) copy-start(s32[1,64]{1,0:T(1,128)} %ids_ref.1) | copy-start | bytes 772
  2.0 23.4 %collective-permute-start.1 = (bf16[96,2304]{1,0:T(8,128)(2,1)S(1)}, bf16[96,2304]{1,0:T(8,128)(2,1)S(1)}, u32[]{:S(2)}, u32[]{:S(2)}) collective-permute-start(bf16[96,2304]{1,0:T(8,128)(2,1)S(1)} %get-tuple-element.28), channel_id=1, source_target_pairs={{0,16},{8,24},{16,0},{24,8},{1,17},{9,25},{17,1},{25,9},{2,18},{10... | collective-permute-start | bytes 1327112 | tf_op jit(solution)/shard_map/ppermute | solution.py:53
  2.6 22.8 %collective-permute-start.2 = (bf16[96,2304]{1,0:T(8,128)(2,1)S(1)}, bf16[96,2304]{1,0:T(8,128)(2,1)}, u32[]{:S(2)}, u32[]{:S(2)}) collective-permute-start(bf16[96,2304]{1,0:T(8,128)(2,1)S(1)} %get-tuple-element.29), channel_id=1, source_target_pairs={{0,16},{8,24},{16,0},{24,8},{1,17},{9,25},{17,1},{25,9},{2,18},{10... | collective-permute-start | bytes 1327112 | tf_op jit(solution)/shard_map/ppermute | solution.py:53
  4.1 20.0 %collective-permute-start = (bf16[128,1536]{1,0:T(8,128)(2,1)S(1)}, bf16[128,1536]{1,0:T(8,128)(2,1)S(1)}, u32[]{:S(2)}, u32[]{:S(2)}) collective-permute-start(bf16[128,1536]{1,0:T(8,128)(2,1)S(1)} %get-tuple-element.27.after_ref), channel_id=1, source_target_pairs={{1,0},{2,1},{3,2},{4,3},{5,4},{6,5},{7,6},{9,8},{10,9},{11,10},{12... | collective-permute-start | bytes 1179656 | tf_op jit(solution)/shard_map/ppermute | solution.py:59
  7.4 25.7 %collective-permute-start.7 = (bf16[384,768]{1,0:T(8,128)(2,1)}, bf16[384,768]{1,0:T(8,128)(2,1)S(1)}, u32[]{:S(2)}, u32[]{:S(2)}) collective-permute-start(bf16[384,768]{1,0:T(8,128)(2,1)} %refs_8_.1), channel_id=1, source_target_pairs={{0,8},{8,0},{16,24},{24,16},{1,9},{9,1},{17,25},{25,17},{2,10},{10... | collective-permute-start | bytes 1769480 | tf_op jit(solution)/shard_map/ppermute | solution.py:53
  7.5 37.7 %collective-permute-start.8 = (bf16[384,1536]{1,0:T(8,128)(2,1)}, bf16[384,1536]{1,0:T(8,128)(2,1)}, u32[]{:S(2)}, u32[]{:S(2)}) collective-permute-start(bf16[384,1536]{1,0:T(8,128)(2,1)} %refs_10_.1), channel_id=1, source_target_pairs={{0,8},{8,0},{16,24},{24,16},{1,9},{9,1},{17,25},{25,17},{2,10},{10... | collective-permute-start | bytes 3538952 | tf_op jit(solution)/shard_map/ppermute | solution.py:53
  13.1 10.4 %all-to-all-start = ((f32[8,1,192]{2,1,0:T(1,128)}), f32[8,1,192]{2,1,0:T(1,128)S(1)}, u32[]{:S(2)}, u32[]{:S(2)}) async-start(f32[8,1,192]{2,1,0:T(1,128)} %copy.25), calls=%async_computation | async-start | bytes 16384 | tf_op jit(solution)/shard_map/all_to_all | solution.py:93
  24.9 7.6 %collective-permute-start.9 = (bf16[96,1536]{1,0:T(8,128)(2,1)S(1)}, bf16[96,1536]{1,0:T(8,128)(2,1)S(1)}, u32[]{:S(2)}, u32[]{:S(2)}) collective-permute-start(bf16[96,1536]{1,0:T(8,128)(2,1)S(1)} %get-tuple-element.34), channel_id=1, source_target_pairs={{0,16},{8,24},{16,0},{24,8},{1,17},{9,25},{17,1},{25,9},{2,18},{10... | collective-permute-start | bytes 884744 | tf_op jit(solution)/shard_map/ppermute | solution.py:53
  25.4 0.8 %copy-start.9 = (bf16[96,2304]{1,0:T(8,128)(2,1)}, bf16[96,2304]{1,0:T(8,128)(2,1)S(1)}, u32[]{:S(2)}) copy-start(bf16[96,2304]{1,0:T(8,128)(2,1)S(1)} %collective-permute-done.1.refs_2_) | copy-start | bytes 1327108
  26.2 6.2 %copy-start.10 = (bf16[96,2304]{1,0:T(8,128)(2,1)S(1)}, bf16[96,2304]{1,0:T(8,128)(2,1)}, u32[]{:S(2)}) copy-start(bf16[96,2304]{1,0:T(8,128)(2,1)} %get-tuple-element.32.refs_0_) | copy-start | bytes 1327108
  28.7 18.4 %collective-permute-start.10 = (bf16[384,1536]{1,0:T(8,128)(2,1)}, bf16[384,1536]{1,0:T(8,128)(2,1)}, u32[]{:S(2)}, u32[]{:S(2)}) collective-permute-start(bf16[384,1536]{1,0:T(8,128)(2,1)} %normalize.1.normed_hbm.refs_12_), channel_id=1, source_target_pairs={{0,16},{1,17},{2,18},{3,19},{4,20},{5,21},{6,22},{7,23}} | collective-permute-start | bytes 3538952 | tf_op jit(solution)/shard_map/ppermute | solution.py:502
  30.0 17.1 %collective-permute-start.11 = (bf16[384,1536]{1,0:T(8,128)(2,1)}, bf16[384,1536]{1,0:T(8,128)(2,1)}, u32[]{:S(2)}, u32[]{:S(2)}) collective-permute-start(bf16[384,1536]{1,0:T(8,128)(2,1)} %normalize.1.normed_hbm.refs_12_), channel_id=1, source_target_pairs={{0,8},{1,9},{2,10},{3,11},{4,12},{5,13},{6,14},{7,15}} | collective-permute-start | bytes 3538952 | tf_op jit(solution)/shard_map/ppermute | solution.py:502
  32.5 14.7 %copy-start.2 = (bf16[96,1536]{1,0:T(8,128)(2,1)}, bf16[96,1536]{1,0:T(8,128)(2,1)S(1)}, u32[]{:S(2)}) copy-start(bf16[96,1536]{1,0:T(8,128)(2,1)S(1)} %collective-permute-done.9.refs_6_) | copy-start | bytes 884740
  32.5 10.1 %collective-permute-start.3 = (bf16[96,2304]{1,0:T(8,128)(2,1)S(1)}, bf16[96,2304]{1,0:T(8,128)(2,1)}, u32[]{:S(2)}, u32[]{:S(2)}) collective-permute-start(bf16[96,2304]{1,0:T(8,128)(2,1)S(1)} %copy-done.10), channel_id=1, source_target_pairs={{0,1},{1,0},{2,3},{3,2},{4,5},{5,4},{6,7},{7,6},{8,9},{9,8},{10,11... | collective-permute-start | bytes 1327112 | tf_op jit(solution)/shard_map/ppermute | solution.py:53
  33.1 9.9 %copy-start.7 = (bf16[384,768]{1,0:T(8,128)(2,1)}, bf16[384,768]{1,0:T(8,128)(2,1)S(1)}, u32[]{:S(2)}) copy-start(bf16[384,768]{1,0:T(8,128)(2,1)S(1)} %collective-permute-done.7.refs_4_) | copy-start | bytes 1769476
  33.1 9.9 %collective-permute-start.4 = (bf16[96,2304]{1,0:T(8,128)(2,1)S(1)}, bf16[96,2304]{1,0:T(8,128)(2,1)}, u32[]{:S(2)}, u32[]{:S(2)}) collective-permute-start(bf16[96,2304]{1,0:T(8,128)(2,1)S(1)} %copy-done.10), channel_id=1, source_target_pairs={{0,2},{1,3},{2,0},{3,1},{4,6},{5,7},{6,4},{7,5},{8,10},{9,11},{10,... | collective-permute-start | bytes 1327112 | tf_op jit(solution)/shard_map/ppermute | solution.py:53
  42.6 1.9 %collective-permute-start.5 = (bf16[96,2304]{1,0:T(8,128)(2,1)S(1)}, bf16[96,2304]{1,0:T(8,128)(2,1)}, u32[]{:S(2)}, u32[]{:S(2)}) collective-permute-start(bf16[96,2304]{1,0:T(8,128)(2,1)S(1)} %copy-done.10), channel_id=1, source_target_pairs={{0,8},{8,0},{16,24},{24,16},{1,9},{9,1},{17,25},{25,17},{2,10},{10... | collective-permute-start | bytes 1327112 | tf_op jit(solution)/shard_map/ppermute | solution.py:53
  43.0 6.1 %copy-start.1 = (bf16[192,1536]{1,0:T(8,128)(2,1)S(1)}, bf16[192,1536]{1,0:T(8,128)(2,1)}, u32[]{:S(2)}) copy-start(bf16[192,1536]{1,0:T(8,128)(2,1)} %refs_0_.1) | copy-start | bytes 1769476
  43.0 10.4 %copy-start.6 = (s32[3,3]{1,0:T(4,128)S(1)}, s32[3,3]{1,0:T(4,128)}, u32[]{:S(2)}) copy-start(s32[3,3]{1,0:T(4,128)} %table_ref.3) | copy-start | bytes 112
  43.0 2.3 %collective-permute-start.6 = (bf16[96,2304]{1,0:T(8,128)(2,1)}, bf16[96,2304]{1,0:T(8,128)(2,1)S(1)}, u32[]{:S(2)}, u32[]{:S(2)}) collective-permute-start(bf16[96,2304]{1,0:T(8,128)(2,1)} %get-tuple-element.33.refs_3_), channel_id=1, source_target_pairs={{0,8},{8,0},{16,24},{24,16},{1,9},{9,1},{17,25},{25,17},{2,10},{10... | collective-permute-start | bytes 1327112 | tf_op jit(solution)/shard_map/ppermute | solution.py:53
  45.3 1.9 %copy-start.8 = (bf16[96,2304]{1,0:T(8,128)(2,1)}, bf16[96,2304]{1,0:T(8,128)(2,1)S(1)}, u32[]{:S(2)}) copy-start(bf16[96,2304]{1,0:T(8,128)(2,1)S(1)} %collective-permute-done.6.refs_3_) | copy-start | bytes 1327108
  47.1 6.2 %collective-permute-start.14 = (bf16[384,1536]{1,0:T(8,128)(2,1)}, bf16[384,1536]{1,0:T(8,128)(2,1)S(1)}, u32[]{:S(2)}, u32[]{:S(2)}) collective-permute-start(bf16[384,1536]{1,0:T(8,128)(2,1)} %get-tuple-element.41.refs_13_), channel_id=1, source_target_pairs={{16,24},{17,25},{18,26},{19,27},{20,28},{21,29},{22,30},{23,31}} | collective-permute-start | bytes 3538952 | tf_op jit(solution)/shard_map/ppermute | solution.py:515
  48.5 4.5 %collective-permute-start.12 = (bf16[96,2304]{1,0:T(8,128)(2,1)}, bf16[96,2304]{1,0:T(8,128)(2,1)S(1)}, u32[]{:S(2)}, u32[]{:S(2)}) collective-permute-start(bf16[96,2304]{1,0:T(8,128)(2,1)} %get-tuple-element.35.refs_1_), channel_id=1, source_target_pairs={{0,8},{8,0},{16,24},{24,16},{1,9},{9,1},{17,25},{25,17},{2,10},{10... | collective-permute-start | bytes 1327112 | tf_op jit(solution)/shard_map/ppermute | solution.py:53
  48.6 4.8 %collective-permute-start.13 = (bf16[96,2304]{1,0:T(8,128)(2,1)}, bf16[96,2304]{1,0:T(8,128)(2,1)}, u32[]{:S(2)}, u32[]{:S(2)}) collective-permute-start(bf16[96,2304]{1,0:T(8,128)(2,1)} %get-tuple-element.36.refs_2_), channel_id=1, source_target_pairs={{0,8},{8,0},{16,24},{24,16},{1,9},{9,1},{17,25},{25,17},{2,10},{10... | collective-permute-start | bytes 1327112 | tf_op jit(solution)/shard_map/ppermute | solution.py:53
  49.1 21.2 %collective-permute-start.17 = (bf16[192,1536]{1,0:T(8,128)(2,1)S(1)}, bf16[192,1536]{1,0:T(8,128)(2,1)S(1)}, u32[]{:S(2)}, u32[]{:S(2)}) collective-permute-start(bf16[192,1536]{1,0:T(8,128)(2,1)S(1)} %copy-done.1), channel_id=1, source_target_pairs={{0,8},{8,0},{16,24},{24,16},{1,9},{9,1},{17,25},{25,17},{2,10},{10... | collective-permute-start | bytes 1769480 | tf_op jit(solution)/shard_map/ppermute | solution.py:53
  50.1 13.6 %collective-permute-start.15 = (bf16[96,1536]{1,0:T(8,128)(2,1)}, bf16[96,1536]{1,0:T(8,128)(2,1)S(1)}, u32[]{:S(2)}, u32[]{:S(2)}) collective-permute-start(bf16[96,1536]{1,0:T(8,128)(2,1)} %get-tuple-element.46.refs_2_), channel_id=1, source_target_pairs={{0,1},{1,0},{2,3},{3,2},{4,5},{5,4},{6,7},{7,6},{8,9},{9,8},{10,11... | collective-permute-start | bytes 884744 | tf_op jit(solution)/shard_map/ppermute | solution.py:53
  53.0 17.3 %collective-permute-start.18 = (bf16[96,1536]{1,0:T(8,128)(2,1)}, bf16[96,1536]{1,0:T(8,128)(2,1)S(1)}, u32[]{:S(2)}, u32[]{:S(2)}) collective-permute-start(bf16[96,1536]{1,0:T(8,128)(2,1)} %get-tuple-element.46.refs_2_), channel_id=1, source_target_pairs={{0,8},{8,0},{16,24},{24,16},{1,9},{9,1},{17,25},{25,17},{2,10},{10... | collective-permute-start | bytes 884744 | tf_op jit(solution)/shard_map/ppermute | solution.py:53
  63.7 9.3 %collective-permute-start.16 = (bf16[128,768]{1,0:T(8,128)(2,1)S(1)}, bf16[128,768]{1,0:T(8,128)(2,1)S(1)}, u32[]{:S(2)}, u32[]{:S(2)}) collective-permute-start(bf16[128,768]{1,0:T(8,128)(2,1)S(1)} %get-tuple-element.47), channel_id=1, source_target_pairs={{0,1},{1,2},{2,3},{3,4},{4,5},{5,6},{6,7},{8,9},{9,10},{10,11},{11... | collective-permute-start | bytes 589832 | tf_op jit(solution)/shard_map/ppermute | solution.py:59
  66.5 6.5 %collective-permute-start.19 = (bf16[96,1536]{1,0:T(8,128)(2,1)S(1)}, bf16[96,1536]{1,0:T(8,128)(2,1)S(1)}, u32[]{:S(2)}, u32[]{:S(2)}) collective-permute-start(bf16[96,1536]{1,0:T(8,128)(2,1)S(1)} %get-tuple-element.48.refs_3_), channel_id=1, source_target_pairs={{0,8},{8,0},{16,24},{24,16},{1,9},{9,1},{17,25},{25,17},{2,10},{10... | collective-permute-start | bytes 884744 | tf_op jit(solution)/shard_map/ppermute | solution.py:53
  66.6 6.4 %copy-start = (bf16[1,256,1536]{2,1,0:T(8,128)(2,1)S(1)}, bf16[1,256,1536]{2,1,0:T(8,128)(2,1)}, u32[]{:S(2)}) copy-start(bf16[1,256,1536]{2,1,0:T(8,128)(2,1)} %param.9) | copy-start | bytes 2359300
  66.6 6.4 %copy-start.3 = (bf16[96,1536]{1,0:T(8,128)(2,1)S(1)}, bf16[96,1536]{1,0:T(8,128)(2,1)}, u32[]{:S(2)}) copy-start(bf16[96,1536]{1,0:T(8,128)(2,1)} %get-tuple-element.46.refs_2_) | copy-start | bytes 884740
  66.6 6.4 %copy-start.5 = (bf16[1,256,1536]{2,1,0:T(8,128)(2,1)S(1)}, bf16[1,256,1536]{2,1,0:T(8,128)(2,1)}, u32[]{:S(2)}) copy-start(bf16[1,256,1536]{2,1,0:T(8,128)(2,1)} %param.10) | copy-start | bytes 2359300
  (1 other events, 0.7 us)

commit v6 on v5

--- a/solution.py
+++ b/solution.py
@@ -391,7 +391,7 @@
 
 
 def project(
-    choice, last, block_table, normed, wide, wide_places, queries, keyvals, pair_places, sources
+    places, block_table, normed, wide, queries, keyvals, sources
 ):
     window_rows, width = normed.shape
     keyval_width = keyvals[0].shape[1]
@@ -421,7 +421,7 @@
         cost_estimate=cost(10 * MICROSECOND),
         name="project_attend_tail",
     )(
-        numbers(choice, last, *wide_places, *pair_places),
+        places,
         block_table,
         *arrays,
     )
@@ -483,7 +483,7 @@
         cost_estimate=cost(3 * MICROSECOND),
         name="blend_and_step",
     )(
-        numbers(*places),
+        places,
         coefs,
         attended,
         received,
@@ -504,16 +504,24 @@
 
 def passed_on(value, arrivals):
     count = lax.axis_size("var")
-    place = lax.axis_index("var")
-    arrays, choice = [value, arrivals[0][0]], (place == arrivals[0][1]).astype(jnp.int32)
+    arrays = [value, arrivals[0][0]]
     for array, bit in arrivals[1:]:
         payload = functools.reduce(jnp.add, arrays[1:])
         route = [(i, i + bit) for i in range(2 * bit, count, 2 * bit)]
-        choice = jnp.where(place == bit, len(arrays), choice)
         arrays.append(array)
-        choice = jnp.where((place > bit) & (place % (2 * bit) == bit), len(arrays), choice)
         arrays.append(lax.ppermute(payload, "var", route))
-    return arrays, choice
+    return arrays
+
+
+def held_by(place):
+    bit = lax.axis_size("var") // 2
+    choice, count = (place == bit).astype(jnp.int32), 2
+    while bit > 1:
+        bit //= 2
+        choice = jnp.where(place == bit, count, choice)
+        choice = jnp.where((place > bit) & (place % (2 * bit) == bit), count + 1, choice)
+        count += 2
+    return choice
 
 
 def local(
@@ -539,16 +547,30 @@
     )
     pooled = pool(prompt_ids, prompt_table, halo_rows)
     halo = shifted(halo_rows, "tm", -1)
+    current, coef_latent, coef_pred, spread = coefficients(timestep)
+    last = tm_place == tm_count - 1
+    coefs = jnp.stack([coef_latent, coef_pred, spread, (tm_place == 0).astype(F32)])
     pooled = whole_rows(pooled)
     if routed:
         quarter = rows // 4
         first = swapped(cuts[0], "var", 2)
         fourth = swapped(cuts[1], "var", 2)
+        here, there = (var_place ^ 2) * rows, (var_place ^ 3) * rows
+        places = [here + (corner ^ k) * quarter for k in range(4)]
+        places += [there + (corner ^ k) * quarter for k in (0, 3, 1, 2)]
+        places += [var_place * rows, (var_place ^ 1) * rows]
+        out_rows = w_out.shape[0]
+        half = out_rows // 2
+        out_places = [var_place * out_rows, (var_place ^ 1) * out_rows]
+        out_places += [(var_place ^ 2) * out_rows + place * half for place in (side, 1 - side)]
+        out_places += [(var_place ^ 3) * out_rows + place * half for place in (side, 1 - side)]
+        coefs, places, out_places, pooled = together(
+            coefs, numbers(held_by(var_place), last, *places), numbers(*out_places), pooled
+        )
         halo, pooled, first, fourth = together(
             halo, pooled, first, fourth, limit=ALL_VMEM
         )
 
-    current, coef_latent, coef_pred, spread = coefficients(timestep)
     normed = normalized(latent, halo, pooled, time_waves(current, model_width))
     sources = from_source(normed)
     if routed:
@@ -558,51 +580,30 @@
         fetched = [second, third]
         fetched += [swapped(piece, "var", 1) for piece in (first, fourth, w_query, w_keyval)]
         fetched += [swapped(out_cut, "var", 2)] + [array for array, _ in sources]
-        second, third, first_over, fourth_over, partner_query, partner_keyval, *fetched = together(
-            *fetched, limit=ALL_VMEM
-        )
+        fetched = together(*fetched, limit=ALL_VMEM)
+        second, third, first_over, fourth_over, partner_query, partner_keyval, *fetched = fetched
         out_first, *fetched = fetched
         sources = [(array, bit) for array, (_, bit) in zip(fetched, sources)]
 
         wide = [first, second, third, fourth, first_over, fourth_over]
         wide += [swapped(second, "var", 1), swapped(third, "var", 1)]
-        here, there = (var_place ^ 2) * rows, (var_place ^ 3) * rows
-        wide_places = [here + (corner ^ k) * quarter for k in range(4)]
-        wide_places += [there + (corner ^ k) * quarter for k in (0, 3, 1, 2)]
         queries, keyvals = [w_query, partner_query], [w_keyval, partner_keyval]
-        pair_places = [var_place * rows, (var_place ^ 1) * rows]
     else:
-        wide, wide_places, pair_places = [], [], [0]
+        wide = []
         queries = [lax.all_gather(w_query, "var", axis=0, tiled=True)]
         keyvals = [lax.all_gather(w_keyval, "var", axis=0, tiled=True)]
-    sources, choice = passed_on(normed, sources)
-    last = tm_place == tm_count - 1
-    query, keyval, tail = project(
-        choice,
-        last,
-        block_table,
-        normed,
-        wide,
-        wide_places,
-        queries,
-        keyvals,
-        pair_places,
-        sources,
-    )
+        places = numbers(held_by(var_place), last, 0)
+        out_places = numbers(0)
+    sources = passed_on(normed, sources)
+    query, keyval, tail = project(places, block_table, normed, wide, queries, keyvals, sources)
     if routed:
         tail, out_second = together(tail, swapped(out_first, "tm", 1))
-        out_rows = w_out.shape[0]
-        half = out_rows // 2
         out_pieces = [w_out, swapped(w_out, "var", 1), out_first, out_second]
         out_pieces += [swapped(out_first, "var", 1), swapped(out_second, "var", 1)]
-        out_places = [var_place * out_rows, (var_place ^ 1) * out_rows]
-        out_places += [(var_place ^ 2) * out_rows + place * half for place in (side, 1 - side)]
-        out_places += [(var_place ^ 3) * out_rows + place * half for place in (side, 1 - side)]
     else:
-        out_pieces, out_places = [lax.all_gather(w_out, "var", axis=0, tiled=True)], [0]
+        out_pieces = [lax.all_gather(w_out, "var", axis=0, tiled=True)]
     received = shifted(tail, "tm", 1)
     attended = attend_main(last, block_table, query, keyval)
-    coefs = jnp.stack([coef_latent, coef_pred, spread, (tm_place == 0).astype(F32)])
     return finish(coefs, attended, received, latent, fresh_noise[0], out_pieces, out_places)[None]
 
 

time: 75.7 us -> 75.7 us (level)
    ppermute x15, waiting for transfers between devices: 13.5 us -> 14.5 us  [swapped(): return lax.ppermute(block, axis, route)]
    all_to_all x1, waiting for transfers between devices: 4.24 us -> 3.41 us  [whole_rows(): arrived = lax.all_to_all(sent, 'tm', 0, 0, tiled=True)]
  transfers between devices with their start and end apart: 21 -> 21, of which waited for: 9 -> 10; matrix products, arithmetic and copies ran while one was open for 2% -> 1% of each run, Pallas kernels for 28% -> 28%
where the time goes in v6:
time: 75.7 us; the launch traced here: 75.3 us
  Pallas kernels  25.1 us (33%)
  starting transfers between devices  22.9 us (30%)
  waiting for transfers between devices  22.7 us (30%)
  local copies, waits for them, and re-layouts  2.92 us (4%)
  between operations  1.45 us (2%)
    ppermute x15, waiting for transfers between devices, swapped(): return lax.ppermute(block, axis, route)  14.5 us
    pallas_call x1, Pallas kernels, project(): pl.pallas_call(functools.partial(project_kernel, len(wide), len(queries),...  10.1 us
    ppermute x15, starting transfers between devices, swapped(): return lax.ppermute(block, axis, route)  7.12 us
    ppermute x2, starting transfers between devices, shifted(): return lax.ppermute(block, axis, route)  6.01 us
    all_to_all x1, starting transfers between devices, whole_rows(): arrived = lax.all_to_all(sent, 'tm', 0, 0, tiled=True)  5.4 us
    pallas_call x1, Pallas kernels, pool(): pl.pallas_call(pool_kernel, out_shape=jax.ShapeDtypeStruct((8, table_colu...  4.52 us
    pallas_call x1, Pallas kernels, attend_main(): pl.pallas_call(main_kernel, out_shape=jax.ShapeDtypeStruct((rows, width),...  3.68 us
    all_to_all x1, waiting for transfers between devices, whole_rows(): arrived = lax.all_to_all(sent, 'tm', 0, 0, tiled=True)  3.41 us
  transfers between devices with their start and end apart: 21, of which 10 were waited for; matrix products, arithmetic and copies ran while one was open for 1% of the time, Pallas kernels for 28%

profile of v6, /device:TPU:10, one launch (start us, length us, event | category | flops | bytes accessed | tf_op | source)
XLA Modules:
  0.0 75.3 jit_solution(7940730900966360393)
XLA Ops:
  0.1 1.9 %first_rows.1 = (bf16[128,1536]{1,0:T(8,128)(2,1)S(1)}, bf16[96,1536]{1,0:T(8,128)(2,1)S(1)}, bf16[96,2304]{1,0:T(8,128)(2,1)S(1)}, bf16[96,2304]{1,0:T(8,128)(2,1)S(1)}) custom-call(s32[3]{0:T(128)S(1)} %pad_add_fusion.places_ref, bf16[384,768]{1,0:T(8,128)(2,1)} %refs_8_.1, bf16[384,1536]{1,0:T(8,128)(2,1)} %refs_10_.1, bf16[192,1536]{1,0:T(8,128)(2,1)} %refs_0_.1, ...), custom_call_target="tpu_custom_call" | custom-call | flops 1 | bytes 1 | tf_op jit(solution)/shard_map/first_rows/pallas_call | solution.py:169
  2.0 0.6 collective-permute-start.1
  2.6 1.5 %collective-permute-start.2 = (bf16[96,2304]{1,0:T(8,128)(2,1)S(1)}, bf16[96,2304]{1,0:T(8,128)(2,1)}, u32[]{:S(2)}, u32[]{:S(2)}) collective-permute-start(bf16[96,2304]{1,0:T(8,128)(2,1)S(1)} %get-tuple-element.37), channel_id=1, source_target_pairs={{0,16},{8,24},{16,0},{24,8},{1,17},{9,25},{17,1},{25,9},{2,18},{10... | collective-permute-start | bytes 1327112 | tf_op jit(solution)/shard_map/ppermute | solution.py:53
  4.1 3.3 %collective-permute-start = (bf16[128,1536]{1,0:T(8,128)(2,1)S(1)}, bf16[128,1536]{1,0:T(8,128)(2,1)S(1)}, u32[]{:S(2)}, u32[]{:S(2)}) collective-permute-start(bf16[128,1536]{1,0:T(8,128)(2,1)S(1)} %get-tuple-element.31.after_ref), channel_id=1, source_target_pairs={{1,0},{2,1},{3,2},{4,3},{5,4},{6,5},{7,6},{9,8},{10,9},{11,10},{12... | collective-permute-start | bytes 1179656 | tf_op jit(solution)/shard_map/ppermute | solution.py:59
  7.5 0.5 collective-permute-start.8
  8.0 4.5 %pool_prompt.1 = f32[8,192]{1,0:T(8,128)S(1)} custom-call(s32[1,64]{1,0:T(1,128)S(1)} %copy-done.5, bf16[192,16384]{1,0:T(8,128)(2,1)} %bitcast.40, bf16[128,1536]{1,0:T(8,128)(2,1)S(1)} %get-tuple-element.31.after_ref), custom_call_target="tpu_custom_call" | custom-call | flops 1 | bytes 1 | tf_op jit(solution)/shard_map/pool_prompt/pallas_call | solution.py:126
  12.5 0.6 copy.29
  13.1 5.4 %all-to-all-start = ((f32[8,1,192]{2,1,0:T(1,128)}), f32[8,1,192]{2,1,0:T(1,128)S(1)}, u32[]{:S(2)}, u32[]{:S(2)}) async-start(f32[8,1,192]{2,1,0:T(1,128)} %copy.29), calls=%async_computation | async-start | bytes 16384 | tf_op jit(solution)/shard_map/all_to_all | solution.py:93
  20.2 3.4 %all-to-all-done = f32[8,1,192]{2,1,0:T(1,128)S(1)} async-done(((f32[8,1,192]{2,1,0:T(1,128)}), f32[8,1,192]{2,1,0:T(1,128)S(1)}, u32[]{:S(2)}, u32[]{:S(2)}) %all-to-all-start) | async-done | bytes 6176 | tf_op jit(solution)/shard_map/all_to_all | solution.py:93
  23.6 0.6 copy-done.4
  24.2 0.7 copy-done.11
  24.9 0.5 collective-permute-start.9
  25.5 0.8 %copy-done.9 = bf16[96,2304]{1,0:T(8,128)(2,1)} copy-done((bf16[96,2304]{1,0:T(8,128)(2,1)}, bf16[96,2304]{1,0:T(8,128)(2,1)S(1)}, u32[]{:S(2)}) %copy-start.9) | copy-done | bytes 442392
  26.2 2.4 %normalize.1.normed_hbm.refs_12_ = bf16[384,1536]{1,0:T(8,128)(2,1)} custom-call(bf16[256,1536]{1,0:T(8,128)(2,1)} %bitcast.35, bf16[128,1536]{1,0:T(8,128)(2,1)} %get-tuple-element.38.halo_ref, f32[8,192]{1,0:T(8,128)} %get-tuple-element.39.rows_ref, f32[1,768]{1,0:T(1,128)S(1)} %get-tuple-element.58.cos_ref, f32[1,768]{1,0:T(1,128)S(1)} %get-tuple-element.57.sin_ref), custom_call_target="tpu_custom_call" | custom-call | flops 1000000000 | bytes 1 | tf_op jit(solution)/shard_map/normalize/pallas_call | solution.py:281
  28.7 1.3 %collective-permute-start.10 = (bf16[384,1536]{1,0:T(8,128)(2,1)}, bf16[384,1536]{1,0:T(8,128)(2,1)}, u32[]{:S(2)}, u32[]{:S(2)}) collective-permute-start(bf16[384,1536]{1,0:T(8,128)(2,1)} %normalize.1.normed_hbm.refs_12_), channel_id=1, source_target_pairs={{0,16},{1,17},{2,18},{3,19},{4,20},{5,21},{6,22},{7,23}} | collective-permute-start | bytes 3538952 | tf_op jit(solution)/shard_map/ppermute | solution.py:502
  30.0 1.7 %collective-permute-start.11 = (bf16[384,1536]{1,0:T(8,128)(2,1)}, bf16[384,1536]{1,0:T(8,128)(2,1)}, u32[]{:S(2)}, u32[]{:S(2)}) collective-permute-start(bf16[384,1536]{1,0:T(8,128)(2,1)} %normalize.1.normed_hbm.refs_12_), channel_id=1, source_target_pairs={{0,8},{1,9},{2,10},{3,11},{4,12},{5,13},{6,14},{7,15}} | collective-permute-start | bytes 3538952 | tf_op jit(solution)/shard_map/ppermute | solution.py:502
  31.6 0.8 %collective-permute-done.9.refs_6_ = bf16[96,1536]{1,0:T(8,128)(2,1)S(1)} collective-permute-done((bf16[96,1536]{1,0:T(8,128)(2,1)S(1)}, bf16[96,1536]{1,0:T(8,128)(2,1)S(1)}, u32[]{:S(2)}, u32[]{:S(2)}) %collective-permute-start.9) | collective-permute-done | bytes 294944 | tf_op jit(solution)/shard_map/ppermute | solution.py:53
  32.5 0.6 collective-permute-start.3
  33.1 1.4 %collective-permute-start.4 = (bf16[96,2304]{1,0:T(8,128)(2,1)S(1)}, bf16[96,2304]{1,0:T(8,128)(2,1)}, u32[]{:S(2)}, u32[]{:S(2)}) collective-permute-start(bf16[96,2304]{1,0:T(8,128)(2,1)S(1)} %copy-done.10), channel_id=1, source_target_pairs={{0,2},{1,3},{2,0},{3,1},{4,6},{5,7},{6,4},{7,5},{8,10},{9,11},{10,... | collective-permute-start | bytes 1327112 | tf_op jit(solution)/shard_map/ppermute | solution.py:53
  34.5 8.0 %collective-permute-done.3.refs_0_ = bf16[96,2304]{1,0:T(8,128)(2,1)} collective-permute-done((bf16[96,2304]{1,0:T(8,128)(2,1)S(1)}, bf16[96,2304]{1,0:T(8,128)(2,1)}, u32[]{:S(2)}, u32[]{:S(2)}) %collective-permute-start.3) | collective-permute-done | bytes 442400 | tf_op jit(solution)/shard_map/ppermute | solution.py:53
  43.1 1.4 %collective-permute-done.5.refs_2_ = bf16[96,2304]{1,0:T(8,128)(2,1)} collective-permute-done((bf16[96,2304]{1,0:T(8,128)(2,1)S(1)}, bf16[96,2304]{1,0:T(8,128)(2,1)}, u32[]{:S(2)}, u32[]{:S(2)}) %collective-permute-start.5) | collective-permute-done | bytes 442400 | tf_op jit(solution)/shard_map/ppermute | solution.py:53
  44.5 0.8 %collective-permute-done.6.refs_3_ = bf16[96,2304]{1,0:T(8,128)(2,1)} collective-permute-done((bf16[96,2304]{1,0:T(8,128)(2,1)}, bf16[96,2304]{1,0:T(8,128)(2,1)}, u32[]{:S(2)}, u32[]{:S(2)}) %collective-permute-start.6) | collective-permute-done | bytes 442400 | tf_op jit(solution)/shard_map/ppermute | solution.py:53
  45.3 1.7 %collective-permute-done.10.refs_7_ = bf16[384,1536]{1,0:T(8,128)(2,1)} collective-permute-done((bf16[384,1536]{1,0:T(8,128)(2,1)}, bf16[384,1536]{1,0:T(8,128)(2,1)}, u32[]{:S(2)}, u32[]{:S(2)}) %collective-permute-start.10) | collective-permute-done | bytes 1179680 | tf_op jit(solution)/shard_map/ppermute | solution.py:502
  47.1 1.4 %collective-permute-start.14 = (bf16[384,1536]{1,0:T(8,128)(2,1)}, bf16[384,1536]{1,0:T(8,128)(2,1)S(1)}, u32[]{:S(2)}, u32[]{:S(2)}) collective-permute-start(bf16[384,1536]{1,0:T(8,128)(2,1)} %get-tuple-element.49.refs_13_), channel_id=1, source_target_pairs={{16,24},{17,25},{18,26},{19,27},{20,28},{21,29},{22,30},{23,31}} | collective-permute-start | bytes 3538952 | tf_op jit(solution)/shard_map/ppermute | solution.py:512
  48.5 0.5 collective-permute-start.13
  49.1 0.6 collective-permute-start.15
  49.7 2.6 %collective-permute-done.12.refs_6_ = bf16[96,2304]{1,0:T(8,128)(2,1)S(1)} collective-permute-done((bf16[96,2304]{1,0:T(8,128)(2,1)}, bf16[96,2304]{1,0:T(8,128)(2,1)S(1)}, u32[]{:S(2)}, u32[]{:S(2)}) %collective-permute-start.12) | collective-permute-done | bytes 442400 | tf_op jit(solution)/shard_map/ppermute | solution.py:53
  53.2 10.1 %project_attend_tail.1 = (bf16[256,768]{1,0:T(8,128)(2,1)S(1)}, bf16[768,1536]{1,0:T(8,128)(2,1)S(1)}, bf16[128,768]{1,0:T(8,128)(2,1)S(1)}) custom-call(s32[12]{0:T(128)S(1)} %get-tuple-element.34.places_ref, s32[3,3]{1,0:T(4,128)S(1)} %copy-done.7, bf16[384,1536]{1,0:T(8,128)(2,1)} %normalize.1.normed_hbm.refs_12_, ...), custom_call_target="tpu_custom_call" | custom-call | flops 10000000000 | bytes 1 | tf_op jit(solution)/shard_map/project_attend_tail/pallas_call | solution.py:404
  63.3 2.7 %collective-permute-start.16 = (bf16[128,768]{1,0:T(8,128)(2,1)S(1)}, bf16[128,768]{1,0:T(8,128)(2,1)S(1)}, u32[]{:S(2)}, u32[]{:S(2)}) collective-permute-start(bf16[128,768]{1,0:T(8,128)(2,1)S(1)} %get-tuple-element.55), channel_id=1, source_target_pairs={{0,1},{1,2},{2,3},{3,4},{4,5},{5,6},{6,7},{8,9},{9,10},{10,11},{11... | collective-permute-start | bytes 589832 | tf_op jit(solution)/shard_map/ppermute | solution.py:59
  66.2 3.7 %attend_main.1.attended_ref = f32[256,768]{1,0:T(8,128)S(1)} custom-call(s32[1]{0:T(128)} %bitcast.6.places_ref, s32[3,3]{1,0:T(4,128)S(1)} %copy-done.7, bf16[256,768]{1,0:T(8,128)(2,1)S(1)} %get-tuple-element.51.query_ref, bf16[768,1536]{1,0:T(8,128)(2,1)S(1)} %get-tuple-element.52.keyval_ref), custom_call_target="tpu_custom_call" | custom-call | flops 4000000000 | bytes 1 | tf_op jit(solution)/shard_map/attend_main/pallas_call | solution.py:442
  69.9 3.1 %collective-permute-done.16.received_ref = bf16[128,768]{1,0:T(8,128)(2,1)S(1)} collective-permute-done((bf16[128,768]{1,0:T(8,128)(2,1)S(1)}, bf16[128,768]{1,0:T(8,128)(2,1)S(1)}, u32[]{:S(2)}, u32[]{:S(2)}) %collective-permute-start.16) | collective-permute-done | bytes 196640 | tf_op jit(solution)/shard_map/ppermute | solution.py:59
  72.9 2.4 %blend_and_step.1 = bf16[256,1536]{1,0:T(8,128)(2,1)} custom-call(s32[6]{0:T(128)S(1)} %get-tuple-element.32.places_ref, f32[4]{0:T(128)S(1)} %get-tuple-element.33.coef_ref, f32[256,768]{1,0:T(8,128)S(1)} %attend_main.1.attended_ref, bf16[128,768]{1,0:T(8,128)(2,1)S(1)} %collective-permute-done.16.received_ref, bf16[256,1536]{1,0:T(8,128)(2,1)S(1)} %bitcast.36, ...), custom_call_target="tpu_custom_call" | custom-call | flops 3000000000 | bytes 1 | tf_op jit(solution)/shard_map/blend_and_step/pallas_call | solution.py:476
  (51 shorter events, 2.2 us)
Async XLA Ops:
  0.1 7.9 %copy-start.5 = (s32[1,64]{1,0:T(1,128)S(1)}, s32[1,64]{1,0:T(1,128)}, u32[]{:S(2)}) copy-start(s32[1,64]{1,0:T(1,128)} %ids_ref.1) | copy-start | bytes 772
  2.0 23.4 %collective-permute-start.1 = (bf16[96,2304]{1,0:T(8,128)(2,1)S(1)}, bf16[96,2304]{1,0:T(8,128)(2,1)S(1)}, u32[]{:S(2)}, u32[]{:S(2)}) collective-permute-start(bf16[96,2304]{1,0:T(8,128)(2,1)S(1)} %get-tuple-element.36), channel_id=1, source_target_pairs={{0,16},{8,24},{16,0},{24,8},{1,17},{9,25},{17,1},{25,9},{2,18},{10... | collective-permute-start | bytes 1327112 | tf_op jit(solution)/shard_map/ppermute | solution.py:53
  2.6 22.8 %collective-permute-start.2 = (bf16[96,2304]{1,0:T(8,128)(2,1)S(1)}, bf16[96,2304]{1,0:T(8,128)(2,1)}, u32[]{:S(2)}, u32[]{:S(2)}) collective-permute-start(bf16[96,2304]{1,0:T(8,128)(2,1)S(1)} %get-tuple-element.37), channel_id=1, source_target_pairs={{0,16},{8,24},{16,0},{24,8},{1,17},{9,25},{17,1},{25,9},{2,18},{10... | collective-permute-start | bytes 1327112 | tf_op jit(solution)/shard_map/ppermute | solution.py:53
  4.1 20.0 %collective-permute-start = (bf16[128,1536]{1,0:T(8,128)(2,1)S(1)}, bf16[128,1536]{1,0:T(8,128)(2,1)S(1)}, u32[]{:S(2)}, u32[]{:S(2)}) collective-permute-start(bf16[128,1536]{1,0:T(8,128)(2,1)S(1)} %get-tuple-element.31.after_ref), channel_id=1, source_target_pairs={{1,0},{2,1},{3,2},{4,3},{5,4},{6,5},{7,6},{9,8},{10,9},{11,10},{12... | collective-permute-start | bytes 1179656 | tf_op jit(solution)/shard_map/ppermute | solution.py:59
  7.4 25.7 %collective-permute-start.7 = (bf16[384,768]{1,0:T(8,128)(2,1)}, bf16[384,768]{1,0:T(8,128)(2,1)S(1)}, u32[]{:S(2)}, u32[]{:S(2)}) collective-permute-start(bf16[384,768]{1,0:T(8,128)(2,1)} %refs_8_.1), channel_id=1, source_target_pairs={{0,8},{8,0},{16,24},{24,16},{1,9},{9,1},{17,25},{25,17},{2,10},{10... | collective-permute-start | bytes 1769480 | tf_op jit(solution)/shard_map/ppermute | solution.py:53
  7.5 37.8 %collective-permute-start.8 = (bf16[384,1536]{1,0:T(8,128)(2,1)}, bf16[384,1536]{1,0:T(8,128)(2,1)}, u32[]{:S(2)}, u32[]{:S(2)}) collective-permute-start(bf16[384,1536]{1,0:T(8,128)(2,1)} %refs_10_.1), channel_id=1, source_target_pairs={{0,8},{8,0},{16,24},{24,16},{1,9},{9,1},{17,25},{25,17},{2,10},{10... | collective-permute-start | bytes 3538952 | tf_op jit(solution)/shard_map/ppermute | solution.py:53
  13.1 10.4 %all-to-all-start = ((f32[8,1,192]{2,1,0:T(1,128)}), f32[8,1,192]{2,1,0:T(1,128)S(1)}, u32[]{:S(2)}, u32[]{:S(2)}) async-start(f32[8,1,192]{2,1,0:T(1,128)} %copy.29), calls=%async_computation | async-start | bytes 16384 | tf_op jit(solution)/shard_map/all_to_all | solution.py:93
  24.2 0.7 copy-start.11
  24.9 7.6 %collective-permute-start.9 = (bf16[96,1536]{1,0:T(8,128)(2,1)S(1)}, bf16[96,1536]{1,0:T(8,128)(2,1)S(1)}, u32[]{:S(2)}, u32[]{:S(2)}) collective-permute-start(bf16[96,1536]{1,0:T(8,128)(2,1)S(1)} %get-tuple-element.42), channel_id=1, source_target_pairs={{0,16},{8,24},{16,0},{24,8},{1,17},{9,25},{17,1},{25,9},{2,18},{10... | collective-permute-start | bytes 884744 | tf_op jit(solution)/shard_map/ppermute | solution.py:53
  25.4 0.8 %copy-start.9 = (bf16[96,2304]{1,0:T(8,128)(2,1)}, bf16[96,2304]{1,0:T(8,128)(2,1)S(1)}, u32[]{:S(2)}) copy-start(bf16[96,2304]{1,0:T(8,128)(2,1)S(1)} %collective-permute-done.1.refs_2_) | copy-start | bytes 1327108
  26.2 6.3 %copy-start.10 = (bf16[96,2304]{1,0:T(8,128)(2,1)S(1)}, bf16[96,2304]{1,0:T(8,128)(2,1)}, u32[]{:S(2)}) copy-start(bf16[96,2304]{1,0:T(8,128)(2,1)} %get-tuple-element.40.refs_0_) | copy-start | bytes 1327108
  28.7 18.4 %collective-permute-start.10 = (bf16[384,1536]{1,0:T(8,128)(2,1)}, bf16[384,1536]{1,0:T(8,128)(2,1)}, u32[]{:S(2)}, u32[]{:S(2)}) collective-permute-start(bf16[384,1536]{1,0:T(8,128)(2,1)} %normalize.1.normed_hbm.refs_12_), channel_id=1, source_target_pairs={{0,16},{1,17},{2,18},{3,19},{4,20},{5,21},{6,22},{7,23}} | collective-permute-start | bytes 3538952 | tf_op jit(solution)/shard_map/ppermute | solution.py:502
  30.0 17.1 %collective-permute-start.11 = (bf16[384,1536]{1,0:T(8,128)(2,1)}, bf16[384,1536]{1,0:T(8,128)(2,1)}, u32[]{:S(2)}, u32[]{:S(2)}) collective-permute-start(bf16[384,1536]{1,0:T(8,128)(2,1)} %normalize.1.normed_hbm.refs_12_), channel_id=1, source_target_pairs={{0,8},{1,9},{2,10},{3,11},{4,12},{5,13},{6,14},{7,15}} | collective-permute-start | bytes 3538952 | tf_op jit(solution)/shard_map/ppermute | solution.py:502
  32.5 14.6 %copy-start.2 = (bf16[96,1536]{1,0:T(8,128)(2,1)}, bf16[96,1536]{1,0:T(8,128)(2,1)S(1)}, u32[]{:S(2)}) copy-start(bf16[96,1536]{1,0:T(8,128)(2,1)S(1)} %collective-permute-done.9.refs_6_) | copy-start | bytes 884740
  32.5 10.1 %collective-permute-start.3 = (bf16[96,2304]{1,0:T(8,128)(2,1)S(1)}, bf16[96,2304]{1,0:T(8,128)(2,1)}, u32[]{:S(2)}, u32[]{:S(2)}) collective-permute-start(bf16[96,2304]{1,0:T(8,128)(2,1)S(1)} %copy-done.10), channel_id=1, source_target_pairs={{0,1},{1,0},{2,3},{3,2},{4,5},{5,4},{6,7},{7,6},{8,9},{9,8},{10,11... | collective-permute-start | bytes 1327112 | tf_op jit(solution)/shard_map/ppermute | solution.py:53
  33.1 14.0 %copy-start.8 = (bf16[384,768]{1,0:T(8,128)(2,1)}, bf16[384,768]{1,0:T(8,128)(2,1)S(1)}, u32[]{:S(2)}) copy-start(bf16[384,768]{1,0:T(8,128)(2,1)S(1)} %collective-permute-done.7.refs_4_) | copy-start | bytes 1769476
  33.1 9.8 %collective-permute-start.4 = (bf16[96,2304]{1,0:T(8,128)(2,1)S(1)}, bf16[96,2304]{1,0:T(8,128)(2,1)}, u32[]{:S(2)}, u32[]{:S(2)}) collective-permute-start(bf16[96,2304]{1,0:T(8,128)(2,1)S(1)} %copy-done.10), channel_id=1, source_target_pairs={{0,2},{1,3},{2,0},{3,1},{4,6},{5,7},{6,4},{7,5},{8,10},{9,11},{10,... | collective-permute-start | bytes 1327112 | tf_op jit(solution)/shard_map/ppermute | solution.py:53
  42.6 1.9 %collective-permute-start.5 = (bf16[96,2304]{1,0:T(8,128)(2,1)S(1)}, bf16[96,2304]{1,0:T(8,128)(2,1)}, u32[]{:S(2)}, u32[]{:S(2)}) collective-permute-start(bf16[96,2304]{1,0:T(8,128)(2,1)S(1)} %copy-done.10), channel_id=1, source_target_pairs={{0,8},{8,0},{16,24},{24,16},{1,9},{9,1},{17,25},{25,17},{2,10},{10... | collective-permute-start | bytes 1327112 | tf_op jit(solution)/shard_map/ppermute | solution.py:53
  42.9 6.1 %copy-start.1 = (bf16[192,1536]{1,0:T(8,128)(2,1)S(1)}, bf16[192,1536]{1,0:T(8,128)(2,1)}, u32[]{:S(2)}) copy-start(bf16[192,1536]{1,0:T(8,128)(2,1)} %refs_0_.1) | copy-start | bytes 1769476
  42.9 10.3 %copy-start.7 = (s32[3,3]{1,0:T(4,128)S(1)}, s32[3,3]{1,0:T(4,128)}, u32[]{:S(2)}) copy-start(s32[3,3]{1,0:T(4,128)} %table_ref.3) | copy-start | bytes 112
  42.9 2.4 %collective-permute-start.6 = (bf16[96,2304]{1,0:T(8,128)(2,1)}, bf16[96,2304]{1,0:T(8,128)(2,1)}, u32[]{:S(2)}, u32[]{:S(2)}) collective-permute-start(bf16[96,2304]{1,0:T(8,128)(2,1)} %get-tuple-element.41.refs_3_), channel_id=1, source_target_pairs={{0,8},{8,0},{16,24},{24,16},{1,9},{9,1},{17,25},{25,17},{2,10},{10... | collective-permute-start | bytes 1327112 | tf_op jit(solution)/shard_map/ppermute | solution.py:53
  47.1 6.1 %collective-permute-start.14 = (bf16[384,1536]{1,0:T(8,128)(2,1)}, bf16[384,1536]{1,0:T(8,128)(2,1)S(1)}, u32[]{:S(2)}, u32[]{:S(2)}) collective-permute-start(bf16[384,1536]{1,0:T(8,128)(2,1)} %get-tuple-element.49.refs_13_), channel_id=1, source_target_pairs={{16,24},{17,25},{18,26},{19,27},{20,28},{21,29},{22,30},{23,31}} | collective-permute-start | bytes 3538952 | tf_op jit(solution)/shard_map/ppermute | solution.py:512
  48.5 3.9 %collective-permute-start.12 = (bf16[96,2304]{1,0:T(8,128)(2,1)}, bf16[96,2304]{1,0:T(8,128)(2,1)S(1)}, u32[]{:S(2)}, u32[]{:S(2)}) collective-permute-start(bf16[96,2304]{1,0:T(8,128)(2,1)} %get-tuple-element.43.refs_1_), channel_id=1, source_target_pairs={{0,8},{8,0},{16,24},{24,16},{1,9},{9,1},{17,25},{25,17},{2,10},{10... | collective-permute-start | bytes 1327112 | tf_op jit(solution)/shard_map/ppermute | solution.py:53
  48.5 4.6 %collective-permute-start.13 = (bf16[96,2304]{1,0:T(8,128)(2,1)}, bf16[96,2304]{1,0:T(8,128)(2,1)S(1)}, u32[]{:S(2)}, u32[]{:S(2)}) collective-permute-start(bf16[96,2304]{1,0:T(8,128)(2,1)} %get-tuple-element.44.refs_2_), channel_id=1, source_target_pairs={{0,8},{8,0},{16,24},{24,16},{1,9},{9,1},{17,25},{25,17},{2,10},{10... | collective-permute-start | bytes 1327112 | tf_op jit(solution)/shard_map/ppermute | solution.py:53
  49.1 20.8 %collective-permute-start.17 = (bf16[192,1536]{1,0:T(8,128)(2,1)S(1)}, bf16[192,1536]{1,0:T(8,128)(2,1)S(1)}, u32[]{:S(2)}, u32[]{:S(2)}) collective-permute-start(bf16[192,1536]{1,0:T(8,128)(2,1)S(1)} %copy-done.1), channel_id=1, source_target_pairs={{0,8},{8,0},{16,24},{24,16},{1,9},{9,1},{17,25},{25,17},{2,10},{10... | collective-permute-start | bytes 1769480 | tf_op jit(solution)/shard_map/ppermute | solution.py:53
  49.1 14.2 %collective-permute-start.15 = (bf16[96,1536]{1,0:T(8,128)(2,1)}, bf16[96,1536]{1,0:T(8,128)(2,1)S(1)}, u32[]{:S(2)}, u32[]{:S(2)}) collective-permute-start(bf16[96,1536]{1,0:T(8,128)(2,1)} %get-tuple-element.54.refs_2_), channel_id=1, source_target_pairs={{0,1},{1,0},{2,3},{3,2},{4,5},{5,4},{6,7},{7,6},{8,9},{9,8},{10,11... | collective-permute-start | bytes 884744 | tf_op jit(solution)/shard_map/ppermute | solution.py:53
  52.3 17.5 %collective-permute-start.18 = (bf16[96,1536]{1,0:T(8,128)(2,1)}, bf16[96,1536]{1,0:T(8,128)(2,1)S(1)}, u32[]{:S(2)}, u32[]{:S(2)}) collective-permute-start(bf16[96,1536]{1,0:T(8,128)(2,1)} %get-tuple-element.54.refs_2_), channel_id=1, source_target_pairs={{0,8},{8,0},{16,24},{24,16},{1,9},{9,1},{17,25},{25,17},{2,10},{10... | collective-permute-start | bytes 884744 | tf_op jit(solution)/shard_map/ppermute | solution.py:53
  63.3 9.6 %collective-permute-start.16 = (bf16[128,768]{1,0:T(8,128)(2,1)S(1)}, bf16[128,768]{1,0:T(8,128)(2,1)S(1)}, u32[]{:S(2)}, u32[]{:S(2)}) collective-permute-start(bf16[128,768]{1,0:T(8,128)(2,1)S(1)} %get-tuple-element.55), channel_id=1, source_target_pairs={{0,1},{1,2},{2,3},{3,4},{4,5},{5,6},{6,7},{8,9},{9,10},{10,11},{11... | collective-permute-start | bytes 589832 | tf_op jit(solution)/shard_map/ppermute | solution.py:59
  66.0 6.9 %collective-permute-start.19 = (bf16[96,1536]{1,0:T(8,128)(2,1)S(1)}, bf16[96,1536]{1,0:T(8,128)(2,1)S(1)}, u32[]{:S(2)}, u32[]{:S(2)}) collective-permute-start(bf16[96,1536]{1,0:T(8,128)(2,1)S(1)} %get-tuple-element.56.refs_3_), channel_id=1, source_target_pairs={{0,8},{8,0},{16,24},{24,16},{1,9},{9,1},{17,25},{25,17},{2,10},{10... | collective-permute-start | bytes 884744 | tf_op jit(solution)/shard_map/ppermute | solution.py:53
  66.1 6.8 %copy-start = (bf16[1,256,1536]{2,1,0:T(8,128)(2,1)S(1)}, bf16[1,256,1536]{2,1,0:T(8,128)(2,1)}, u32[]{:S(2)}) copy-start(bf16[1,256,1536]{2,1,0:T(8,128)(2,1)} %param.9) | copy-start | bytes 2359300
  66.1 6.8 %copy-start.3 = (bf16[96,1536]{1,0:T(8,128)(2,1)S(1)}, bf16[96,1536]{1,0:T(8,128)(2,1)}, u32[]{:S(2)}) copy-start(bf16[96,1536]{1,0:T(8,128)(2,1)} %get-tuple-element.54.refs_2_) | copy-start | bytes 884740
  66.1 6.8 %copy-start.6 = (bf16[1,256,1536]{2,1,0:T(8,128)(2,1)S(1)}, bf16[1,256,1536]{2,1,0:T(8,128)(2,1)}, u32[]{:S(2)}) copy-start(bf16[1,256,1536]{2,1,0:T(8,128)(2,1)} %param.10) | copy-start | bytes 2359300
  (1 other events, 0.6 us)

commit v7 on v6

--- a/solution.py
+++ b/solution.py
@@ -398,7 +398,7 @@
     head_width = keyval_width // 2
     n_copies = 1 + 2 * (len(wide) + len(queries))
     arrays = (normed, *wide, *queries, *keyvals, *sources)
-    late = (*wide[6:], sources[-1])
+    late = (*wide[6:], sources[-1], queries[0], keyvals[0])
     specs = [anywhere() if any(a is b for b in late) else hbm() for a in arrays]
     arrays = [a if any(a is b for b in late) else in_hbm(a) for a in arrays]
     return pl.pallas_call(

time: 75.7 us -> 75 us (level)
  starting transfers between devices: 22.9 us -> 25.3 us
  waiting for transfers between devices: 22.7 us -> 21 us
  local copies, waits for them, and re-layouts: 2.92 us -> 1.56 us
    unnamed x25 -> x23, local copies, waits for them, and re-layouts: 2.15 us -> 0.79 us
    ppermute x2, waiting for transfers between devices: 1.73 us -> 0.61 us  [from_source(): return [(lax.ppermute(value, 'var', [(0, bit)]), bit) for bit in bits]]
  transfers between devices with their start and end apart: 21 -> 21, of which waited for: 10 -> 10; matrix products, arithmetic and copies ran while one was open for 1% -> 1% of each run, Pallas kernels for 28% -> 27%
where the time goes in v7:
time: 75 us; the launch traced here: 74.7 us
  starting transfers between devices  25.3 us (34%)
  Pallas kernels  25.1 us (33%)
  waiting for transfers between devices  21 us (28%)
  local copies, waits for them, and re-layouts  1.56 us (2%)
  between operations  1.46 us (2%)
    ppermute x15, waiting for transfers between devices, swapped(): return lax.ppermute(block, axis, route)  14.2 us
    pallas_call x1, Pallas kernels, project(): pl.pallas_call(functools.partial(project_kernel, len(wide), len(queries),...  9.72 us
    ppermute x15, starting transfers between devices, swapped(): return lax.ppermute(block, axis, route)  7.62 us
    ppermute x2, starting transfers between devices, shifted(): return lax.ppermute(block, axis, route)  6.51 us
    all_to_all x1, starting transfers between devices, whole_rows(): arrived = lax.all_to_all(sent, 'tm', 0, 0, tiled=True)  6.08 us
    pallas_call x1, Pallas kernels, pool(): pl.pallas_call(pool_kernel, out_shape=jax.ShapeDtypeStruct((8, table_colu...  4.52 us
    pallas_call x1, Pallas kernels, attend_main(): pl.pallas_call(main_kernel, out_shape=jax.ShapeDtypeStruct((rows, width),...  3.68 us
    all_to_all x1, waiting for transfers between devices, whole_rows(): arrived = lax.all_to_all(sent, 'tm', 0, 0, tiled=True)  3.41 us
  transfers between devices with their start and end apart: 21, of which 10 were waited for; matrix products, arithmetic and copies ran while one was open for 1% of the time, Pallas kernels for 27%

profile of v7, /device:TPU:10, one launch (start us, length us, event | category | flops | bytes accessed | tf_op | source)
XLA Modules:
  0.0 74.7 jit_solution(6807789360065619508)
XLA Ops:
  0.1 1.9 %first_rows.1 = (bf16[128,1536]{1,0:T(8,128)(2,1)S(1)}, bf16[96,1536]{1,0:T(8,128)(2,1)S(1)}, bf16[96,2304]{1,0:T(8,128)(2,1)S(1)}, bf16[96,2304]{1,0:T(8,128)(2,1)S(1)}) custom-call(s32[3]{0:T(128)S(1)} %pad_add_fusion.places_ref, bf16[384,768]{1,0:T(8,128)(2,1)} %refs_8_.1, bf16[384,1536]{1,0:T(8,128)(2,1)} %refs_10_.1, bf16[192,1536]{1,0:T(8,128)(2,1)} %refs_0_.1, ...), custom_call_target="tpu_custom_call" | custom-call | flops 1 | bytes 1 | tf_op jit(solution)/shard_map/first_rows/pallas_call | solution.py:169
  2.0 0.6 collective-permute-start.1
  2.6 1.5 %collective-permute-start.2 = (bf16[96,2304]{1,0:T(8,128)(2,1)S(1)}, bf16[96,2304]{1,0:T(8,128)(2,1)}, u32[]{:S(2)}, u32[]{:S(2)}) collective-permute-start(bf16[96,2304]{1,0:T(8,128)(2,1)S(1)} %get-tuple-element.37), channel_id=1, source_target_pairs={{0,16},{8,24},{16,0},{24,8},{1,17},{9,25},{17,1},{25,9},{2,18},{10... | collective-permute-start | bytes 1327112 | tf_op jit(solution)/shard_map/ppermute | solution.py:53
  4.1 3.3 %collective-permute-start = (bf16[128,1536]{1,0:T(8,128)(2,1)S(1)}, bf16[128,1536]{1,0:T(8,128)(2,1)}, u32[]{:S(2)}, u32[]{:S(2)}) collective-permute-start(bf16[128,1536]{1,0:T(8,128)(2,1)S(1)} %get-tuple-element.31.after_ref), channel_id=1, source_target_pairs={{1,0},{2,1},{3,2},{4,3},{5,4},{6,5},{7,6},{9,8},{10,9},{11,10},{12... | collective-permute-start | bytes 1179656 | tf_op jit(solution)/shard_map/ppermute | solution.py:59
  7.5 0.5 collective-permute-start.8
  8.0 4.5 %pool_prompt.1 = f32[8,192]{1,0:T(8,128)S(1)} custom-call(s32[1,64]{1,0:T(1,128)S(1)} %copy-done.5, bf16[192,16384]{1,0:T(8,128)(2,1)} %bitcast.40, bf16[128,1536]{1,0:T(8,128)(2,1)S(1)} %get-tuple-element.31.after_ref), custom_call_target="tpu_custom_call" | custom-call | flops 1 | bytes 1 | tf_op jit(solution)/shard_map/pool_prompt/pallas_call | solution.py:126
  12.6 0.6 copy.29
  13.2 6.1 %all-to-all-start = ((f32[8,1,192]{2,1,0:T(1,128)}), f32[8,1,192]{2,1,0:T(1,128)S(1)}, u32[]{:S(2)}, u32[]{:S(2)}) async-start(f32[8,1,192]{2,1,0:T(1,128)} %copy.29), calls=%async_computation | async-start | bytes 16384 | tf_op jit(solution)/shard_map/all_to_all | solution.py:93
  20.9 3.4 %all-to-all-done = f32[8,1,192]{2,1,0:T(1,128)S(1)} async-done(((f32[8,1,192]{2,1,0:T(1,128)}), f32[8,1,192]{2,1,0:T(1,128)S(1)}, u32[]{:S(2)}, u32[]{:S(2)}) %all-to-all-start) | async-done | bytes 6176 | tf_op jit(solution)/shard_map/all_to_all | solution.py:93
  24.3 0.6 copy-done.4
  24.9 0.5 collective-permute-start.9
  25.4 2.4 %normalize.1.normed_hbm.refs_12_ = bf16[384,1536]{1,0:T(8,128)(2,1)} custom-call(bf16[256,1536]{1,0:T(8,128)(2,1)} %bitcast.35, bf16[128,1536]{1,0:T(8,128)(2,1)} %get-tuple-element.38.halo_ref, f32[8,192]{1,0:T(8,128)} %get-tuple-element.39.rows_ref, f32[1,768]{1,0:T(1,128)S(1)} %get-tuple-element.58.cos_ref, f32[1,768]{1,0:T(1,128)S(1)} %get-tuple-element.57.sin_ref), custom_call_target="tpu_custom_call" | custom-call | flops 1000000000 | bytes 1 | tf_op jit(solution)/shard_map/normalize/pallas_call | solution.py:281
  27.8 1.3 %collective-permute-start.10 = (bf16[384,1536]{1,0:T(8,128)(2,1)}, bf16[384,1536]{1,0:T(8,128)(2,1)}, u32[]{:S(2)}, u32[]{:S(2)}) collective-permute-start(bf16[384,1536]{1,0:T(8,128)(2,1)} %normalize.1.normed_hbm.refs_12_), channel_id=1, source_target_pairs={{0,16},{1,17},{2,18},{3,19},{4,20},{5,21},{6,22},{7,23}} | collective-permute-start | bytes 3538952 | tf_op jit(solution)/shard_map/ppermute | solution.py:502
  29.1 1.7 %collective-permute-start.11 = (bf16[384,1536]{1,0:T(8,128)(2,1)}, bf16[384,1536]{1,0:T(8,128)(2,1)}, u32[]{:S(2)}, u32[]{:S(2)}) collective-permute-start(bf16[384,1536]{1,0:T(8,128)(2,1)} %normalize.1.normed_hbm.refs_12_), channel_id=1, source_target_pairs={{0,8},{1,9},{2,10},{3,11},{4,12},{5,13},{6,14},{7,15}} | collective-permute-start | bytes 3538952 | tf_op jit(solution)/shard_map/ppermute | solution.py:502
  30.8 2.0 %collective-permute-done.9.refs_6_ = bf16[96,1536]{1,0:T(8,128)(2,1)} collective-permute-done((bf16[96,1536]{1,0:T(8,128)(2,1)}, bf16[96,1536]{1,0:T(8,128)(2,1)}, u32[]{:S(2)}, u32[]{:S(2)}) %collective-permute-start.9) | collective-permute-done | bytes 294944 | tf_op jit(solution)/shard_map/ppermute | solution.py:53
  32.7 0.6 collective-permute-start.3
  33.4 1.4 %collective-permute-start.4 = (bf16[96,2304]{1,0:T(8,128)(2,1)}, bf16[96,2304]{1,0:T(8,128)(2,1)}, u32[]{:S(2)}, u32[]{:S(2)}) collective-permute-start(bf16[96,2304]{1,0:T(8,128)(2,1)} %get-tuple-element.40.refs_0_), channel_id=1, source_target_pairs={{0,2},{1,3},{2,0},{3,1},{4,6},{5,7},{6,4},{7,5},{8,10},{9,11},{10,... | collective-permute-start | bytes 1327112 | tf_op jit(solution)/shard_map/ppermute | solution.py:53
  34.8 8.0 %collective-permute-done.3.refs_0_ = bf16[96,2304]{1,0:T(8,128)(2,1)} collective-permute-done((bf16[96,2304]{1,0:T(8,128)(2,1)}, bf16[96,2304]{1,0:T(8,128)(2,1)}, u32[]{:S(2)}, u32[]{:S(2)}) %collective-permute-start.3) | collective-permute-done | bytes 442400 | tf_op jit(solution)/shard_map/ppermute | solution.py:53
  42.8 0.3 collective-permute-done.4.refs_1_
  43.3 1.5 %collective-permute-done.5.refs_2_ = bf16[96,2304]{1,0:T(8,128)(2,1)S(1)} collective-permute-done((bf16[96,2304]{1,0:T(8,128)(2,1)}, bf16[96,2304]{1,0:T(8,128)(2,1)S(1)}, u32[]{:S(2)}, u32[]{:S(2)}) %collective-permute-start.5) | collective-permute-done | bytes 442400 | tf_op jit(solution)/shard_map/ppermute | solution.py:53
  44.8 0.6 collective-permute-done.6.refs_3_
  45.6 0.6 collective-permute-done.10.refs_7_
  46.2 2.1 %collective-permute-start.14 = (bf16[384,1536]{1,0:T(8,128)(2,1)}, bf16[384,1536]{1,0:T(8,128)(2,1)S(1)}, u32[]{:S(2)}, u32[]{:S(2)}) collective-permute-start(bf16[384,1536]{1,0:T(8,128)(2,1)} %get-tuple-element.49.refs_13_), channel_id=1, source_target_pairs={{16,24},{17,25},{18,26},{19,27},{20,28},{21,29},{22,30},{23,31}} | collective-permute-start | bytes 3538952 | tf_op jit(solution)/shard_map/ppermute | solution.py:512
  48.4 0.5 collective-permute-start.13
  49.0 1.1 %collective-permute-start.15 = (bf16[96,1536]{1,0:T(8,128)(2,1)}, bf16[96,1536]{1,0:T(8,128)(2,1)S(1)}, u32[]{:S(2)}, u32[]{:S(2)}) collective-permute-start(bf16[96,1536]{1,0:T(8,128)(2,1)} %get-tuple-element.54.refs_2_), channel_id=1, source_target_pairs={{0,1},{1,0},{2,3},{3,2},{4,5},{5,4},{6,7},{7,6},{8,9},{9,8},{10,11... | collective-permute-start | bytes 884744 | tf_op jit(solution)/shard_map/ppermute | solution.py:53
  50.1 1.4 %collective-permute-done.12.refs_6_ = bf16[96,2304]{1,0:T(8,128)(2,1)S(1)} collective-permute-done((bf16[96,2304]{1,0:T(8,128)(2,1)}, bf16[96,2304]{1,0:T(8,128)(2,1)S(1)}, u32[]{:S(2)}, u32[]{:S(2)}) %collective-permute-start.12) | collective-permute-done | bytes 442400 | tf_op jit(solution)/shard_map/ppermute | solution.py:53
  51.6 0.4 collective-permute-start.18
  52.2 9.7 %project_attend_tail.1 = (bf16[256,768]{1,0:T(8,128)(2,1)S(1)}, bf16[768,1536]{1,0:T(8,128)(2,1)S(1)}, bf16[128,768]{1,0:T(8,128)(2,1)S(1)}) custom-call(s32[12]{0:T(128)S(1)} %get-tuple-element.34.places_ref, s32[3,3]{1,0:T(4,128)S(1)} %copy-done.8, bf16[384,1536]{1,0:T(8,128)(2,1)} %normalize.1.normed_hbm.refs_12_, ...), custom_call_target="tpu_custom_call" | custom-call | flops 10000000000 | bytes 1 | tf_op jit(solution)/shard_map/project_attend_tail/pallas_call | solution.py:404
  62.0 3.2 %collective-permute-start.16 = (bf16[128,768]{1,0:T(8,128)(2,1)S(1)}, bf16[128,768]{1,0:T(8,128)(2,1)S(1)}, u32[]{:S(2)}, u32[]{:S(2)}) collective-permute-start(bf16[128,768]{1,0:T(8,128)(2,1)S(1)} %get-tuple-element.55), channel_id=1, source_target_pairs={{0,1},{1,2},{2,3},{3,4},{4,5},{5,6},{6,7},{8,9},{9,10},{10,11},{11... | collective-permute-start | bytes 589832 | tf_op jit(solution)/shard_map/ppermute | solution.py:59
  65.3 3.7 %attend_main.1.attended_ref = f32[256,768]{1,0:T(8,128)S(1)} custom-call(s32[1]{0:T(128)} %bitcast.6.places_ref, s32[3,3]{1,0:T(4,128)S(1)} %copy-done.8, bf16[256,768]{1,0:T(8,128)(2,1)S(1)} %get-tuple-element.51.query_ref, bf16[768,1536]{1,0:T(8,128)(2,1)S(1)} %get-tuple-element.52.keyval_ref), custom_call_target="tpu_custom_call" | custom-call | flops 4000000000 | bytes 1 | tf_op jit(solution)/shard_map/attend_main/pallas_call | solution.py:442
  69.0 2.8 %collective-permute-done.16.received_ref = bf16[128,768]{1,0:T(8,128)(2,1)S(1)} collective-permute-done((bf16[128,768]{1,0:T(8,128)(2,1)S(1)}, bf16[128,768]{1,0:T(8,128)(2,1)S(1)}, u32[]{:S(2)}, u32[]{:S(2)}) %collective-permute-start.16) | collective-permute-done | bytes 196640 | tf_op jit(solution)/shard_map/ppermute | solution.py:59
  71.8 2.8 %blend_and_step.1 = bf16[256,1536]{1,0:T(8,128)(2,1)} custom-call(s32[6]{0:T(128)S(1)} %get-tuple-element.32.places_ref, f32[4]{0:T(128)S(1)} %get-tuple-element.33.coef_ref, f32[256,768]{1,0:T(8,128)S(1)} %attend_main.1.attended_ref, bf16[128,768]{1,0:T(8,128)(2,1)S(1)} %collective-permute-done.16.received_ref, bf16[256,1536]{1,0:T(8,128)(2,1)S(1)} %bitcast.36, ...), custom_call_target="tpu_custom_call" | custom-call | flops 3000000000 | bytes 1 | tf_op jit(solution)/shard_map/blend_and_step/pallas_call | solution.py:476
  (49 shorter events, 1.4 us)
Async XLA Ops:
  0.1 7.4 %copy-start.2 = (bf16[384,768]{1,0:T(8,128)(2,1)S(1)}, bf16[384,768]{1,0:T(8,128)(2,1)}, u32[]{:S(2)}) copy-start(bf16[384,768]{1,0:T(8,128)(2,1)} %refs_8_.1) | copy-start | bytes 1769476
  0.1 7.5 %copy-start = (bf16[384,1536]{1,0:T(8,128)(2,1)S(1)}, bf16[384,1536]{1,0:T(8,128)(2,1)}, u32[]{:S(2)}) copy-start(bf16[384,1536]{1,0:T(8,128)(2,1)} %refs_10_.1) | copy-start | bytes 3538948
  0.1 8.0 %copy-start.5 = (s32[1,64]{1,0:T(1,128)S(1)}, s32[1,64]{1,0:T(1,128)}, u32[]{:S(2)}) copy-start(s32[1,64]{1,0:T(1,128)} %ids_ref.1) | copy-start | bytes 772
  2.0 6.0 %copy-start.7 = (bf16[96,1536]{1,0:T(8,128)(2,1)}, bf16[96,1536]{1,0:T(8,128)(2,1)S(1)}, u32[]{:S(2)}) copy-start(bf16[96,1536]{1,0:T(8,128)(2,1)S(1)} %get-tuple-element.42) | copy-start | bytes 884740
  2.0 23.4 %collective-permute-start.1 = (bf16[96,2304]{1,0:T(8,128)(2,1)S(1)}, bf16[96,2304]{1,0:T(8,128)(2,1)}, u32[]{:S(2)}, u32[]{:S(2)}) collective-permute-start(bf16[96,2304]{1,0:T(8,128)(2,1)S(1)} %get-tuple-element.36), channel_id=1, source_target_pairs={{0,16},{8,24},{16,0},{24,8},{1,17},{9,25},{17,1},{25,9},{2,18},{10... | collective-permute-start | bytes 1327112 | tf_op jit(solution)/shard_map/ppermute | solution.py:53
  2.6 22.8 %collective-permute-start.2 = (bf16[96,2304]{1,0:T(8,128)(2,1)S(1)}, bf16[96,2304]{1,0:T(8,128)(2,1)}, u32[]{:S(2)}, u32[]{:S(2)}) collective-permute-start(bf16[96,2304]{1,0:T(8,128)(2,1)S(1)} %get-tuple-element.37), channel_id=1, source_target_pairs={{0,16},{8,24},{16,0},{24,8},{1,17},{9,25},{17,1},{25,9},{2,18},{10... | collective-permute-start | bytes 1327112 | tf_op jit(solution)/shard_map/ppermute | solution.py:53
  4.1 20.7 %collective-permute-start = (bf16[128,1536]{1,0:T(8,128)(2,1)S(1)}, bf16[128,1536]{1,0:T(8,128)(2,1)}, u32[]{:S(2)}, u32[]{:S(2)}) collective-permute-start(bf16[128,1536]{1,0:T(8,128)(2,1)S(1)} %get-tuple-element.31.after_ref), channel_id=1, source_target_pairs={{1,0},{2,1},{3,2},{4,3},{5,4},{6,5},{7,6},{9,8},{10,9},{11,10},{12... | collective-permute-start | bytes 1179656 | tf_op jit(solution)/shard_map/ppermute | solution.py:59
  7.5 25.9 %collective-permute-start.7 = (bf16[384,768]{1,0:T(8,128)(2,1)S(1)}, bf16[384,768]{1,0:T(8,128)(2,1)}, u32[]{:S(2)}, u32[]{:S(2)}) collective-permute-start(bf16[384,768]{1,0:T(8,128)(2,1)S(1)} %copy-done.2), channel_id=1, source_target_pairs={{0,8},{8,0},{16,24},{24,16},{1,9},{9,1},{17,25},{25,17},{2,10},{10... | collective-permute-start | bytes 1769480 | tf_op jit(solution)/shard_map/ppermute | solution.py:53
  7.5 37.9 %collective-permute-start.8 = (bf16[384,1536]{1,0:T(8,128)(2,1)S(1)}, bf16[384,1536]{1,0:T(8,128)(2,1)}, u32[]{:S(2)}, u32[]{:S(2)}) collective-permute-start(bf16[384,1536]{1,0:T(8,128)(2,1)S(1)} %copy-done), channel_id=1, source_target_pairs={{0,8},{8,0},{16,24},{24,16},{1,9},{9,1},{17,25},{25,17},{2,10},{10... | collective-permute-start | bytes 3538952 | tf_op jit(solution)/shard_map/ppermute | solution.py:53
  13.2 11.1 %all-to-all-start = ((f32[8,1,192]{2,1,0:T(1,128)}), f32[8,1,192]{2,1,0:T(1,128)S(1)}, u32[]{:S(2)}, u32[]{:S(2)}) async-start(f32[8,1,192]{2,1,0:T(1,128)} %copy.29), calls=%async_computation | async-start | bytes 16384 | tf_op jit(solution)/shard_map/all_to_all | solution.py:93
  24.3 0.6 copy-start.4
  24.9 7.9 %collective-permute-start.9 = (bf16[96,1536]{1,0:T(8,128)(2,1)}, bf16[96,1536]{1,0:T(8,128)(2,1)}, u32[]{:S(2)}, u32[]{:S(2)}) collective-permute-start(bf16[96,1536]{1,0:T(8,128)(2,1)} %copy-done.7), channel_id=1, source_target_pairs={{0,16},{8,24},{16,0},{24,8},{1,17},{9,25},{17,1},{25,9},{2,18},{10... | collective-permute-start | bytes 884744 | tf_op jit(solution)/shard_map/ppermute | solution.py:53
  27.8 18.4 %collective-permute-start.10 = (bf16[384,1536]{1,0:T(8,128)(2,1)}, bf16[384,1536]{1,0:T(8,128)(2,1)}, u32[]{:S(2)}, u32[]{:S(2)}) collective-permute-start(bf16[384,1536]{1,0:T(8,128)(2,1)} %normalize.1.normed_hbm.refs_12_), channel_id=1, source_target_pairs={{0,16},{1,17},{2,18},{3,19},{4,20},{5,21},{6,22},{7,23}} | collective-permute-start | bytes 3538952 | tf_op jit(solution)/shard_map/ppermute | solution.py:502
  29.1 17.2 %collective-permute-start.11 = (bf16[384,1536]{1,0:T(8,128)(2,1)}, bf16[384,1536]{1,0:T(8,128)(2,1)}, u32[]{:S(2)}, u32[]{:S(2)}) collective-permute-start(bf16[384,1536]{1,0:T(8,128)(2,1)} %normalize.1.normed_hbm.refs_12_), channel_id=1, source_target_pairs={{0,8},{1,9},{2,10},{3,11},{4,12},{5,13},{6,14},{7,15}} | collective-permute-start | bytes 3538952 | tf_op jit(solution)/shard_map/ppermute | solution.py:502
  32.7 10.1 %collective-permute-start.3 = (bf16[96,2304]{1,0:T(8,128)(2,1)}, bf16[96,2304]{1,0:T(8,128)(2,1)}, u32[]{:S(2)}, u32[]{:S(2)}) collective-permute-start(bf16[96,2304]{1,0:T(8,128)(2,1)} %get-tuple-element.40.refs_0_), channel_id=1, source_target_pairs={{0,1},{1,0},{2,3},{3,2},{4,5},{5,4},{6,7},{7,6},{8,9},{9,8},{10,11... | collective-permute-start | bytes 1327112 | tf_op jit(solution)/shard_map/ppermute | solution.py:53
  33.4 9.8 %collective-permute-start.4 = (bf16[96,2304]{1,0:T(8,128)(2,1)}, bf16[96,2304]{1,0:T(8,128)(2,1)}, u32[]{:S(2)}, u32[]{:S(2)}) collective-permute-start(bf16[96,2304]{1,0:T(8,128)(2,1)} %get-tuple-element.40.refs_0_), channel_id=1, source_target_pairs={{0,2},{1,3},{2,0},{3,1},{4,6},{5,7},{6,4},{7,5},{8,10},{9,11},{10,... | collective-permute-start | bytes 1327112 | tf_op jit(solution)/shard_map/ppermute | solution.py:53
  42.8 2.0 %collective-permute-start.5 = (bf16[96,2304]{1,0:T(8,128)(2,1)}, bf16[96,2304]{1,0:T(8,128)(2,1)S(1)}, u32[]{:S(2)}, u32[]{:S(2)}) collective-permute-start(bf16[96,2304]{1,0:T(8,128)(2,1)} %get-tuple-element.40.refs_0_), channel_id=1, source_target_pairs={{0,8},{8,0},{16,24},{24,16},{1,9},{9,1},{17,25},{25,17},{2,10},{10... | collective-permute-start | bytes 1327112 | tf_op jit(solution)/shard_map/ppermute | solution.py:53
  43.2 9.0 %copy-start.8 = (s32[3,3]{1,0:T(4,128)S(1)}, s32[3,3]{1,0:T(4,128)}, u32[]{:S(2)}) copy-start(s32[3,3]{1,0:T(4,128)} %table_ref.3) | copy-start | bytes 112
  43.2 2.3 %collective-permute-start.6 = (bf16[96,2304]{1,0:T(8,128)(2,1)}, bf16[96,2304]{1,0:T(8,128)(2,1)S(1)}, u32[]{:S(2)}, u32[]{:S(2)}) collective-permute-start(bf16[96,2304]{1,0:T(8,128)(2,1)} %get-tuple-element.41.refs_3_), channel_id=1, source_target_pairs={{0,8},{8,0},{16,24},{24,16},{1,9},{9,1},{17,25},{25,17},{2,10},{10... | collective-permute-start | bytes 1327112 | tf_op jit(solution)/shard_map/ppermute | solution.py:53
  44.8 0.8 %copy-start.9 = (bf16[96,2304]{1,0:T(8,128)(2,1)}, bf16[96,2304]{1,0:T(8,128)(2,1)S(1)}, u32[]{:S(2)}) copy-start(bf16[96,2304]{1,0:T(8,128)(2,1)S(1)} %collective-permute-done.5.refs_2_) | copy-start | bytes 1327108
  45.5 0.8 %copy-start.10 = (bf16[96,2304]{1,0:T(8,128)(2,1)}, bf16[96,2304]{1,0:T(8,128)(2,1)S(1)}, u32[]{:S(2)}) copy-start(bf16[96,2304]{1,0:T(8,128)(2,1)S(1)} %collective-permute-done.6.refs_3_) | copy-start | bytes 1327108
  46.2 6.0 %collective-permute-start.14 = (bf16[384,1536]{1,0:T(8,128)(2,1)}, bf16[384,1536]{1,0:T(8,128)(2,1)S(1)}, u32[]{:S(2)}, u32[]{:S(2)}) collective-permute-start(bf16[384,1536]{1,0:T(8,128)(2,1)} %get-tuple-element.49.refs_13_), channel_id=1, source_target_pairs={{16,24},{17,25},{18,26},{19,27},{20,28},{21,29},{22,30},{23,31}} | collective-permute-start | bytes 3538952 | tf_op jit(solution)/shard_map/ppermute | solution.py:512
  48.4 3.2 %collective-permute-start.12 = (bf16[96,2304]{1,0:T(8,128)(2,1)}, bf16[96,2304]{1,0:T(8,128)(2,1)S(1)}, u32[]{:S(2)}, u32[]{:S(2)}) collective-permute-start(bf16[96,2304]{1,0:T(8,128)(2,1)} %get-tuple-element.43.refs_1_), channel_id=1, source_target_pairs={{0,8},{8,0},{16,24},{24,16},{1,9},{9,1},{17,25},{25,17},{2,10},{10... | collective-permute-start | bytes 1327112 | tf_op jit(solution)/shard_map/ppermute | solution.py:53
  48.4 3.8 %collective-permute-start.13 = (bf16[96,2304]{1,0:T(8,128)(2,1)}, bf16[96,2304]{1,0:T(8,128)(2,1)S(1)}, u32[]{:S(2)}, u32[]{:S(2)}) collective-permute-start(bf16[96,2304]{1,0:T(8,128)(2,1)} %get-tuple-element.44.refs_2_), channel_id=1, source_target_pairs={{0,8},{8,0},{16,24},{24,16},{1,9},{9,1},{17,25},{25,17},{2,10},{10... | collective-permute-start | bytes 1327112 | tf_op jit(solution)/shard_map/ppermute | solution.py:53
  48.9 20.1 %collective-permute-start.17 = (bf16[192,1536]{1,0:T(8,128)(2,1)}, bf16[192,1536]{1,0:T(8,128)(2,1)S(1)}, u32[]{:S(2)}, u32[]{:S(2)}) collective-permute-start(bf16[192,1536]{1,0:T(8,128)(2,1)} %refs_0_.1), channel_id=1, source_target_pairs={{0,8},{8,0},{16,24},{24,16},{1,9},{9,1},{17,25},{25,17},{2,10},{10... | collective-permute-start | bytes 1769480 | tf_op jit(solution)/shard_map/ppermute | solution.py:53
  49.0 12.9 %collective-permute-start.15 = (bf16[96,1536]{1,0:T(8,128)(2,1)}, bf16[96,1536]{1,0:T(8,128)(2,1)S(1)}, u32[]{:S(2)}, u32[]{:S(2)}) collective-permute-start(bf16[96,1536]{1,0:T(8,128)(2,1)} %get-tuple-element.54.refs_2_), channel_id=1, source_target_pairs={{0,1},{1,0},{2,3},{3,2},{4,5},{5,4},{6,7},{7,6},{8,9},{9,8},{10,11... | collective-permute-start | bytes 884744 | tf_op jit(solution)/shard_map/ppermute | solution.py:53
  51.6 17.4 %collective-permute-start.18 = (bf16[96,1536]{1,0:T(8,128)(2,1)}, bf16[96,1536]{1,0:T(8,128)(2,1)S(1)}, u32[]{:S(2)}, u32[]{:S(2)}) collective-permute-start(bf16[96,1536]{1,0:T(8,128)(2,1)} %get-tuple-element.54.refs_2_), channel_id=1, source_target_pairs={{0,8},{8,0},{16,24},{24,16},{1,9},{9,1},{17,25},{25,17},{2,10},{10... | collective-permute-start | bytes 884744 | tf_op jit(solution)/shard_map/ppermute | solution.py:53
  62.0 9.8 %collective-permute-start.16 = (bf16[128,768]{1,0:T(8,128)(2,1)S(1)}, bf16[128,768]{1,0:T(8,128)(2,1)S(1)}, u32[]{:S(2)}, u32[]{:S(2)}) collective-permute-start(bf16[128,768]{1,0:T(8,128)(2,1)S(1)} %get-tuple-element.55), channel_id=1, source_target_pairs={{0,1},{1,2},{2,3},{3,4},{4,5},{5,6},{6,7},{8,9},{9,10},{10,11},{11... | collective-permute-start | bytes 589832 | tf_op jit(solution)/shard_map/ppermute | solution.py:59
  65.2 6.6 %collective-permute-start.19 = (bf16[96,1536]{1,0:T(8,128)(2,1)S(1)}, bf16[96,1536]{1,0:T(8,128)(2,1)S(1)}, u32[]{:S(2)}, u32[]{:S(2)}) collective-permute-start(bf16[96,1536]{1,0:T(8,128)(2,1)S(1)} %get-tuple-element.56.refs_3_), channel_id=1, source_target_pairs={{0,8},{8,0},{16,24},{24,16},{1,9},{9,1},{17,25},{25,17},{2,10},{10... | collective-permute-start | bytes 884744 | tf_op jit(solution)/shard_map/ppermute | solution.py:53
  65.3 6.6 %copy-start.1 = (bf16[1,256,1536]{2,1,0:T(8,128)(2,1)S(1)}, bf16[1,256,1536]{2,1,0:T(8,128)(2,1)}, u32[]{:S(2)}) copy-start(bf16[1,256,1536]{2,1,0:T(8,128)(2,1)} %param.9) | copy-start | bytes 2359300
  65.3 6.5 %copy-start.3 = (bf16[192,1536]{1,0:T(8,128)(2,1)S(1)}, bf16[192,1536]{1,0:T(8,128)(2,1)}, u32[]{:S(2)}) copy-start(bf16[192,1536]{1,0:T(8,128)(2,1)} %refs_0_.1) | copy-start | bytes 1769476
  65.3 6.5 %copy-start.6 = (bf16[1,256,1536]{2,1,0:T(8,128)(2,1)S(1)}, bf16[1,256,1536]{2,1,0:T(8,128)(2,1)}, u32[]{:S(2)}) copy-start(bf16[1,256,1536]{2,1,0:T(8,128)(2,1)} %param.10) | copy-start | bytes 2359300
